TPU v7x, 768 devices: a whole 4x8x12 slice. The times are simulated.
768 devices in a mesh: bx: 48 (over z_lo, x, core), by: 16 (over z_hi, y).
Axes of the slice: x: 4, y: 8, z: 12 (z_hi: 2, z_lo: 6; z = z_hi * 6 + z_lo), core: 2. Of those that a mesh axis runs over, the one named last changes fastest.
Arguments:
- populations: float32 [19, 1, 6144, 2048], P(None, None, 'bx', 'by'), may hold values from 0 to 1, as said below
- solid_mask: int32 [1, 6144, 2048], P(None, 'bx', 'by'), may hold values 0 or 1
- pore_list: int32 [48, 16, 4], P('bx', 'by'), may hold values from 0 to 3, each once within a row
- pore_count: int32 [48, 16], P(None, 'by'), may hold values from 0 to 4, as said below
Outputs:
- final_populations: float32 [19, 1, 6144, 2048], P(None, None, 'bx', 'by')
Inputs may be any that keep to these rules, and one draw needn't show every extreme that they name: Positive; each cell's populations are a perturbed equilibrium with velocity components of order 0.1. pore_count[i, j] + pore_count[(i + 24) mod 48, j] <= 4 for every i and j; some device has 4 pore blocks in every draw.
All inputs are finite; a program needn't handle non-finite values. No bound on the sum of `solid_mask` on one device may be relied on, other than what follows from the above.
Results may differ from a plain program's by a relative error of at most 0.0001.
Values sent between devices are 32-bit elements; how exact they have to be, the bound alone decides.
No kernel may reach another device: no remote copies, remote signals or barrier semaphores. Data moves between devices by JAX's collectives and lax.ppermute only.
A program may use at most 32 MiB of HBM per device.

v0:
```python
import jax
import jax.numpy as jnp
import numpy as np
from jax import lax
from jax.sharding import PartitionSpec as P

BLOCK_SIDE = 64
BLOCK_SLOTS = 4


VELOCITY = np.array(
    [
        [0, 0, 0],
        [1, 0, 0],
        [-1, 0, 0],
        [0, 1, 0],
        [0, -1, 0],
        [0, 0, 1],
        [0, 0, -1],
        [1, 1, 0],
        [-1, -1, 0],
        [1, -1, 0],
        [-1, 1, 0],
        [1, 0, 1],
        [-1, 0, -1],
        [1, 0, -1],
        [-1, 0, 1],
        [0, 1, 1],
        [0, -1, -1],
        [0, 1, -1],
        [0, -1, 1],
    ]
)
WEIGHT = np.array([1.0 / 3.0] + [1.0 / 18.0] * 6 + [1.0 / 36.0] * 12)
OPPOSITE = np.array([0, 2, 1, 4, 3, 6, 5, 8, 7, 10, 9, 12, 11, 14, 13, 16, 15, 18, 17])
OMEGA_PLUS = 1.0 / 0.8
OMEGA_MINUS = 1.0 / (0.1875 / 0.3 + 0.5)


def with_halo(block, sides, width):
    for axis, dim in sides:
        count = lax.axis_size(axis)
        forward = [(i, i + 1) for i in range(count - 1)]
        forward.append((count - 1, 0))
        backward = [(target, source) for source, target in forward]
        low = lax.ppermute(
            lax.slice_in_dim(block, block.shape[dim] - width, None, axis=dim), axis, forward
        )
        high = lax.ppermute(lax.slice_in_dim(block, 0, width, axis=dim), axis, backward)
        block = jnp.concatenate([low, block, high], axis=dim)
    return block


def collide(populations):
    extra_dims = (1,) * (populations.ndim - 1)
    along = [
        jnp.asarray(VELOCITY[:, a].reshape((19,) + extra_dims), populations.dtype) for a in range(3)
    ]
    weights = jnp.asarray(WEIGHT.reshape((19,) + extra_dims), populations.dtype)
    density = jnp.sum(populations, axis=0)
    speed_x = jnp.sum(along[0] * populations, axis=0) / density
    speed_y = jnp.sum(along[1] * populations, axis=0) / density
    speed_z = jnp.sum(along[2] * populations, axis=0) / density
    dotted = along[0] * speed_x + along[1] * speed_y + along[2] * speed_z
    square = speed_x * speed_x + speed_y * speed_y + speed_z * speed_z
    equilibrium = weights * density * (1.0 + 3.0 * dotted + 4.5 * dotted * dotted - 1.5 * square)
    mirror = populations[OPPOSITE]
    emirror = equilibrium[OPPOSITE]
    even_part = 0.5 * (populations + mirror) - 0.5 * (equilibrium + emirror)
    odd_part = 0.5 * (populations - mirror) - 0.5 * (equilibrium - emirror)
    return populations - OMEGA_PLUS * even_part - OMEGA_MINUS * odd_part


def live_tile(listed, own_count, side):
    positions = jnp.arange(listed.shape[0], dtype=jnp.int32)
    counted = positions < own_count
    flags = jnp.stack([jnp.any(counted & (listed == b)) for b in range(BLOCK_SLOTS)]).reshape(2, 2)
    return jnp.repeat(jnp.repeat(flags, side, axis=0), side, axis=1)


def local_stream(padded, relaxed, populations, active):
    rows_x, rows_y = (relaxed.shape[2], relaxed.shape[3])
    solid_index = relaxed.shape[0]
    columns = []
    for k in range(19):
        step_x, step_y, step_z = (int(v) for v in VELOCITY[k])
        window = padded[:, :, 1 - step_x : 1 - step_x + rows_x, 1 - step_y : 1 - step_y + rows_y]
        shifted = jnp.roll(window[k], step_z, axis=0)
        blocked = jnp.roll(window[solid_index], step_z, axis=0) != 0.0
        columns.append(jnp.where(blocked, relaxed[int(OPPOSITE[k])], shifted))
    return jnp.where(active[None], jnp.stack(columns), populations)


def local(populations, solid_mask, pore_list, pore_count):
    side = BLOCK_SIDE
    position = lax.axis_index("bx")
    own_count = pore_count[position, 0]
    listed = pore_list.reshape(-1)
    live_columns = live_tile(listed, own_count, side)[None, :, :]
    active = live_columns & (solid_mask == 0)
    solid_float = solid_mask.astype(jnp.float32)
    relaxed = jnp.where(live_columns[None], collide(populations), populations)
    stacked = jnp.concatenate([relaxed, solid_float[None]], axis=0)
    padded = with_halo(stacked, (("bx", 2), ("by", 3)), 1)
    populations = local_stream(padded, relaxed, populations, active)
    return populations


def solution(mesh):
    placed = (P(None, None, "bx", "by"), P(None, "bx", "by"), P("bx", "by", None), P(None, "by"))
    return jax.shard_map(
        local, mesh=mesh, in_specs=placed, out_specs=P(None, None, "bx", "by"), check_vma=False
    )
```

profile of v0, /device:TPU:56, one launch (start us, length us, event | category | flops | bytes accessed | tf_op | source)
XLA Modules:
  0.0 79.4 jit_solution(18284492219315338762)
XLA Ops:
  0.0 0.8 pad_clamp_fusion
  1.4 2.0 %fusion.42 = (pred[]{:T(512)}, pred[]{:T(512)}, pred[]{:T(512)}, pred[]{:T(512)}) fusion(s32[1,1,4]{2,1,0:T(1,128)} %param.13, s32[]{:T(128)} %bitcast), kind=kLoop, calls=%fused_computation.105 | loop fusion | flops 48 | bytes 24 | tf_op jit(solution)/shard_map/reduce_or | solution.py:77
  3.4 2.6 %pad_add_fusion = pred[4]{0:T(512)(128)(4,1)S(1)} fusion(pred[1]{0:T(512)(128)(4,1)} %bitcast.8, pred[1]{0:T(512)(128)(4,1)} %bitcast.6, pred[1]{0:T(512)(128)(4,1)} %bitcast.4, pred[1]{0:T(512)(128)(4,1)} %bitcast.2), kind=kLoop, calls=%fused_computation.97 | loop fusion | flops 12 | bytes 8 | tf_op jit(solution)/shard_map/stack | solution.py:77
  6.5 1.4 %reduce_sum.36 = f32[128,128]{1,0:T(8,128)S(1)} reduce(f32[19,1,128,128]{3,2,1,0:T(8,128)} %param.11, f32[]{:T(128)} %constant.14.clone.1), dimensions={0,1}, to_apply=%region_4.0 | reduce | flops 294912 | bytes 1310724 | tf_op jit(solution)/shard_map/reduce_sum | solution.py:60
  9.3 1.7 %gather_fusion.1 = f32[19,128,128]{2,1,0:T(8,128)} fusion(f32[19,128,128]{2,1,0:T(8,128)S(1)} %fusion.18, s32[1024]{0:T(1024)S(1)} %pad_clamp_fusion), kind=kCustom, calls=%fused_computation.1 | custom fusion | bytes 2490444 | tf_op jit(solution)/shard_map/gather | solution.py:68
  11.0 1.7 %gather_fusion = f32[19,128,128]{2,1,0:T(8,128)} fusion(f32[19,128,128]{2,1,0:T(8,128)S(1)} %bitcast.105, s32[1024]{0:T(1024)S(1)} %pad_clamp_fusion), kind=kCustom, calls=%fused_computation | custom fusion | bytes 2490444 | tf_op jit(solution)/shard_map/gather | solution.py:67
  12.6 3.0 %fusion.8 = f32[19,1,128,128]{3,2,0,1:T(8,128)S(1)} fusion(f32[19,128,128]{2,1,0:T(8,128)} %gather_fusion.1, f32[19,128,128]{2,1,0:T(8,128)} %gather_fusion, f32[19,1,128,128]{3,2,1,0:T(8,128)S(1)} %copy-done.2, f32[128,128]{1,0:T(8,128)S(1)} %get-tuple-element.14, f32[128,128]{1,0:T(8,128)S(1)} %get-tuple-element.17, f32[19]{0:T(128)S(1)} %copy-done.8, ...), kind=kLoop, calls=%fused_computation.14 | loop fusion | flops 8716288 | bytes 5325104 | tf_op jit(solution)/shard_map/jit(_where)/select_n | solution.py:102
  15.7 1.9 %collective-permute-start = (f32[20,1,1,128]{3,2,0,1:T(1,128)S(1)}, f32[20,1,1,128]{3,2,0,1:T(1,128)S(1)}, u32[]{:S(2)}, u32[]{:S(2)}) collective-permute-start(f32[20,1,1,128]{3,2,0,1:T(1,128)S(1)} %get-tuple-element.21), channel_id=1, source_target_pairs={{0,16},{16,32},{32,48},{48,64},{64,80},{80,96},{96,112},{112,128},... | collective-permute-start | bytes 30728 | tf_op jit(solution)/shard_map/ppermute | solution.py:46
  17.7 14.4 %collective-permute-start.1 = (f32[20,1,1,128]{3,2,0,1:T(1,128)S(1)}, f32[20,1,1,128]{3,2,0,1:T(1,128)S(1)}, u32[]{:S(2)}, u32[]{:S(2)}) collective-permute-start(f32[20,1,1,128]{3,2,0,1:T(1,128)S(1)} %get-tuple-element.20), channel_id=1, source_target_pairs={{16,0},{32,16},{48,32},{64,48},{80,64},{96,80},{112,96},{128,112},... | collective-permute-start | bytes 30728 | tf_op jit(solution)/shard_map/ppermute | solution.py:49
  33.5 2.0 %fusion.43 = (f32[20,1,130,1]{3,2,0,1:T(8,128)}, f32[20,1,130,1]{3,2,0,1:T(8,128)}) fusion(f32[20,1,130,128]{3,2,0,1:T(8,128)S(1)} %pad_maximum_fusion), kind=kLoop, calls=%fused_computation.108 | loop fusion | bytes 41600 | tf_op jit(solution)/shard_map/slice | solution.py:49
  35.5 2.3 %copy.43 = f32[20,1,130,1]{2,0,3,1:T(8,128)S(1)} copy(f32[20,1,130,1]{3,2,0,1:T(8,128)} %get-tuple-element.19) | data formatting | bytes 20800 | tf_op jit(solution)/shard_map/slice | solution.py:47
  37.9 10.5 %collective-permute-start.2 = (f32[20,1,130,1]{2,0,3,1:T(8,128)S(1)}, f32[20,1,130,1]{2,0,3,1:T(8,128)S(1)}, u32[]{:S(2)}, u32[]{:S(2)}) collective-permute-start(f32[20,1,130,1]{2,0,3,1:T(8,128)S(1)} %copy.43), channel_id=1, source_target_pairs={{0,1},{1,2},{2,3},{3,4},{4,5},{5,6},{6,7},{7,8},{8,9},{9,10},{10,1... | collective-permute-start | bytes 31208 | tf_op jit(solution)/shard_map/ppermute | solution.py:46
  48.4 0.9 %copy.45 = f32[20,1,130,1]{2,0,3,1:T(8,128)S(1)} copy(f32[20,1,130,1]{3,2,0,1:T(8,128)S(1)} %copy-done.4) | data formatting | bytes 20800 | tf_op jit(solution)/shard_map/slice | solution.py:49
  49.3 1.9 %collective-permute-start.3 = (f32[20,1,130,1]{2,0,3,1:T(8,128)S(1)}, f32[20,1,130,1]{2,0,3,1:T(8,128)S(1)}, u32[]{:S(2)}, u32[]{:S(2)}) collective-permute-start(f32[20,1,130,1]{2,0,3,1:T(8,128)S(1)} %copy.45), channel_id=1, source_target_pairs={{1,0},{2,1},{3,2},{4,3},{5,4},{6,5},{7,6},{8,7},{9,8},{10,9},{11,1... | collective-permute-start | bytes 31208 | tf_op jit(solution)/shard_map/ppermute | solution.py:49
  52.5 1.6 %copy.44 = f32[20,1,130,1]{3,2,0,1:T(8,128)} copy(f32[20,1,130,1]{2,0,3,1:T(8,128)S(1)} %collective-permute-done.2) | data formatting | bytes 20800 | tf_op jit(solution)/shard_map/ppermute | solution.py:46
  54.1 9.3 %collective-permute-done.3 = f32[20,1,130,1]{2,0,3,1:T(8,128)S(1)} collective-permute-done((f32[20,1,130,1]{2,0,3,1:T(8,128)S(1)}, f32[20,1,130,1]{2,0,3,1:T(8,128)S(1)}, u32[]{:S(2)}, u32[]{:S(2)}) %collective-permute-start.3) | collective-permute-done | bytes 10432 | tf_op jit(solution)/shard_map/ppermute | solution.py:49
  64.0 1.7 %fusion.36 = f32[19,1,128,128]{3,2,0,1:T(8,128)} fusion(f32[19,1,128,128]{3,2,0,1:T(8,128)} %fusion.37, f32[20,1,130,1]{3,2,0,1:T(8,128)} %copy.44, f32[20,1,1,128]{3,2,0,1:T(1,128)S(1)} %collective-permute-done.1, f32[20,1,1,128]{3,2,0,1:T(1,128)S(1)} %collective-permute-done, f32[1,1,128,128]{3,2,0,1:T(8,128)S(1)} %convert_bitcast_fusion, ...), kind=kLoop, calls=%fused_computation.78 | loop fusion | flops 163840 | bytes 2854912
  65.6 0.8 fusion.35
  68.4 0.8 fusion.33
  69.2 0.8 fusion.32
  70.0 0.7 fusion.31
  74.0 0.8 fusion.23
  75.5 0.8 fusion.20
  76.8 2.5 %fusion.14 = f32[19,1,128,128]{3,2,1,0:T(8,128)} fusion(f32[19,1,128,128]{3,2,0,1:T(8,128)} %fusion.20, f32[19,1,128,128]{3,2,1,0:T(8,128)S(1)} %copy-done.3, pred[128,128]{1,0:T(8,128)(4,1)S(1)} %copy.34), kind=kLoop, calls=%fused_computation.26 | loop fusion | flops 311296 | bytes 3751936 | tf_op jit(solution)/shard_map/jit(_where)/select_n | solution.py:91
  (52 shorter events, 12.3 us)
Async XLA Ops:
  0.0 0.8 %copy-start = (s32[48,1]{0,1:T(1,128)S(1)}, s32[48,1]{0,1:T(1,128)}, u32[]{:S(2)}) copy-start(s32[48,1]{0,1:T(1,128)} %param.14) | copy-start | bytes 580
  0.0 7.9 %copy-start.6 = (f32[19]{0:T(128)S(1)}, f32[19]{0:T(128)}, u32[]{:S(2)}) copy-start(f32[19]{0:T(128)} %constant.62) | copy-start | bytes 232
  0.0 7.9 %copy-start.7 = (f32[19]{0:T(128)S(1)}, f32[19]{0:T(128)}, u32[]{:S(2)}) copy-start(f32[19]{0:T(128)} %constant.63) | copy-start | bytes 232
  0.0 7.9 %copy-start.8 = (f32[19]{0:T(128)S(1)}, f32[19]{0:T(128)}, u32[]{:S(2)}) copy-start(f32[19]{0:T(128)} %constant.64) | copy-start | bytes 232
  0.0 7.9 %copy-start.2 = (f32[19,1,128,128]{3,2,1,0:T(8,128)S(1)}, f32[19,1,128,128]{3,2,1,0:T(8,128)}, u32[]{:S(2)}) copy-start(f32[19,1,128,128]{3,2,1,0:T(8,128)} %param.11) | copy-start | bytes 3735556
  7.9 0.7 copy-start.9
  11.0 1.7 %copy-start.5 = (s32[1,128,128]{2,1,0:T(8,128)S(1)}, s32[1,128,128]{2,1,0:T(8,128)}, u32[]{:S(2)}) copy-start(s32[1,128,128]{2,1,0:T(8,128)} %param.12) | copy-start | bytes 196612
  15.7 17.2 %collective-permute-start = (f32[20,1,1,128]{3,2,0,1:T(1,128)S(1)}, f32[20,1,1,128]{3,2,0,1:T(1,128)S(1)}, u32[]{:S(2)}, u32[]{:S(2)}) collective-permute-start(f32[20,1,1,128]{3,2,0,1:T(1,128)S(1)} %get-tuple-element.21), channel_id=1, source_target_pairs={{0,16},{16,32},{32,48},{48,64},{64,80},{80,96},{96,112},{112,128},... | collective-permute-start | bytes 30728 | tf_op jit(solution)/shard_map/ppermute | solution.py:46
  17.7 15.7 %collective-permute-start.1 = (f32[20,1,1,128]{3,2,0,1:T(1,128)S(1)}, f32[20,1,1,128]{3,2,0,1:T(1,128)S(1)}, u32[]{:S(2)}, u32[]{:S(2)}) collective-permute-start(f32[20,1,1,128]{3,2,0,1:T(1,128)S(1)} %get-tuple-element.20), channel_id=1, source_target_pairs={{16,0},{32,16},{48,32},{64,48},{80,64},{96,80},{112,96},{128,112},... | collective-permute-start | bytes 30728 | tf_op jit(solution)/shard_map/ppermute | solution.py:49
  35.5 12.9 %copy-start.4 = (f32[20,1,130,1]{3,2,0,1:T(8,128)S(1)}, f32[20,1,130,1]{3,2,0,1:T(8,128)}, u32[]{:S(2)}) copy-start(f32[20,1,130,1]{3,2,0,1:T(8,128)} %get-tuple-element.18) | copy-start | bytes 31204
  37.9 14.7 %collective-permute-start.2 = (f32[20,1,130,1]{2,0,3,1:T(8,128)S(1)}, f32[20,1,130,1]{2,0,3,1:T(8,128)S(1)}, u32[]{:S(2)}, u32[]{:S(2)}) collective-permute-start(f32[20,1,130,1]{2,0,3,1:T(8,128)S(1)} %copy.43), channel_id=1, source_target_pairs={{0,1},{1,2},{2,3},{3,4},{4,5},{5,6},{6,7},{7,8},{8,9},{9,10},{10,1... | collective-permute-start | bytes 31208 | tf_op jit(solution)/shard_map/ppermute | solution.py:46
  49.3 14.1 %collective-permute-start.3 = (f32[20,1,130,1]{2,0,3,1:T(8,128)S(1)}, f32[20,1,130,1]{2,0,3,1:T(8,128)S(1)}, u32[]{:S(2)}, u32[]{:S(2)}) collective-permute-start(f32[20,1,130,1]{2,0,3,1:T(8,128)S(1)} %copy.45), channel_id=1, source_target_pairs={{1,0},{2,1},{3,2},{4,3},{5,4},{6,5},{7,6},{8,7},{9,8},{10,9},{11,1... | collective-permute-start | bytes 31208 | tf_op jit(solution)/shard_map/ppermute | solution.py:49
  65.6 2.1 %copy-start.1 = (f32[20,1,130,1]{3,2,0,1:T(8,128)S(1)}, f32[20,1,130,1]{3,2,0,1:T(8,128)}, u32[]{:S(2)}) copy-start(f32[20,1,130,1]{3,2,0,1:T(8,128)} %copy.44) | copy-start | bytes 31204
  75.5 1.3 %copy-start.3 = (f32[19,1,128,128]{3,2,1,0:T(8,128)S(1)}, f32[19,1,128,128]{3,2,1,0:T(8,128)}, u32[]{:S(2)}) copy-start(f32[19,1,128,128]{3,2,1,0:T(8,128)} %param.11) | copy-start | bytes 3735556
where the time goes:
time: 79.9 us; the launch traced here: 79.4 us
  starting transfers between devices  28.7 us (36%)
  other arithmetic  27.2 us (34%)
  local copies, waits for them, and re-layouts  13.4 us (17%)
  waiting for transfers between devices  9.79 us (12%)
    ppermute x2, starting transfers between devices, with_halo(): lax.ppermute(lax.slice_in_dim(block, 0, width, axis=dim), axis, backward)  16.3 us
    unnamed x17, other arithmetic  12.9 us
    ppermute x2, starting transfers between devices, with_halo(): lax.ppermute(lax.slice_in_dim(block, block.shape[dim] - width, None, axis...  12.5 us
    ppermute x2, waiting for transfers between devices, with_halo(): lax.ppermute(lax.slice_in_dim(block, 0, width, axis=dim), axis, backward)  9.78 us
    select_n x1, other arithmetic, local(): relaxed = jnp.where(live_columns[None], collide(populations), populations)  3.05 us
    slice x2, local copies, waits for them, and re-layouts, with_halo(): lax.slice_in_dim(block, 0, width, axis=dim)  2.89 us
    another operation x1, other arithmetic, live_tile(): jnp.stack([jnp.any(counted & (listed == b)) for b in range(BLOCK_SLOTS)])  2.59 us
    select_n x1, other arithmetic, local_stream(): return jnp.where(active[None], jnp.stack(columns), populations)  2.53 us
  transfers between devices with their start and end apart: 4, of which 2 were waited for; matrix products, arithmetic and copies ran while one was open for 6% of the time, Pallas kernels for 0%

commit v1 on v0

v1 whole, which is shorter than its diff:
```python
import functools

import jax
import jax.numpy as jnp
from jax import lax
from jax.experimental import pallas as pl
from jax.experimental.pallas import tpu as pltpu
from jax.sharding import PartitionSpec as P

F32 = jnp.float32
SIDE = 128
TILES = SIDE // 8
CHUNKS = 4

PAIRS = (
    (1, 2, (1, 0, 0)),
    (3, 4, (0, 1, 0)),
    (5, 6, (0, 0, 1)),
    (7, 8, (1, 1, 0)),
    (9, 10, (1, -1, 0)),
    (11, 12, (1, 0, 1)),
    (13, 14, (1, 0, -1)),
    (15, 16, (0, 1, 1)),
    (17, 18, (0, 1, -1)),
)
VELOCITY = {0: (0, 0, 0)}
OPPOSITE = {0: 0}
for _k, _o, _c in PAIRS:
    VELOCITY[_k], VELOCITY[_o] = _c, tuple(-v for v in _c)
    OPPOSITE[_k], OPPOSITE[_o] = _o, _k
OMEGA_PLUS = 1.0 / 0.8
OMEGA_MINUS = 1.0 / (0.1875 / 0.3 + 0.5)

X_UP, X_DOWN = (1, 7, 9, 11, 13), (2, 8, 10, 12, 14)
Y_UP, Y_DOWN = (3, 7, 10, 15, 17), (4, 8, 9, 16, 18)
Y_ALL = Y_UP + Y_DOWN
REST = tuple(k for k in range(19) if k not in Y_ALL)
FLAG_ROW = (5, 6, 7, 5, 5)


def iota(axis):
    return lax.broadcasted_iota(jnp.int32, (8, SIDE), axis)


def relax(f):
    total = {p: f[k] + f[o] for p, (k, o, _) in enumerate(PAIRS)}
    diff = {p: f[k] - f[o] for p, (k, o, _) in enumerate(PAIRS)}
    density = ((total[0] + total[1]) + (total[2] + total[3])) + (
        (total[4] + total[5]) + (total[6] + total[7])
    )
    density = density + (total[8] + f[0])
    jx = (diff[0] + diff[3]) + (diff[4] + diff[5]) + diff[6]
    jy = (diff[1] + diff[3]) + (diff[7] - diff[4]) + diff[8]
    jz = (diff[2] + diff[5]) + (diff[7] - diff[6]) - diff[8]
    inverse = 1.0 / density
    speed = (jx * inverse, jy * inverse, jz * inverse)
    square = speed[0] * speed[0] + speed[1] * speed[1] + speed[2] * speed[2]
    base = 1.0 - 1.5 * square
    out = {0: f[0] - OMEGA_PLUS * (f[0] - (density * base) * (1.0 / 3.0))}
    for p, (k, o, c) in enumerate(PAIRS):
        weight = 1.0 / 18.0 if p < 3 else 1.0 / 36.0
        dotted = None
        for axis in range(3):
            if c[axis]:
                term = speed[axis] if c[axis] > 0 else -speed[axis]
                dotted = term if dotted is None else dotted + term
        scaled = density * weight
        even = 0.5 * total[p] - scaled * (base + 4.5 * (dotted * dotted))
        odd = 0.5 * diff[p] - scaled * (3.0 * dotted)
        out[k] = f[k] - OMEGA_PLUS * even - OMEGA_MINUS * odd
        out[o] = f[o] - OMEGA_PLUS * even + OMEGA_MINUS * odd
    return out


def collide_kernel(
    count_hbm, list_hbm, f_hbm, m_hbm,
    f_v, r_v, solid_v, active_v, chip_msg, off_msg, y_pre,
    count_ref, list_ref, mask_v, columns, sems,
):
    rows = SIDE // CHUNKS
    first = [
        pltpu.make_async_copy(source, target, sems.at[CHUNKS + n])
        for n, (source, target) in enumerate(
            ((count_hbm, count_ref), (list_hbm, list_ref), (m_hbm, mask_v))
        )
    ]
    copies = []
    for c in range(CHUNKS):
        part = pl.ds(c * rows, rows)
        copies.append(
            pltpu.make_async_copy(f_hbm.at[:, part, :], f_v.at[:, part, :], sems.at[c])
        )
    for copy in first + copies:
        copy.start()
    for copy in first:
        copy.wait()
    position = lax.axis_index("bx")
    count = count_ref[0, position]
    live = []
    for b in range(4):
        hit = jnp.int32(0)
        for s in range(4):
            found = jnp.logical_and(s < count, list_ref[0, 0, s] == b)
            hit = jnp.where(found, jnp.int32(1), hit)
        live.append(hit)
    lane, row = iota(1), iota(0)

    def tile(t, carry):
        at = pl.ds(pl.multiple_of(t * 8, 8), 8)
        low_half = t < TILES // 2
        left = jnp.where(low_half, live[0], live[2])
        right = jnp.where(low_half, live[1], live[3])
        is_live = jnp.where(lane < SIDE // 2, left, right) != 0
        f = [f_v[k, at, :] for k in range(19)]
        out = relax(f)
        out = [jnp.where(is_live, out[k], f[k]) for k in range(19)]
        for k in range(19):
            r_v[k, at, :] = out[k]
        solid = mask_v[at, :].astype(F32)
        solid_v[at, :] = solid
        active_v[at, :] = jnp.where(jnp.logical_and(is_live, solid == 0.0), 1.0, 0.0)
        packed = jnp.zeros((8, SIDE), F32)
        for start, edge, pops in ((0, SIDE - 1, Y_UP), (8, 0, Y_DOWN)):
            for n, k in enumerate(pops):
                packed = jnp.where(lane == start + n, out[k][:, edge : edge + 1], packed)
            flags = jnp.logical_and(lane >= start + 5, lane < start + 8)
            packed = jnp.where(flags, solid[:, edge : edge + 1], packed)
        columns[at, :] = packed
        return carry

    for c in range(CHUNKS):
        copies[c].wait()
        lax.fori_loop(c * (rows // 8), (c + 1) * (rows // 8), tile, 0)

    up = [r_v[k, SIDE - 1 : SIDE, :] for k in X_UP] + [solid_v[SIDE - 1 : SIDE, :]] * 3
    down = [r_v[k, 0:1, :] for k in X_DOWN] + [solid_v[0:1, :]] * 3
    up, down = jnp.concatenate(up, axis=0), jnp.concatenate(down, axis=0)
    even = lax.rem(position, 2) == 0
    chip_msg[...] = jnp.where(even, up, down)
    off_msg[...] = jnp.where(even, down, up)

    turned = jnp.transpose(columns[...])
    high, low = turned[0:8, :], turned[8:16, :]
    fore = jnp.logical_or(row == 1, row == 6)
    back = jnp.logical_or(row == 2, row == 7)
    y_pre[0] = jnp.where(
        fore, pltpu.roll(high, 1, 1), jnp.where(back, pltpu.roll(high, SIDE - 1, 1), high)
    )
    y_pre[1] = jnp.where(
        fore, pltpu.roll(low, SIDE - 1, 1), jnp.where(back, pltpu.roll(low, 1, 1), low)
    )
    for slab, flags, first, second in ((2, low, 0, 2), (3, high, 1, 3)):
        is_live = jnp.where(lane < SIDE // 2, live[first], live[second]) != 0
        free = jnp.broadcast_to(flags[5:6, :], (8, SIDE)) == 0.0
        y_pre[slab] = jnp.where(jnp.logical_and(is_live, free), 1.0, 0.0)


def halos(chip_ref, off_ref):
    parity = lax.rem(lax.axis_index("bx"), 2)
    chip, off = chip_ref[1 - parity], off_ref[...]
    return jnp.where(parity == 0, off, chip), jnp.where(parity == 0, chip, off)


def corner_kernel(y_pre, chip_ref, off_ref, near_msg, far_msg):
    low, high = halos(chip_ref, off_ref)
    lane, row = iota(1), iota(0)
    fore = jnp.logical_or(row == 1, row == 6)
    back = jnp.logical_or(row == 2, row == 7)
    first, last = lane == 0, lane == SIDE - 1
    up = jnp.where(jnp.logical_and(fore, first), pltpu.roll(low, 1, 1), y_pre[0])
    up = jnp.where(jnp.logical_and(back, last), high, up)
    down = jnp.where(jnp.logical_and(fore, last), pltpu.roll(high, SIDE - 1, 1), y_pre[1])
    down = jnp.where(jnp.logical_and(back, first), low, down)
    even = lax.rem(lax.axis_index("by"), 2) == 0
    near_msg[...] = jnp.where(even, up, down)
    far_msg[...] = jnp.where(even, down, up)


def stream_kernel(
    f_v, r_v, solid_v, active_v, chip_ref, off_ref, out_hbm, partial, stage, edges, sems
):
    low, high = halos(chip_ref, off_ref)
    edges[0], edges[1] = low, high
    lane, row = iota(1), iota(0)
    top, bottom = row == 0, row == 7
    first, last = lane == 0, lane == SIDE - 1

    def tile(t, carry):
        at = pl.ds(pl.multiple_of(t * 8, 8), 8)
        before = pl.ds(jnp.maximum(t * 8 - 1, 0), 1)
        after = pl.ds(jnp.minimum(t * 8 + 8, SIDE - 1), 1)

        def shift_x(block, row_before, row_after, step, halo_row):
            if step == 0:
                return block
            if step > 0:
                edge = jnp.where(t == 0, edges[0, halo_row : halo_row + 1, :], row_before())
                return jnp.where(top, edge, pltpu.roll(block, 1, 0))
            edge = jnp.where(t == TILES - 1, edges[1, halo_row : halo_row + 1, :], row_after())
            return jnp.where(bottom, edge, pltpu.roll(block, 7, 0))

        def shift_y(block, step):
            if step == 0:
                return block
            return pltpu.roll(block, 1 if step > 0 else SIDE - 1, 1)

        solid = solid_v[at, :]
        active = active_v[at, :] != 0.0
        blocked = {}
        for sx in (-1, 0, 1):
            moved = shift_x(
                solid, lambda: solid_v[before, :], lambda: solid_v[after, :], sx, 5
            )
            for sy in (-1, 0, 1):
                if sx or sy:
                    hit = shift_y(moved, sy) != 0.0
                    if sy:
                        hit = jnp.logical_or(hit, first if sy > 0 else last)
                    blocked[sx, sy] = hit
        own = [r_v[k, at, :] for k in range(19)]
        for k in range(19):
            sx, sy, _ = VELOCITY[k]
            moved = own[k]
            if sx:
                halo_row = X_UP.index(k) if sx > 0 else X_DOWN.index(k)
                moved = shift_x(
                    moved, lambda: r_v[k, before, :], lambda: r_v[k, after, :], sx, halo_row
                )
            moved = shift_y(moved, sy)
            if sx or sy:
                moved = jnp.where(blocked[sx, sy], own[OPPOSITE[k]], moved)
            result = jnp.where(active, moved, f_v[k, at, :])
            if k in Y_ALL:
                partial[Y_ALL.index(k), at, :] = result
            else:
                stage[REST.index(k), at, :] = result
        return carry

    lax.fori_loop(0, TILES, tile, 0)
    copies = [
        pltpu.make_async_copy(stage.at[n], out_hbm.at[k], sems.at[n]) for n, k in enumerate(REST)
    ]
    for copy in copies:
        copy.start()
    for copy in copies:
        copy.wait()


def patch_kernel(near_ref, far_ref, y_pre, partial, started, out_hbm, stage, sems):
    del started
    even = lax.rem(lax.axis_index("by"), 2) == 0
    near, far = near_ref[...], far_ref[...]
    below, above = jnp.where(even, far, near), jnp.where(even, near, far)
    flags = iota(0) >= 5
    free = [
        jnp.where(flags, jnp.where(message == 0.0, y_pre[slab], 0.0), message)
        for message, slab in ((below, 2), (above, 3))
    ]
    turned = jnp.transpose(
        jnp.concatenate(free + [jnp.zeros((SIDE - 16, SIDE), F32)], axis=0)
    )
    lane = lax.broadcasted_iota(jnp.int32, (SIDE, SIDE), 1)
    copies = []
    for n, k in enumerate(Y_ALL):
        side, which = n // 5, n % 5
        value = turned[:, side * 8 + which : side * 8 + which + 1]
        flag = side * 8 + FLAG_ROW[which]
        take = jnp.logical_and(
            lane == (0 if side == 0 else SIDE - 1), turned[:, flag : flag + 1] != 0.0
        )
        stage[n] = jnp.where(take, value, partial[n])
        copies.append(pltpu.make_async_copy(stage.at[n], out_hbm.at[k], sems.at[n]))
        copies[-1].start()
    for copy in copies:
        copy.wait()


def shape(*dims):
    return jax.ShapeDtypeStruct(dims, F32)


def in_vmem(*dims):
    return pltpu.VMEM(dims, F32)


def keep(x):
    return pltpu.with_memory_space_constraint(x, pltpu.VMEM)


def stay(x):
    return pltpu.with_memory_space_constraint(x, pltpu.HBM)


def pairs_of(count, first):
    pairs = []
    for low in range(first, count, 2):
        high = (low + 1) % count
        pairs += [(low, high), (high, low)]
    return sorted(pairs)


def local(n_bx, n_by, populations, solid_mask, pore_list, pore_count):
    vmem = pl.BlockSpec(memory_space=pltpu.VMEM)
    anywhere = pl.BlockSpec(memory_space=pl.ANY)
    plane = (SIDE, SIDE)
    f = populations.reshape(19, *plane)
    f_v, r_v, solid_v, active_v, chip_msg, off_msg, y_pre = pl.pallas_call(
        collide_kernel,
        out_shape=(
            in_vmem(19, *plane), in_vmem(19, *plane), in_vmem(*plane), in_vmem(*plane),
            in_vmem(8, SIDE), in_vmem(8, SIDE), in_vmem(4, 8, SIDE),
        ),
        in_specs=[pl.BlockSpec(memory_space=pltpu.HBM)] * 4,
        out_specs=[vmem] * 7,
        scratch_shapes=[
            pltpu.SMEM((1, n_bx), jnp.int32), pltpu.SMEM((1, 1, 4), jnp.int32),
            pltpu.VMEM(plane, jnp.int32), pltpu.VMEM(plane, F32),
            pltpu.SemaphoreType.DMA((CHUNKS + 3,)),
        ],
        compiler_params=pltpu.CompilerParams(vmem_limit_bytes=24 * 2**20),
        name="collide",
    )(stay(pore_count.T), stay(pore_list), stay(f), stay(solid_mask.reshape(plane)))

    off = lax.ppermute(off_msg, "bx", pairs_of(n_bx, 1))
    groups = [[low, low + 1] for low in range(0, n_bx, 2)]
    chip = lax.all_gather(chip_msg, "bx", axis_index_groups=groups)

    near_msg, far_msg = pl.pallas_call(
        corner_kernel,
        out_shape=(in_vmem(8, SIDE), in_vmem(8, SIDE)),
        in_specs=[vmem] * 3,
        out_specs=[vmem] * 2,
        name="corner",
    )(keep(y_pre), keep(chip), keep(off))

    near = lax.ppermute(near_msg, "by", pairs_of(n_by, 0))
    far = lax.ppermute(far_msg, "by", pairs_of(n_by, 1))

    out, partial = pl.pallas_call(
        stream_kernel,
        out_shape=(shape(19, *plane), in_vmem(10, *plane)),
        in_specs=[vmem] * 6,
        out_specs=[anywhere, vmem],
        scratch_shapes=[
            pltpu.VMEM((9, *plane), F32), pltpu.VMEM((2, 8, SIDE), F32),
            pltpu.SemaphoreType.DMA((9,)),
        ],
        compiler_params=pltpu.CompilerParams(vmem_limit_bytes=24 * 2**20),
        cost_estimate=pl.CostEstimate(
            flops=8_000_000, bytes_accessed=4_000_000, transcendentals=0
        ),
        name="stream",
    )(keep(f_v), keep(r_v), keep(solid_v), keep(active_v), keep(chip), keep(off))

    out = pl.pallas_call(
        patch_kernel,
        out_shape=shape(19, *plane),
        in_specs=[vmem] * 4 + [anywhere],
        out_specs=anywhere,
        scratch_shapes=[pltpu.VMEM((10, *plane), F32), pltpu.SemaphoreType.DMA((10,))],
        input_output_aliases={4: 0},
        compiler_params=pltpu.CompilerParams(vmem_limit_bytes=24 * 2**20),
        name="patch",
    )(keep(near), keep(far), keep(y_pre), keep(partial), out)
    return out.reshape(19, 1, *plane)


def solution(mesh):
    placed = (P(None, None, "bx", "by"), P(None, "bx", "by"), P("bx", "by", None), P(None, "by"))
    return jax.shard_map(
        functools.partial(local, mesh.shape["bx"], mesh.shape["by"]),
        mesh=mesh,
        in_specs=placed,
        out_specs=P(None, None, "bx", "by"),
        check_vma=False,
    )
```

time: 79.9 us -> 40.2 us (0.50)
  the two profiles are of different devices: /device:TPU:56 before, /device:TPU:1 now
where the time goes in v1:
time: 40.2 us; the launch traced here: 40 us
  starting transfers between devices  20.1 us (50%)
  blocking collectives  12.8 us (32%)
  Pallas kernels  6.91 us (17%)
    all_gather x1, blocking collectives, local(): chip = lax.all_gather(chip_msg, 'bx', axis_index_groups=groups)  12.8 us
    ppermute x1, starting transfers between devices, local(): far = lax.ppermute(far_msg, 'by', pairs_of(n_by, 1))  12.4 us
    ppermute x1, starting transfers between devices, local(): off = lax.ppermute(off_msg, 'bx', pairs_of(n_bx, 1))  4.51 us
    pallas_call x1, Pallas kernels, local(): pl.pallas_call(collide_kernel, out_shape=(in_vmem(19, *plane), in_vmem(19...  3.25 us
    ppermute x1, starting transfers between devices, local(): near = lax.ppermute(near_msg, 'by', pairs_of(n_by, 0))  3.19 us
    pallas_call x1, Pallas kernels, local(): pl.pallas_call(stream_kernel, out_shape=(shape(19, *plane), in_vmem(10, *...  2.37 us
    pallas_call x1, Pallas kernels, local(): pl.pallas_call(patch_kernel, out_shape=shape(19, *plane), in_specs=[vmem]...  1.22 us
  transfers between devices with their start and end apart: 3, of which 0 were waited for; matrix products, arithmetic and copies ran while one was open for 0% of the time, Pallas kernels for 6%

profile of v1, /device:TPU:1, one launch (start us, length us, event | category | flops | bytes accessed | tf_op | source)
XLA Modules:
  0.0 40.0 jit_solution(13811109257682787910)
XLA Ops:
  0.0 3.2 %collide.1 = (f32[19,128,128]{2,1,0:T(8,128)S(1)}, f32[19,128,128]{2,1,0:T(8,128)S(1)}, f32[128,128]{1,0:T(8,128)S(1)}, f32[128,128]{1,0:T(8,128)S(1)}, f32[8,12...) custom-call(s32[1,48]{1,0:T(1,128)} %bitcast.11, s32[1,1,4]{2,1,0:T(1,128)} %list_hbm.1, ...), custom_call_target="tpu_custom_call" | custom-call | tf_op jit(solution)/shard_map/collide/pallas_call | solution.py:307
  3.3 4.5 %collective-permute-start = (f32[8,128]{1,0:T(8,128)S(1)}, f32[8,128]{1,0:T(8,128)S(1)}, u32[]{:S(2)}, u32[]{:S(2)}) collective-permute-start(f32[8,128]{1,0:T(8,128)S(1)} %get-tuple-element.18), channel_id=1, source_target_pairs={{0,752},{16,32},{32,16},{48,64},{64,48},{80,96},{96,80},{112,128},... | collective-permute-start | bytes 12296 | tf_op jit(solution)/shard_map/ppermute | solution.py:324
  7.8 12.8 %all-gather = f32[16,128]{1,0:T(8,128)S(1)} all-gather(f32[8,128]{1,0:T(8,128)S(1)} %get-tuple-element.17), channel_id=2, replica_groups={{0,16},{32,48},{64,80},{96,112},{128,144},{160,176},{192,208},{224,240}..., dimensions={0}, use_global_device_ids=true | all-gather | bytes 12288 | tf_op jit(solution)/shard_map/all_gather | solution.py:326
  20.6 0.0 collective-permute-done.off_ref
  20.6 0.1 corner.1
  20.7 3.2 %collective-permute-start.1 = (f32[8,128]{1,0:T(8,128)S(1)}, f32[8,128]{1,0:T(8,128)S(1)}, u32[]{:S(2)}, u32[]{:S(2)}) collective-permute-start(f32[8,128]{1,0:T(8,128)S(1)} %get-tuple-element.19), channel_id=1, source_target_pairs={{0,1},{1,0},{2,3},{3,2},{4,5},{5,4},{6,7},{7,6},{8,9},{9,8},{10,11... | collective-permute-start | bytes 12296 | tf_op jit(solution)/shard_map/ppermute | solution.py:336
  23.9 12.4 %collective-permute-start.2 = (f32[8,128]{1,0:T(8,128)S(1)}, f32[8,128]{1,0:T(8,128)S(1)}, u32[]{:S(2)}, u32[]{:S(2)}) collective-permute-start(f32[8,128]{1,0:T(8,128)S(1)} %get-tuple-element.20), channel_id=1, source_target_pairs={{0,15},{1,2},{2,1},{3,4},{4,3},{5,6},{6,5},{7,8},{8,7},{9,10},{10,... | collective-permute-start | bytes 12296 | tf_op jit(solution)/shard_map/ppermute | solution.py:337
  36.4 2.4 %stream.1 = (f32[19,128,128]{2,1,0:T(8,128)}, f32[10,128,128]{2,1,0:T(8,128)S(1)}) custom-call(f32[19,128,128]{2,1,0:T(8,128)S(1)} %get-tuple-element.21.f_v, f32[19,128,128]{2,1,0:T(8,128)S(1)} %get-tuple-element.22.r_v, f32[128,128]{1,0:T(8,128)S(1)} %get-tuple-element.23.solid_v, f32[128,128]{1,0:T(8,128)S(1)} %get-tuple-element.24.active_v, ...), custom_call_target="tpu_custom_call" | custom-call | flops 8000000 | bytes 4000000 | tf_op jit(solution)/shard_map/stream/pallas_call | solution.py:339
  38.7 0.0 collective-permute-done.1.near_ref
  38.7 0.0 collective-permute-done.2.far_ref
  38.7 1.2 %patch.1 = f32[19,128,128]{2,1,0:T(8,128)} custom-call(f32[8,128]{1,0:T(8,128)S(1)} %collective-permute-done.1.near_ref, f32[8,128]{1,0:T(8,128)S(1)} %collective-permute-done.2.far_ref, f32[4,8,128]{2,1,0:T(8,128)S(1)} %get-tuple-element.16.y_pre, f32[10,128,128]{2,1,0:T(8,128)S(1)} %get-tuple-element.25.partial, ...), custom_call_target="tpu_custom_call", output_to_operand_aliasing={{}: (4, {})} | custom-call | tf_op jit(solution)/shard_map/patch/pallas_call | solution.py:355
Async XLA Ops:
  3.3 17.4 %collective-permute-start = (f32[8,128]{1,0:T(8,128)S(1)}, f32[8,128]{1,0:T(8,128)S(1)}, u32[]{:S(2)}, u32[]{:S(2)}) collective-permute-start(f32[8,128]{1,0:T(8,128)S(1)} %get-tuple-element.18), channel_id=1, source_target_pairs={{0,752},{16,32},{32,16},{48,64},{64,48},{80,96},{96,80},{112,128},... | collective-permute-start | bytes 12296 | tf_op jit(solution)/shard_map/ppermute | solution.py:324
  20.7 18.0 %collective-permute-start.1 = (f32[8,128]{1,0:T(8,128)S(1)}, f32[8,128]{1,0:T(8,128)S(1)}, u32[]{:S(2)}, u32[]{:S(2)}) collective-permute-start(f32[8,128]{1,0:T(8,128)S(1)} %get-tuple-element.19), channel_id=1, source_target_pairs={{0,1},{1,0},{2,3},{3,2},{4,5},{5,4},{6,7},{7,6},{8,9},{9,8},{10,11... | collective-permute-start | bytes 12296 | tf_op jit(solution)/shard_map/ppermute | solution.py:336
  23.9 14.8 %collective-permute-start.2 = (f32[8,128]{1,0:T(8,128)S(1)}, f32[8,128]{1,0:T(8,128)S(1)}, u32[]{:S(2)}, u32[]{:S(2)}) collective-permute-start(f32[8,128]{1,0:T(8,128)S(1)} %get-tuple-element.20), channel_id=1, source_target_pairs={{0,15},{1,2},{2,1},{3,4},{4,3},{5,6},{6,5},{7,8},{8,7},{9,10},{10,... | collective-permute-start | bytes 12296 | tf_op jit(solution)/shard_map/ppermute | solution.py:337

commit v2 on v1

v2 whole, which is shorter than its diff:
```python
import functools

import jax
import jax.numpy as jnp
from jax import lax
from jax.experimental import pallas as pl
from jax.experimental.pallas import tpu as pltpu
from jax.sharding import PartitionSpec as P

F32 = jnp.float32
SIDE = 128
TILES = SIDE // 8
CHUNKS = 4

PAIRS = (
    (1, 2, (1, 0, 0)),
    (3, 4, (0, 1, 0)),
    (5, 6, (0, 0, 1)),
    (7, 8, (1, 1, 0)),
    (9, 10, (1, -1, 0)),
    (11, 12, (1, 0, 1)),
    (13, 14, (1, 0, -1)),
    (15, 16, (0, 1, 1)),
    (17, 18, (0, 1, -1)),
)
VELOCITY = {0: (0, 0, 0)}
OPPOSITE = {0: 0}
for _k, _o, _c in PAIRS:
    VELOCITY[_k], VELOCITY[_o] = _c, tuple(-v for v in _c)
    OPPOSITE[_k], OPPOSITE[_o] = _o, _k
OMEGA_PLUS = 1.0 / 0.8
OMEGA_MINUS = 1.0 / (0.1875 / 0.3 + 0.5)

X_UP, X_DOWN = (1, 7, 9, 11, 13), (2, 8, 10, 12, 14)
Y_UP, Y_DOWN = (3, 7, 10, 15, 17), (4, 8, 9, 16, 18)
Y_ALL = Y_UP + Y_DOWN
X_ALL = X_UP + X_DOWN
REST = tuple(k for k in range(19) if k not in Y_ALL)
FLAG_ROW = (5, 6, 7, 5, 5)


def iota(axis):
    return lax.broadcasted_iota(jnp.int32, (8, SIDE), axis)


def relax(f):
    total = {p: f[k] + f[o] for p, (k, o, _) in enumerate(PAIRS)}
    diff = {p: f[k] - f[o] for p, (k, o, _) in enumerate(PAIRS)}
    density = ((total[0] + total[1]) + (total[2] + total[3])) + (
        (total[4] + total[5]) + (total[6] + total[7])
    )
    density = density + (total[8] + f[0])
    jx = (diff[0] + diff[3]) + (diff[4] + diff[5]) + diff[6]
    jy = (diff[1] + diff[3]) + (diff[7] - diff[4]) + diff[8]
    jz = (diff[2] + diff[5]) + (diff[7] - diff[6]) - diff[8]
    inverse = 1.0 / density
    speed = (jx * inverse, jy * inverse, jz * inverse)
    square = speed[0] * speed[0] + speed[1] * speed[1] + speed[2] * speed[2]
    base = 1.0 - 1.5 * square
    out = {0: f[0] - OMEGA_PLUS * (f[0] - (density * base) * (1.0 / 3.0))}
    for p, (k, o, c) in enumerate(PAIRS):
        weight = 1.0 / 18.0 if p < 3 else 1.0 / 36.0
        dotted = None
        for axis in range(3):
            if c[axis]:
                term = speed[axis] if c[axis] > 0 else -speed[axis]
                dotted = term if dotted is None else dotted + term
        scaled = density * weight
        even = 0.5 * total[p] - scaled * (base + 4.5 * (dotted * dotted))
        odd = 0.5 * diff[p] - scaled * (3.0 * dotted)
        out[k] = f[k] - OMEGA_PLUS * even - OMEGA_MINUS * odd
        out[o] = f[o] - OMEGA_PLUS * even + OMEGA_MINUS * odd
    return out


def is_early():
    return jnp.logical_and(
        lax.axis_index("bx") < lax.axis_size("bx") // 2,
        lax.axis_index("by") < lax.axis_size("by") // 2,
    )


def stream_interior(f_v, r_v, solid_v, active_v, partial):
    lane, row = iota(1), iota(0)
    first, last = lane == 0, lane == SIDE - 1

    def tile(t, carry):
        at = pl.ds(pl.multiple_of(t * 8, 8), 8)
        before = pl.ds(jnp.maximum(t * 8 - 1, 0), 1)
        after = pl.ds(jnp.minimum(t * 8 + 8, SIDE - 1), 1)
        top, bottom = row == 0, row == 7
        outer_top = row == jnp.where(t == 0, 0, -1)
        outer_bottom = row == jnp.where(t == TILES - 1, 7, -1)

        def shift_x(ref, block, step):
            if step > 0:
                return jnp.where(top, ref[before, :], pltpu.roll(block, 1, 0))
            if step < 0:
                return jnp.where(bottom, ref[after, :], pltpu.roll(block, 7, 0))
            return block

        def shift_y(block, step):
            return pltpu.roll(block, 1 if step > 0 else SIDE - 1, 1) if step else block

        solid = solid_v[at, :]
        active = active_v[at, :] != 0.0
        blocked = {}
        for sx in (-1, 0, 1):
            moved = shift_x(solid_v, solid, sx)
            for sy in (-1, 0, 1):
                if sx or sy:
                    hit = shift_y(moved, sy) != 0.0
                    if sx:
                        hit = jnp.logical_or(hit, outer_top if sx > 0 else outer_bottom)
                    if sy:
                        hit = jnp.logical_or(hit, first if sy > 0 else last)
                    blocked[sx, sy] = hit
        own = [r_v[k, at, :] for k in range(19)]
        for k in range(19):
            sx, sy, _ = VELOCITY[k]
            moved = shift_y(shift_x(r_v.at[k], own[k], sx), sy)
            if sx or sy:
                moved = jnp.where(blocked[sx, sy], own[OPPOSITE[k]], moved)
            partial[k, at, :] = jnp.where(active, moved, f_v[k, at, :])
        return carry

    lax.fori_loop(0, TILES, tile, 0)


def collide_kernel(
    count_hbm, list_hbm, f_hbm, m_hbm,
    f_v, r_v, solid_v, active_v, near_msg, far_msg, y_active, partial,
    count_ref, list_ref, mask_v, columns, sems,
):
    rows = SIDE // CHUNKS
    first = [
        pltpu.make_async_copy(source, target, sems.at[CHUNKS + n])
        for n, (source, target) in enumerate(
            ((count_hbm, count_ref), (list_hbm, list_ref), (m_hbm, mask_v))
        )
    ]
    copies = []
    for c in range(CHUNKS):
        part = pl.ds(c * rows, rows)
        copies.append(
            pltpu.make_async_copy(f_hbm.at[:, part, :], f_v.at[:, part, :], sems.at[c])
        )
    for copy in first + copies:
        copy.start()
    for copy in first:
        copy.wait()
    position = lax.axis_index("bx")
    count = count_ref[0, position]
    live = []
    for b in range(4):
        hit = jnp.int32(0)
        for s in range(4):
            found = jnp.logical_and(s < count, list_ref[0, 0, s] == b)
            hit = jnp.where(found, jnp.int32(1), hit)
        live.append(hit)
    lane = iota(1)

    def tile(t, carry):
        at = pl.ds(pl.multiple_of(t * 8, 8), 8)
        low_half = t < TILES // 2
        left = jnp.where(low_half, live[0], live[2])
        right = jnp.where(low_half, live[1], live[3])
        is_live = jnp.where(lane < SIDE // 2, left, right) != 0
        f = [f_v[k, at, :] for k in range(19)]
        out = relax(f)
        out = [jnp.where(is_live, out[k], f[k]) for k in range(19)]
        for k in range(19):
            r_v[k, at, :] = out[k]
        solid = mask_v[at, :].astype(F32)
        solid_v[at, :] = solid
        active_v[at, :] = jnp.where(jnp.logical_and(is_live, solid == 0.0), 1.0, 0.0)
        packed = jnp.zeros((8, SIDE), F32)
        for start, edge, pops in ((0, SIDE - 1, Y_UP), (8, 0, Y_DOWN)):
            for n, k in enumerate(pops):
                packed = jnp.where(lane == start + n, out[k][:, edge : edge + 1], packed)
            flags = jnp.logical_and(lane >= start + 5, lane < start + 8)
            packed = jnp.where(flags, solid[:, edge : edge + 1], packed)
        columns[at, :] = packed
        return carry

    for c in range(CHUNKS):
        copies[c].wait()
        lax.fori_loop(c * (rows // 8), (c + 1) * (rows // 8), tile, 0)

    turned = jnp.transpose(columns[...])
    up, down = turned[0:8, :], turned[8:16, :]
    even = lax.rem(lax.axis_index("by"), 2) == 0
    near_msg[...] = jnp.where(even, up, down)
    far_msg[...] = jnp.where(even, down, up)
    for slab, flags in ((0, down), (1, up)):
        is_live = jnp.where(lane < SIDE // 2, live[slab], live[2 + slab]) != 0
        free = jnp.broadcast_to(flags[5:6, :], (8, SIDE)) == 0.0
        y_active[slab] = jnp.where(jnp.logical_and(is_live, free), 1.0, 0.0)

    @pl.when(is_early())
    def _():
        stream_interior(f_v, r_v, solid_v, active_v, partial)


def stream_kernel(f_v, r_v, solid_v, active_v, begun, partial):
    del begun

    @pl.when(jnp.logical_not(is_early()))
    def _():
        stream_interior(f_v, r_v, solid_v, active_v, partial)


def from_sides(axis, near_ref, far_ref):
    even = lax.rem(lax.axis_index(axis), 2) == 0
    near, far = near_ref[...], far_ref[...]
    return jnp.where(even, far, near), jnp.where(even, near, far)


def corner_kernel(r_v, solid_v, partial, far_ref, near_ref, chip_msg, off_msg, wrap_msg):
    del partial
    below, above = from_sides("by", near_ref, far_ref)
    lane, row = iota(1), iota(0)
    fore = jnp.logical_or(row == 1, row == 6)
    back = jnp.logical_or(row == 2, row == 7)

    def message(pops, x, from_below, from_above):
        edge = pl.ds(x, 1)
        rows = [r_v[k, edge, :] for k in pops] + [solid_v[edge, :]] * 3
        rows = jnp.concatenate(rows, axis=0)
        lower = jnp.broadcast_to(below[:, x : x + 1], (8, SIDE))
        upper = jnp.broadcast_to(above[:, x : x + 1], (8, SIDE))
        raised = jnp.where(lane == 0, lower, pltpu.roll(rows, 1, 1))
        lowered = jnp.where(lane == SIDE - 1, upper, pltpu.roll(rows, SIDE - 1, 1))
        return jnp.where(from_below, raised, jnp.where(from_above, lowered, rows))

    up = message(X_UP, SIDE - 1, fore, back)
    down = message(X_DOWN, 0, back, fore)
    even = lax.rem(lax.axis_index("bx"), 2) == 0
    chip_msg[...] = jnp.where(even, up, down)
    off_msg[...] = jnp.where(even, down, up)
    wrap_msg[...] = jnp.where(even, down, up)


def y_patch_kernel(far_ref, near_ref, y_active, partial, out_hbm, edges, stage, sems):
    copies = [
        pltpu.make_async_copy(partial.at[k], out_hbm.at[k], sems.at[10 + n])
        for n, k in enumerate(REST)
    ]
    for copy in copies:
        copy.start()
    below, above = from_sides("by", near_ref, far_ref)
    flags = iota(0) >= 5
    messages = []
    lane8, row8 = iota(1), iota(0)
    fore = jnp.logical_or(row8 == 1, row8 == 6)
    back = jnp.logical_or(row8 == 2, row8 == 7)
    for message, slab, step in ((below, 0, 1), (above, 1, -1)):
        raised, lowered = pltpu.roll(message, 1, 1), pltpu.roll(message, SIDE - 1, 1)
        ahead, behind = (fore, back) if step > 0 else (back, fore)
        moved = jnp.where(ahead, raised, jnp.where(behind, lowered, message))
        outside = jnp.logical_or(
            jnp.logical_and(ahead, lane8 == 0), jnp.logical_and(behind, lane8 == SIDE - 1)
        )
        free = jnp.logical_and(moved == 0.0, jnp.logical_not(outside))
        messages.append(jnp.where(flags, jnp.where(free, y_active[slab], 0.0), moved))
    turned = jnp.transpose(
        jnp.concatenate(messages + [jnp.zeros((SIDE - 16, SIDE), F32)], axis=0)
    )
    lane = lax.broadcasted_iota(jnp.int32, (SIDE, SIDE), 1)
    for n, k in enumerate(Y_ALL):
        side, which = n // 5, n % 5
        value = turned[:, side * 8 + which : side * 8 + which + 1]
        flag = side * 8 + FLAG_ROW[which]
        take = jnp.logical_and(
            lane == (0 if side == 0 else SIDE - 1), turned[:, flag : flag + 1] != 0.0
        )
        stage[n] = jnp.where(take, value, partial[k])
        copies.append(pltpu.make_async_copy(stage.at[n], out_hbm.at[k], sems.at[n]))
        copies[-1].start()
    for n, k in enumerate(X_ALL):
        at = pl.ds(0 if n < 5 else SIDE - 8, 8)
        edges[n] = stage[Y_ALL.index(k), at, :] if k in Y_ALL else partial[k, at, :]
    for copy in copies:
        copy.wait()


def x_patch_kernel(off_ref, chip_ref, wrap_ref, active_v, edges, started, out_hbm, stage, sems):
    del started
    position = lax.axis_index("bx")
    outer = jnp.logical_or(position == 0, position == lax.axis_size("bx") - 1)
    even = lax.rem(position, 2) == 0
    chip, off = chip_ref[...], jnp.where(outer, wrap_ref[...], off_ref[...])
    below, above = jnp.where(even, off, chip), jnp.where(even, chip, off)
    row = iota(0)
    copies = []
    for n, k in enumerate(X_ALL):
        side, which = n // 5, n % 5
        message = below if side == 0 else above
        at = pl.ds(0 if side == 0 else SIDE - 8, 8)
        flag = FLAG_ROW[which]
        take = jnp.logical_and(active_v[at, :] != 0.0, message[flag : flag + 1, :] == 0.0)
        take = jnp.logical_and(take, row == (0 if side == 0 else 7))
        stage[n] = jnp.where(take, message[which : which + 1, :], edges[n])
        copies.append(pltpu.make_async_copy(stage.at[n], out_hbm.at[k, at, :], sems.at[n]))
        copies[-1].start()
    for copy in copies:
        copy.wait()


def shape(*dims):
    return jax.ShapeDtypeStruct(dims, F32)


def in_vmem(*dims):
    return pltpu.VMEM(dims, F32)


def keep(x):
    return pltpu.with_memory_space_constraint(x, pltpu.VMEM)


def stay(x):
    return pltpu.with_memory_space_constraint(x, pltpu.HBM)


def pairs_of(first, last):
    pairs = []
    for low in range(first, last, 2):
        pairs += [(low, low + 1), (low + 1, low)]
    return pairs


def wrap_pairs(count):
    return [(count - 1, 0), (0, count - 1)]


def local(n_bx, n_by, populations, solid_mask, pore_list, pore_count):
    vmem = pl.BlockSpec(memory_space=pltpu.VMEM)
    anywhere = pl.BlockSpec(memory_space=pl.ANY)
    params = pltpu.CompilerParams(vmem_limit_bytes=24 * 2**20)
    plane = (SIDE, SIDE)
    f = populations.reshape(19, *plane)
    f_v, r_v, solid_v, active_v, near_msg, far_msg, y_active, partial = pl.pallas_call(
        collide_kernel,
        out_shape=(
            in_vmem(19, *plane), in_vmem(19, *plane), in_vmem(*plane), in_vmem(*plane),
            in_vmem(8, SIDE), in_vmem(8, SIDE), in_vmem(2, 8, SIDE), in_vmem(19, *plane),
        ),
        in_specs=[pl.BlockSpec(memory_space=pltpu.HBM)] * 4,
        out_specs=[vmem] * 8,
        scratch_shapes=[
            pltpu.SMEM((1, n_bx), jnp.int32), pltpu.SMEM((1, 1, 4), jnp.int32),
            pltpu.VMEM(plane, jnp.int32), pltpu.VMEM(plane, F32),
            pltpu.SemaphoreType.DMA((CHUNKS + 3,)),
        ],
        compiler_params=params,
        name="collide",
    )(stay(pore_count.T), stay(pore_list), stay(f), stay(solid_mask.reshape(plane)))

    far = lax.ppermute(far_msg, "by", pairs_of(1, n_by - 1) + wrap_pairs(n_by))
    near = lax.ppermute(near_msg, "by", pairs_of(0, n_by))

    partial = pl.pallas_call(
        stream_kernel,
        out_shape=in_vmem(19, *plane),
        in_specs=[vmem] * 5,
        out_specs=vmem,
        input_output_aliases={4: 0},
        compiler_params=params,
        cost_estimate=pl.CostEstimate(
            flops=8_000_000, bytes_accessed=4_000_000, transcendentals=0
        ),
        name="stream",
    )(keep(f_v), keep(r_v), keep(solid_v), keep(active_v), keep(partial))

    chip_msg, off_msg, wrap_msg = pl.pallas_call(
        corner_kernel,
        out_shape=(in_vmem(8, SIDE),) * 3,
        in_specs=[vmem] * 5,
        out_specs=[vmem] * 3,
        compiler_params=params,
        name="corner",
    )(keep(r_v), keep(solid_v), keep(partial), keep(far), keep(near))

    off = lax.ppermute(off_msg, "bx", pairs_of(1, n_bx - 1))
    chip = lax.ppermute(chip_msg, "bx", pairs_of(0, n_bx))
    wrap = lax.ppermute(wrap_msg, "bx", wrap_pairs(n_bx))

    out, edges = pl.pallas_call(
        y_patch_kernel,
        out_shape=(shape(19, *plane), in_vmem(10, 8, SIDE)),
        in_specs=[vmem] * 4,
        out_specs=[anywhere, vmem],
        scratch_shapes=[pltpu.VMEM((10, *plane), F32), pltpu.SemaphoreType.DMA((19,))],
        compiler_params=params,
        cost_estimate=pl.CostEstimate(
            flops=8_000_000, bytes_accessed=4_000_000, transcendentals=0
        ),
        name="y_patch",
    )(keep(far), keep(near), keep(y_active), keep(partial))

    out = pl.pallas_call(
        x_patch_kernel,
        out_shape=shape(19, *plane),
        in_specs=[vmem] * 5 + [anywhere],
        out_specs=anywhere,
        scratch_shapes=[pltpu.VMEM((10, 8, SIDE), F32), pltpu.SemaphoreType.DMA((10,))],
        input_output_aliases={5: 0},
        compiler_params=params,
        name="x_patch",
    )(keep(off), keep(chip), keep(wrap), keep(active_v), keep(edges), out)
    return out.reshape(19, 1, *plane)


def solution(mesh):
    placed = (P(None, None, "bx", "by"), P(None, "bx", "by"), P("bx", "by", None), P(None, "by"))
    return jax.shard_map(
        functools.partial(local, mesh.shape["bx"], mesh.shape["by"]),
        mesh=mesh,
        in_specs=placed,
        out_specs=P(None, None, "bx", "by"),
        check_vma=False,
    )
```

time: 40.2 us -> 43.5 us (1.082)
  the two profiles are of different devices: /device:TPU:1 before, /device:TPU:8 now
where the time goes in v2:
time: 43.5 us; the launch traced here: 43.3 us
  starting transfers between devices  32.1 us (74%)
  Pallas kernels  6.9 us (16%)
  waiting for transfers between devices  4.2 us (10%)
    ppermute x1, starting transfers between devices, local(): near = lax.ppermute(near_msg, 'by', pairs_of(0, n_by))  15.4 us
    ppermute x1, starting transfers between devices, local(): wrap = lax.ppermute(wrap_msg, 'bx', wrap_pairs(n_bx))  7.73 us
    ppermute x1, starting transfers between devices, local(): chip = lax.ppermute(chip_msg, 'bx', pairs_of(0, n_bx))  4.76 us
    pallas_call x1, Pallas kernels, local(): pl.pallas_call(collide_kernel, out_shape=(in_vmem(19, *plane), in_vmem(19...  4.66 us
    ppermute x1, starting transfers between devices, local(): far = lax.ppermute(far_msg, 'by', pairs_of(1, n_by - 1) + wrap_pairs(n_by))  3.48 us
    ppermute x1, waiting for transfers between devices, local(): wrap = lax.ppermute(wrap_msg, 'bx', wrap_pairs(n_bx))  2.67 us
    ppermute x1, waiting for transfers between devices, local(): near = lax.ppermute(near_msg, 'by', pairs_of(0, n_by))  1.53 us
    pallas_call x1, Pallas kernels, local(): pl.pallas_call(y_patch_kernel, out_shape=(shape(19, *plane), in_vmem(10,...  1.4 us
  transfers between devices with their start and end apart: 5, of which 2 were waited for; matrix products, arithmetic and copies ran while one was open for 0% of the time, Pallas kernels for 3%

profile of v2, /device:TPU:8, one launch (start us, length us, event | category | flops | bytes accessed | tf_op | source)
XLA Modules:
  0.0 43.3 jit_solution(10608401919095504283)
XLA Ops:
  0.0 4.7 %collide.1 = (f32[19,128,128]{2,1,0:T(8,128)S(1)}, f32[19,128,128]{2,1,0:T(8,128)S(1)}, f32[128,128]{1,0:T(8,128)S(1)}, f32[128,128]{1,0:T(8,128)S(1)}, f32[8,12...) custom-call(s32[1,48]{1,0:T(1,128)} %bitcast.8, ...), custom_call_target="tpu_custom_call" | custom-call | tf_op jit(solution)/shard_map/collide/pallas_call | solution.py:343
  4.7 3.5 %collective-permute-start = (f32[8,128]{1,0:T(8,128)S(1)}, f32[8,128]{1,0:T(8,128)S(1)}, u32[]{:S(2)}, u32[]{:S(2)}) collective-permute-start(f32[8,128]{1,0:T(8,128)S(1)} %get-tuple-element.23), channel_id=1, source_target_pairs={{1,2},{2,1},{3,4},{4,3},{5,6},{6,5},{7,8},{8,7},{9,10},{10,9},{11,... | collective-permute-start | bytes 12296 | tf_op jit(solution)/shard_map/ppermute | solution.py:360
  8.2 15.4 %collective-permute-start.1 = (f32[8,128]{1,0:T(8,128)S(1)}, f32[8,128]{1,0:T(8,128)S(1)}, u32[]{:S(2)}, u32[]{:S(2)}) collective-permute-start(f32[8,128]{1,0:T(8,128)S(1)} %get-tuple-element.24), channel_id=1, source_target_pairs={{0,1},{1,0},{2,3},{3,2},{4,5},{5,4},{6,7},{7,6},{8,9},{9,8},{10,11... | collective-permute-start | bytes 12296 | tf_op jit(solution)/shard_map/ppermute | solution.py:361
  23.6 0.0 collective-permute-done.far_ref
  23.6 1.5 %collective-permute-done.1.near_ref = f32[8,128]{1,0:T(8,128)S(1)} collective-permute-done((f32[8,128]{1,0:T(8,128)S(1)}, f32[8,128]{1,0:T(8,128)S(1)}, u32[]{:S(2)}, u32[]{:S(2)}) %collective-permute-start.1) | collective-permute-done | bytes 4128 | tf_op jit(solution)/shard_map/ppermute | solution.py:361
  25.2 0.1 corner.1
  25.3 0.7 %collective-permute-start.2 = (f32[8,128]{1,0:T(8,128)S(1)}, f32[8,128]{1,0:T(8,128)S(1)}, u32[]{:S(2)}, u32[]{:S(2)}) collective-permute-start(f32[8,128]{1,0:T(8,128)S(1)} %get-tuple-element.25), channel_id=1, source_target_pairs={{16,32},{32,16},{48,64},{64,48},{80,96},{96,80},{112,128},{128,112... | collective-permute-start | bytes 12296 | tf_op jit(solution)/shard_map/ppermute | solution.py:385
  25.9 4.8 %collective-permute-start.3 = (f32[8,128]{1,0:T(8,128)S(1)}, f32[8,128]{1,0:T(8,128)S(1)}, u32[]{:S(2)}, u32[]{:S(2)}) collective-permute-start(f32[8,128]{1,0:T(8,128)S(1)} %get-tuple-element.26), channel_id=1, source_target_pairs={{0,16},{16,0},{32,48},{48,32},{64,80},{80,64},{96,112},{112,96},{1... | collective-permute-start | bytes 12296 | tf_op jit(solution)/shard_map/ppermute | solution.py:386
  30.7 7.7 %collective-permute-start.4 = (f32[8,128]{1,0:T(8,128)S(1)}, f32[8,128]{1,0:T(8,128)S(1)}, u32[]{:S(2)}, u32[]{:S(2)}) collective-permute-start(f32[8,128]{1,0:T(8,128)S(1)} %get-tuple-element.27), channel_id=1, source_target_pairs={{752,0},{0,752},{753,1},{1,753},{754,2},{2,754},{755,3},{3,755},{7... | collective-permute-start | bytes 12296 | tf_op jit(solution)/shard_map/ppermute | solution.py:387
  38.4 1.4 %y_patch.1 = (f32[19,128,128]{2,1,0:T(8,128)}, f32[10,8,128]{2,1,0:T(8,128)S(1)}) custom-call(f32[8,128]{1,0:T(8,128)S(1)} %collective-permute-done.far_ref, f32[8,128]{1,0:T(8,128)S(1)} %collective-permute-done.1.near_ref, f32[2,8,128]{2,1,0:T(8,128)S(1)} %get-tuple-element.28.y_active, f32[19,128,128]{2,1,0:T(8,128)S(1)} %stream.1.partial), custom_call_target="tpu_custom_call" | custom-call | flops 8000000 | bytes 4000000 | tf_op jit(solution)/shard_map/y_patch/pallas_call | solution.py:389
  39.8 0.0 collective-permute-done.2.off_ref
  39.9 0.0 collective-permute-done.3.chip_ref
  39.9 2.7 %collective-permute-done.4.wrap_ref = f32[8,128]{1,0:T(8,128)S(1)} collective-permute-done((f32[8,128]{1,0:T(8,128)S(1)}, f32[8,128]{1,0:T(8,128)S(1)}, u32[]{:S(2)}, u32[]{:S(2)}) %collective-permute-start.4) | collective-permute-done | bytes 4128 | tf_op jit(solution)/shard_map/ppermute | solution.py:387
  42.5 0.7 %x_patch.1 = f32[19,128,128]{2,1,0:T(8,128)} custom-call(f32[8,128]{1,0:T(8,128)S(1)} %collective-permute-done.2.off_ref, f32[8,128]{1,0:T(8,128)S(1)} %collective-permute-done.3.chip_ref, f32[8,128]{1,0:T(8,128)S(1)} %collective-permute-done.4.wrap_ref, f32[128,128]{1,0:T(8,128)S(1)} %get-tuple-element.21.active_v, ...), custom_call_target="tpu_custom_call", output_to_operand_aliasing={{}: (5, {})} | custom-call | tf_op jit(solution)/shard_map/x_patch/pallas_call | solution.py:402
  (1 shorter events, 0.0 us)
Async XLA Ops:
  4.7 19.0 %collective-permute-start = (f32[8,128]{1,0:T(8,128)S(1)}, f32[8,128]{1,0:T(8,128)S(1)}, u32[]{:S(2)}, u32[]{:S(2)}) collective-permute-start(f32[8,128]{1,0:T(8,128)S(1)} %get-tuple-element.23), channel_id=1, source_target_pairs={{1,2},{2,1},{3,4},{4,3},{5,6},{6,5},{7,8},{8,7},{9,10},{10,9},{11,... | collective-permute-start | bytes 12296 | tf_op jit(solution)/shard_map/ppermute | solution.py:360
  8.2 17.0 %collective-permute-start.1 = (f32[8,128]{1,0:T(8,128)S(1)}, f32[8,128]{1,0:T(8,128)S(1)}, u32[]{:S(2)}, u32[]{:S(2)}) collective-permute-start(f32[8,128]{1,0:T(8,128)S(1)} %get-tuple-element.24), channel_id=1, source_target_pairs={{0,1},{1,0},{2,3},{3,2},{4,5},{5,4},{6,7},{7,6},{8,9},{9,8},{10,11... | collective-permute-start | bytes 12296 | tf_op jit(solution)/shard_map/ppermute | solution.py:361
  25.3 14.6 %collective-permute-start.2 = (f32[8,128]{1,0:T(8,128)S(1)}, f32[8,128]{1,0:T(8,128)S(1)}, u32[]{:S(2)}, u32[]{:S(2)}) collective-permute-start(f32[8,128]{1,0:T(8,128)S(1)} %get-tuple-element.25), channel_id=1, source_target_pairs={{16,32},{32,16},{48,64},{64,48},{80,96},{96,80},{112,128},{128,112... | collective-permute-start | bytes 12296 | tf_op jit(solution)/shard_map/ppermute | solution.py:385
  25.9 13.9 %collective-permute-start.3 = (f32[8,128]{1,0:T(8,128)S(1)}, f32[8,128]{1,0:T(8,128)S(1)}, u32[]{:S(2)}, u32[]{:S(2)}) collective-permute-start(f32[8,128]{1,0:T(8,128)S(1)} %get-tuple-element.26), channel_id=1, source_target_pairs={{0,16},{16,0},{32,48},{48,32},{64,80},{80,64},{96,112},{112,96},{1... | collective-permute-start | bytes 12296 | tf_op jit(solution)/shard_map/ppermute | solution.py:386
  30.7 11.8 %collective-permute-start.4 = (f32[8,128]{1,0:T(8,128)S(1)}, f32[8,128]{1,0:T(8,128)S(1)}, u32[]{:S(2)}, u32[]{:S(2)}) collective-permute-start(f32[8,128]{1,0:T(8,128)S(1)} %get-tuple-element.27), channel_id=1, source_target_pairs={{752,0},{0,752},{753,1},{1,753},{754,2},{2,754},{755,3},{3,755},{7... | collective-permute-start | bytes 12296 | tf_op jit(solution)/shard_map/ppermute | solution.py:387

commit v3 on v1

--- a/solution.py
+++ b/solution.py
@@ -72,30 +72,19 @@
     return out
 
 
-def collide_kernel(
-    count_hbm, list_hbm, f_hbm, m_hbm,
-    f_v, r_v, solid_v, active_v, chip_msg, off_msg, y_pre,
-    count_ref, list_ref, mask_v, columns, sems,
-):
-    rows = SIDE // CHUNKS
-    first = [
-        pltpu.make_async_copy(source, target, sems.at[CHUNKS + n])
-        for n, (source, target) in enumerate(
-            ((count_hbm, count_ref), (list_hbm, list_ref), (m_hbm, mask_v))
-        )
-    ]
-    copies = []
-    for c in range(CHUNKS):
-        part = pl.ds(c * rows, rows)
-        copies.append(
-            pltpu.make_async_copy(f_hbm.at[:, part, :], f_v.at[:, part, :], sems.at[c])
-        )
-    for copy in first + copies:
-        copy.start()
-    for copy in first:
-        copy.wait()
-    position = lax.axis_index("bx")
-    count = count_ref[0, position]
+def is_early():
+    position = lax.axis_index("bx") + lax.axis_index("by")
+    return jnp.logical_and(
+        jnp.logical_and(
+            lax.axis_index("bx") < lax.axis_size("bx") // 2,
+            lax.axis_index("by") < lax.axis_size("by") // 2,
+        ),
+        position > 0,
+    )
+
+
+def live_blocks(count_ref, list_ref):
+    count = count_ref[0, lax.axis_index("bx")]
     live = []
     for b in range(4):
         hit = jnp.int32(0)
@@ -103,14 +92,23 @@
             found = jnp.logical_and(s < count, list_ref[0, 0, s] == b)
             hit = jnp.where(found, jnp.int32(1), hit)
         live.append(hit)
+    return live
+
+
+def live_lanes(live, t):
+    low_half = t < TILES // 2
+    left = jnp.where(low_half, live[0], live[2])
+    right = jnp.where(low_half, live[1], live[3])
+    return jnp.where(iota(1) < SIDE // 2, left, right) != 0
+
+
+def collide_block(count_ref, list_ref, f_v, mask_v, r_v, solid_v, active_v, y_pre, columns):
+    live = live_blocks(count_ref, list_ref)
     lane, row = iota(1), iota(0)
 
     def tile(t, carry):
         at = pl.ds(pl.multiple_of(t * 8, 8), 8)
-        low_half = t < TILES // 2
-        left = jnp.where(low_half, live[0], live[2])
-        right = jnp.where(low_half, live[1], live[3])
-        is_live = jnp.where(lane < SIDE // 2, left, right) != 0
+        is_live = live_lanes(live, t)
         f = [f_v[k, at, :] for k in range(19)]
         out = relax(f)
         out = [jnp.where(is_live, out[k], f[k]) for k in range(19)]
@@ -128,16 +126,7 @@
         columns[at, :] = packed
         return carry
 
-    for c in range(CHUNKS):
-        copies[c].wait()
-        lax.fori_loop(c * (rows // 8), (c + 1) * (rows // 8), tile, 0)
-
-    up = [r_v[k, SIDE - 1 : SIDE, :] for k in X_UP] + [solid_v[SIDE - 1 : SIDE, :]] * 3
-    down = [r_v[k, 0:1, :] for k in X_DOWN] + [solid_v[0:1, :]] * 3
-    up, down = jnp.concatenate(up, axis=0), jnp.concatenate(down, axis=0)
-    even = lax.rem(position, 2) == 0
-    chip_msg[...] = jnp.where(even, up, down)
-    off_msg[...] = jnp.where(even, down, up)
+    lax.fori_loop(0, TILES, tile, 0)
 
     turned = jnp.transpose(columns[...])
     high, low = turned[0:8, :], turned[8:16, :]
@@ -155,13 +144,69 @@
         y_pre[slab] = jnp.where(jnp.logical_and(is_live, free), 1.0, 0.0)
 
 
+def rim_kernel(
+    count_hbm, list_hbm, f_hbm, m_hbm,
+    chip_msg, off_msg, f_v, mask_v, r_v, solid_v, active_v, y_pre,
+    edge_f, edge_m, count_ref, list_ref, columns, sems,
+):
+    ends = (pl.ds(SIDE - 8, 8), pl.ds(0, 8))
+    pairs = [(count_hbm, count_ref), (list_hbm, list_ref)]
+    for n, end in enumerate(ends):
+        pairs += [(m_hbm.at[end, :], edge_m.at[n]), (f_hbm.at[:, end, :], edge_f.at[n])]
+    first = len(pairs)
+    pairs += [(m_hbm, mask_v)]
+    for c in range(CHUNKS):
+        part = pl.ds(c * (SIDE // CHUNKS), SIDE // CHUNKS)
+        pairs.append((f_hbm.at[:, part, :], f_v.at[:, part, :]))
+    copies = [pltpu.make_async_copy(s, t, sems.at[n]) for n, (s, t) in enumerate(pairs)]
+    for copy in copies:
+        copy.start()
+    for copy in copies[:first]:
+        copy.wait()
+    live = live_blocks(count_ref, list_ref)
+    messages = []
+    for n, (pops, inner) in enumerate(((X_UP, 7), (X_DOWN, 0))):
+        f = [edge_f[n, k] for k in range(19)]
+        out = relax(f)
+        is_live = live_lanes(live, TILES - 1 if n == 0 else 0)
+        solid = edge_m[n].astype(F32)
+        rows = [jnp.where(is_live, out[k], f[k])[inner : inner + 1, :] for k in pops]
+        rows += [solid[inner : inner + 1, :]] * 3
+        messages.append(jnp.concatenate(rows, axis=0))
+    up, down = messages
+    even = lax.rem(lax.axis_index("bx"), 2) == 0
+    chip_msg[...] = jnp.where(even, up, down)
+    off_msg[...] = jnp.where(even, down, up)
+    for copy in copies[first:]:
+        copy.wait()
+
+    @pl.when(is_early())
+    def _():
+        collide_block(
+            count_ref, list_ref, f_v, mask_v, r_v, solid_v, active_v, y_pre, columns
+        )
+
+
+def collide_kernel(
+    count_ref, list_ref, f_v, mask_v, r_in, solid_in, active_in, y_in,
+    r_v, solid_v, active_v, y_pre, columns,
+):
+    del r_in, solid_in, active_in, y_in
+
+    @pl.when(jnp.logical_not(is_early()))
+    def _():
+        collide_block(
+            count_ref, list_ref, f_v, mask_v, r_v, solid_v, active_v, y_pre, columns
+        )
+
+
 def halos(chip_ref, off_ref):
     parity = lax.rem(lax.axis_index("bx"), 2)
-    chip, off = chip_ref[1 - parity], off_ref[...]
+    chip, off = chip_ref[...], off_ref[...]
     return jnp.where(parity == 0, off, chip), jnp.where(parity == 0, chip, off)
 
 
-def corner_kernel(y_pre, chip_ref, off_ref, near_msg, far_msg):
+def corner_kernel(y_pre, chip_ref, off_ref, first_msg, far_msg, second_msg):
     low, high = halos(chip_ref, off_ref)
     lane, row = iota(1), iota(0)
     fore = jnp.logical_or(row == 1, row == 6)
@@ -172,8 +217,9 @@
     down = jnp.where(jnp.logical_and(fore, last), pltpu.roll(high, SIDE - 1, 1), y_pre[1])
     down = jnp.where(jnp.logical_and(back, first), low, down)
     even = lax.rem(lax.axis_index("by"), 2) == 0
-    near_msg[...] = jnp.where(even, up, down)
+    first_msg[...] = jnp.where(even, up, down)
     far_msg[...] = jnp.where(even, down, up)
+    second_msg[...] = jnp.where(even, up, down)
 
 
 def stream_kernel(
@@ -246,10 +292,15 @@
         copy.wait()
 
 
-def patch_kernel(near_ref, far_ref, y_pre, partial, started, out_hbm, stage, sems):
+def patch_kernel(first_ref, far_ref, second_ref, y_pre, partial, started, out_hbm, stage, sems):
     del started
-    even = lax.rem(lax.axis_index("by"), 2) == 0
-    near, far = near_ref[...], far_ref[...]
+    x, y, n_by = lax.axis_index("bx"), lax.axis_index("by"), lax.axis_size("by")
+    even = lax.rem(y, 2) == 0
+    seam = jnp.logical_or(y == 0, y == n_by // 2 - 1)
+    ahead = jnp.logical_or(
+        jnp.logical_and(x < lax.axis_size("bx") // 2, seam), jnp.logical_and(x == 0, y == 1)
+    )
+    near, far = jnp.where(ahead, first_ref[...], second_ref[...]), far_ref[...]
     below, above = jnp.where(even, far, near), jnp.where(even, near, far)
     flags = iota(0) >= 5
     free = [
@@ -291,50 +342,82 @@
     return pltpu.with_memory_space_constraint(x, pltpu.HBM)
 
 
-def pairs_of(count, first):
+def pairs_of(first, last):
     pairs = []
-    for low in range(first, count, 2):
-        high = (low + 1) % count
-        pairs += [(low, high), (high, low)]
-    return sorted(pairs)
+    for low in range(first, last, 2):
+        pairs += [(low, low + 1), (low + 1, low)]
+    return pairs
+
+
+def wrap_pairs(count):
+    return [(count - 1, 0), (0, count - 1)]
+
+
+def near_pairs(n_bx, n_by):
+    ahead, rest = [], []
+    for x in range(n_bx):
+        for source, target in pairs_of(0, n_by):
+            early = x < n_bx // 2 and target in (0, n_by // 2 - 1)
+            pair = (x * n_by + source, x * n_by + target)
+            (ahead if early or (x == 0 and target == 1) else rest).append(pair)
+    return ahead, rest
 
 
 def local(n_bx, n_by, populations, solid_mask, pore_list, pore_count):
     vmem = pl.BlockSpec(memory_space=pltpu.VMEM)
+    smem = pl.BlockSpec(memory_space=pltpu.SMEM)
+    hbm = pl.BlockSpec(memory_space=pltpu.HBM)
     anywhere = pl.BlockSpec(memory_space=pl.ANY)
+    params = pltpu.CompilerParams(vmem_limit_bytes=24 * 2**20)
     plane = (SIDE, SIDE)
     f = populations.reshape(19, *plane)
-    f_v, r_v, solid_v, active_v, chip_msg, off_msg, y_pre = pl.pallas_call(
+    count, listed = pore_count.T, pore_list
+    message = in_vmem(8, SIDE)
+    collided = (in_vmem(19, *plane), in_vmem(*plane), in_vmem(*plane), in_vmem(4, 8, SIDE))
+    chip_msg, off_msg, f_v, mask_v, *begun = pl.pallas_call(
+        rim_kernel,
+        out_shape=(message, message, in_vmem(19, *plane), pltpu.VMEM(plane, jnp.int32)) + collided,
+        in_specs=[hbm] * 4,
+        out_specs=[vmem] * 8,
+        scratch_shapes=[
+            pltpu.VMEM((2, 19, 8, SIDE), F32), pltpu.VMEM((2, 8, SIDE), jnp.int32),
+            pltpu.SMEM((1, n_bx), jnp.int32), pltpu.SMEM((1, 1, 4), jnp.int32),
+            pltpu.VMEM(plane, F32), pltpu.SemaphoreType.DMA((7 + CHUNKS,)),
+        ],
+        compiler_params=params,
+        name="rim",
+    )(stay(count), stay(listed), stay(f), stay(solid_mask.reshape(plane)))
+
+    chip = lax.ppermute(chip_msg, "bx", pairs_of(0, n_bx))
+    off = lax.ppermute(off_msg, "bx", pairs_of(1, n_bx - 1) + wrap_pairs(n_bx))
+
+    r_v, solid_v, active_v, y_pre = pl.pallas_call(
         collide_kernel,
-        out_shape=(
-            in_vmem(19, *plane), in_vmem(19, *plane), in_vmem(*plane), in_vmem(*plane),
-            in_vmem(8, SIDE), in_vmem(8, SIDE), in_vmem(4, 8, SIDE),
+        out_shape=collided,
+        in_specs=[smem] * 2 + [vmem] * 6,
+        out_specs=[vmem] * 4,
+        scratch_shapes=[pltpu.VMEM(plane, F32)],
+        input_output_aliases={4: 0, 5: 1, 6: 2, 7: 3},
+        compiler_params=params,
+        cost_estimate=pl.CostEstimate(
+            flops=8_000_000, bytes_accessed=4_000_000, transcendentals=0
         ),
-        in_specs=[pl.BlockSpec(memory_space=pltpu.HBM)] * 4,
-        out_specs=[vmem] * 7,
-        scratch_shapes=[
-            pltpu.SMEM((1, n_bx), jnp.int32), pltpu.SMEM((1, 1, 4), jnp.int32),
-            pltpu.VMEM(plane, jnp.int32), pltpu.VMEM(plane, F32),
-            pltpu.SemaphoreType.DMA((CHUNKS + 3,)),
-        ],
-        compiler_params=pltpu.CompilerParams(vmem_limit_bytes=24 * 2**20),
         name="collide",
-    )(stay(pore_count.T), stay(pore_list), stay(f), stay(solid_mask.reshape(plane)))
-
-    off = lax.ppermute(off_msg, "bx", pairs_of(n_bx, 1))
-    groups = [[low, low + 1] for low in range(0, n_bx, 2)]
-    chip = lax.all_gather(chip_msg, "bx", axis_index_groups=groups)
-
-    near_msg, far_msg = pl.pallas_call(
+    )(count, listed, keep(f_v), keep(mask_v), *(keep(x) for x in begun))
+
+    first_msg, far_msg, second_msg = pl.pallas_call(
         corner_kernel,
-        out_shape=(in_vmem(8, SIDE), in_vmem(8, SIDE)),
+        out_shape=(message,) * 3,
         in_specs=[vmem] * 3,
-        out_specs=[vmem] * 2,
+        out_specs=[vmem] * 3,
+        compiler_params=params,
         name="corner",
     )(keep(y_pre), keep(chip), keep(off))
 
-    near = lax.ppermute(near_msg, "by", pairs_of(n_by, 0))
-    far = lax.ppermute(far_msg, "by", pairs_of(n_by, 1))
+    ahead, rest = near_pairs(n_bx, n_by)
+    first = lax.ppermute(first_msg, ("bx", "by"), ahead)
+    far = lax.ppermute(far_msg, "by", pairs_of(1, n_by - 1) + wrap_pairs(n_by))
+    second = lax.ppermute(second_msg, ("bx", "by"), rest)
 
     out, partial = pl.pallas_call(
         stream_kernel,
@@ -345,7 +428,7 @@
             pltpu.VMEM((9, *plane), F32), pltpu.VMEM((2, 8, SIDE), F32),
             pltpu.SemaphoreType.DMA((9,)),
         ],
-        compiler_params=pltpu.CompilerParams(vmem_limit_bytes=24 * 2**20),
+        compiler_params=params,
         cost_estimate=pl.CostEstimate(
             flops=8_000_000, bytes_accessed=4_000_000, transcendentals=0
         ),
@@ -355,13 +438,13 @@
     out = pl.pallas_call(
         patch_kernel,
         out_shape=shape(19, *plane),
-        in_specs=[vmem] * 4 + [anywhere],
+        in_specs=[vmem] * 5 + [anywhere],
         out_specs=anywhere,
         scratch_shapes=[pltpu.VMEM((10, *plane), F32), pltpu.SemaphoreType.DMA((10,))],
-        input_output_aliases={4: 0},
-        compiler_params=pltpu.CompilerParams(vmem_limit_bytes=24 * 2**20),
+        input_output_aliases={5: 0},
+        compiler_params=params,
         name="patch",
-    )(keep(near), keep(far), keep(y_pre), keep(partial), out)
+    )(keep(first), keep(far), keep(second), keep(y_pre), keep(partial), out)
     return out.reshape(19, 1, *plane)
 
 

time: 40.2 us -> 36.5 us (0.908)
  the two profiles are of different devices: /device:TPU:1 before, /device:TPU:56 now
where the time goes in v3:
time: 36.5 us; the launch traced here: 36.3 us
  starting transfers between devices  27.4 us (75%)
  Pallas kernels  7.91 us (22%)
  waiting for transfers between devices  0.83 us (2%)
    ppermute x1, starting transfers between devices, local(): off = lax.ppermute(off_msg, 'bx', pairs_of(1, n_bx - 1) + wrap_pairs(n_bx))  12.8 us
    ppermute x1, starting transfers between devices, local(): far = lax.ppermute(far_msg, 'by', pairs_of(1, n_by - 1) + wrap_pairs(n_by))  10.1 us
    pallas_call x1, Pallas kernels, local(): pl.pallas_call(rim_kernel, out_shape=(message, message, in_vmem(19, *plan...  3.69 us
    pallas_call x1, Pallas kernels, local(): pl.pallas_call(stream_kernel, out_shape=(shape(19, *plane), in_vmem(10, *...  2.37 us
    ppermute x1, starting transfers between devices, local(): chip = lax.ppermute(chip_msg, 'bx', pairs_of(0, n_bx))  1.92 us
    ppermute x1, starting transfers between devices, local(): second = lax.ppermute(second_msg, ('bx', 'by'), rest)  1.29 us
    ppermute x1, starting transfers between devices, local(): first = lax.ppermute(first_msg, ('bx', 'by'), ahead)  1.28 us
    pallas_call x1, Pallas kernels, local(): pl.pallas_call(patch_kernel, out_shape=shape(19, *plane), in_specs=[vmem]...  1.21 us
  transfers between devices with their start and end apart: 5, of which 2 were waited for; matrix products, arithmetic and copies ran while one was open for 0% of the time, Pallas kernels for 8%

profile of v3, /device:TPU:56, one launch (start us, length us, event | category | flops | bytes accessed | tf_op | source)
XLA Modules:
  0.0 36.3 jit_solution(6548961714699215237)
XLA Ops:
  0.0 0.0 copy-start.1
  0.0 0.0 copy-start
  0.0 3.7 %rim.1 = (f32[8,128]{1,0:T(8,128)S(1)}, f32[8,128]{1,0:T(8,128)S(1)}, f32[19,128,128]{2,1,0:T(8,128)S(1)}, s32[128,128]{1,0:T(8,128)S(1)}, f32[19,128,128]{2,1,0...) custom-call(s32[1,48]{1,0:T(1,128)} %bitcast.6, s32[1,1,4]{2,1,0:T(1,128)} %list_ref.1, ...), custom_call_target="tpu_custom_call" | custom-call | tf_op jit(solution)/shard_map/rim/pallas_call | solution.py:377
  3.7 1.9 %collective-permute-start = (f32[8,128]{1,0:T(8,128)S(1)}, f32[8,128]{1,0:T(8,128)S(1)}, u32[]{:S(2)}, u32[]{:S(2)}) collective-permute-start(f32[8,128]{1,0:T(8,128)S(1)} %get-tuple-element.29), channel_id=1, source_target_pairs={{0,16},{16,0},{32,48},{48,32},{64,80},{80,64},{96,112},{112,96},{1... | collective-permute-start | bytes 12296 | tf_op jit(solution)/shard_map/ppermute | solution.py:391
  5.6 12.8 %collective-permute-start.1 = (f32[8,128]{1,0:T(8,128)S(1)}, f32[8,128]{1,0:T(8,128)S(1)}, u32[]{:S(2)}, u32[]{:S(2)}) collective-permute-start(f32[8,128]{1,0:T(8,128)S(1)} %get-tuple-element.30), channel_id=1, source_target_pairs={{16,32},{32,16},{48,64},{64,48},{80,96},{96,80},{112,128},{128,112... | collective-permute-start | bytes 12296 | tf_op jit(solution)/shard_map/ppermute | solution.py:392
  18.5 0.0 copy-done.1
  18.5 0.0 copy-done
  18.5 0.6 %collide.1 = (f32[19,128,128]{2,1,0:T(8,128)S(1)}, f32[128,128]{1,0:T(8,128)S(1)}, f32[128,128]{1,0:T(8,128)S(1)}, f32[4,8,128]{2,1,0:T(8,128)S(1)}) custom-call(s32[1,48]{1,0:T(1,128)S(1)} %bitcast.7, s32[1,1,4]{2,1,0:T(1,128)S(1)} %copy-done.1, ...), custom_call_target="tpu_custom_call", output_to_operand_aliasing={{0}: (4, {}), {1}: (5, {}), {2}: (6, {}), {3}: (7, {})} | custom-call | flops 8000000 | bytes 4000000 | tf_op jit(solution)/shard_map/collide/pallas_call | solution.py:394
  19.1 0.0 collective-permute-done.chip_ref
  19.1 0.7 %collective-permute-done.1.off_ref = f32[8,128]{1,0:T(8,128)S(1)} collective-permute-done((f32[8,128]{1,0:T(8,128)S(1)}, f32[8,128]{1,0:T(8,128)S(1)}, u32[]{:S(2)}, u32[]{:S(2)}) %collective-permute-start.1) | collective-permute-done | bytes 4128 | tf_op jit(solution)/shard_map/ppermute | solution.py:392
  19.8 0.1 corner.1
  19.9 1.3 %collective-permute-start.2 = (f32[8,128]{1,0:T(8,128)S(1)}, f32[8,128]{1,0:T(8,128)S(1)}, u32[]{:S(2)}, u32[]{:S(2)}) collective-permute-start(f32[8,128]{1,0:T(8,128)S(1)} %get-tuple-element.31), channel_id=1, source_target_pairs={{0,1},{1,0},{6,7},{17,16},{22,23},{33,32},{38,39},{49,48},{54,55},... | collective-permute-start | bytes 12296 | tf_op jit(solution)/shard_map/ppermute | solution.py:418
  21.2 10.1 %collective-permute-start.3 = (f32[8,128]{1,0:T(8,128)S(1)}, f32[8,128]{1,0:T(8,128)S(1)}, u32[]{:S(2)}, u32[]{:S(2)}) collective-permute-start(f32[8,128]{1,0:T(8,128)S(1)} %get-tuple-element.32), channel_id=1, source_target_pairs={{1,2},{2,1},{3,4},{4,3},{5,6},{6,5},{7,8},{8,7},{9,10},{10,9},{11,... | collective-permute-start | bytes 12296 | tf_op jit(solution)/shard_map/ppermute | solution.py:419
  31.3 1.3 %collective-permute-start.4 = (f32[8,128]{1,0:T(8,128)S(1)}, f32[8,128]{1,0:T(8,128)S(1)}, u32[]{:S(2)}, u32[]{:S(2)}) collective-permute-start(f32[8,128]{1,0:T(8,128)S(1)} %get-tuple-element.33), channel_id=1, source_target_pairs={{2,3},{3,2},{4,5},{5,4},{7,6},{8,9},{9,8},{10,11},{11,10},{12,13},... | collective-permute-start | bytes 12296 | tf_op jit(solution)/shard_map/ppermute | solution.py:420
  32.6 2.4 %stream.1 = (f32[19,128,128]{2,1,0:T(8,128)}, f32[10,128,128]{2,1,0:T(8,128)S(1)}) custom-call(f32[19,128,128]{2,1,0:T(8,128)S(1)} %get-tuple-element.22.f_v, f32[19,128,128]{2,1,0:T(8,128)S(1)} %get-tuple-element.34.r_v, f32[128,128]{1,0:T(8,128)S(1)} %get-tuple-element.35.solid_v, f32[128,128]{1,0:T(8,128)S(1)} %get-tuple-element.36.active_v, ...), custom_call_target="tpu_custom_call" | custom-call | flops 8000000 | bytes 4000000 | tf_op jit(solution)/shard_map/stream/pallas_call | solution.py:422
  35.0 0.0 collective-permute-done.2.first_ref
  35.0 0.1 collective-permute-done.3.far_ref
  35.1 0.0 collective-permute-done.4.second_ref
  35.1 1.2 %patch.1 = f32[19,128,128]{2,1,0:T(8,128)} custom-call(f32[8,128]{1,0:T(8,128)S(1)} %collective-permute-done.2.first_ref, f32[8,128]{1,0:T(8,128)S(1)} %collective-permute-done.3.far_ref, f32[8,128]{1,0:T(8,128)S(1)} %collective-permute-done.4.second_ref, f32[4,8,128]{2,1,0:T(8,128)S(1)} %get-tuple-element.28.y_pre, ...), custom_call_target="tpu_custom_call", output_to_operand_aliasing={{}: (5, {})} | custom-call | tf_op jit(solution)/shard_map/patch/pallas_call | solution.py:438
Async XLA Ops:
  0.0 18.5 %copy-start.1 = (s32[1,1,4]{2,1,0:T(1,128)S(1)}, s32[1,1,4]{2,1,0:T(1,128)}, u32[]{:S(2)}) copy-start(s32[1,1,4]{2,1,0:T(1,128)} %list_ref.1) | copy-start | bytes 52
  0.0 18.5 %copy-start = (s32[48,1]{0,1:T(1,128)S(1)}, s32[48,1]{0,1:T(1,128)}, u32[]{:S(2)}) copy-start(s32[48,1]{0,1:T(1,128)} %param.7) | copy-start | bytes 580
  3.7 15.4 %collective-permute-start = (f32[8,128]{1,0:T(8,128)S(1)}, f32[8,128]{1,0:T(8,128)S(1)}, u32[]{:S(2)}, u32[]{:S(2)}) collective-permute-start(f32[8,128]{1,0:T(8,128)S(1)} %get-tuple-element.29), channel_id=1, source_target_pairs={{0,16},{16,0},{32,48},{48,32},{64,80},{80,64},{96,112},{112,96},{1... | collective-permute-start | bytes 12296 | tf_op jit(solution)/shard_map/ppermute | solution.py:391
  5.6 14.2 %collective-permute-start.1 = (f32[8,128]{1,0:T(8,128)S(1)}, f32[8,128]{1,0:T(8,128)S(1)}, u32[]{:S(2)}, u32[]{:S(2)}) collective-permute-start(f32[8,128]{1,0:T(8,128)S(1)} %get-tuple-element.30), channel_id=1, source_target_pairs={{16,32},{32,16},{48,64},{64,48},{80,96},{96,80},{112,128},{128,112... | collective-permute-start | bytes 12296 | tf_op jit(solution)/shard_map/ppermute | solution.py:392
  19.9 15.1 %collective-permute-start.2 = (f32[8,128]{1,0:T(8,128)S(1)}, f32[8,128]{1,0:T(8,128)S(1)}, u32[]{:S(2)}, u32[]{:S(2)}) collective-permute-start(f32[8,128]{1,0:T(8,128)S(1)} %get-tuple-element.31), channel_id=1, source_target_pairs={{0,1},{1,0},{6,7},{17,16},{22,23},{33,32},{38,39},{49,48},{54,55},... | collective-permute-start | bytes 12296 | tf_op jit(solution)/shard_map/ppermute | solution.py:418
  21.2 13.9 %collective-permute-start.3 = (f32[8,128]{1,0:T(8,128)S(1)}, f32[8,128]{1,0:T(8,128)S(1)}, u32[]{:S(2)}, u32[]{:S(2)}) collective-permute-start(f32[8,128]{1,0:T(8,128)S(1)} %get-tuple-element.32), channel_id=1, source_target_pairs={{1,2},{2,1},{3,4},{4,3},{5,6},{6,5},{7,8},{8,7},{9,10},{10,9},{11,... | collective-permute-start | bytes 12296 | tf_op jit(solution)/shard_map/ppermute | solution.py:419
  31.3 3.8 %collective-permute-start.4 = (f32[8,128]{1,0:T(8,128)S(1)}, f32[8,128]{1,0:T(8,128)S(1)}, u32[]{:S(2)}, u32[]{:S(2)}) collective-permute-start(f32[8,128]{1,0:T(8,128)S(1)} %get-tuple-element.33), channel_id=1, source_target_pairs={{2,3},{3,2},{4,5},{5,4},{7,6},{8,9},{9,8},{10,11},{11,10},{12,13},... | collective-permute-start | bytes 12296 | tf_op jit(solution)/shard_map/ppermute | solution.py:420

commit v4 on v3

--- a/solution.py
+++ b/solution.py
@@ -10,7 +10,7 @@
 F32 = jnp.float32
 SIDE = 128
 TILES = SIDE // 8
-CHUNKS = 4
+CHUNKS = 2
 
 PAIRS = (
     (1, 2, (1, 0, 0)),
@@ -35,6 +35,8 @@
 Y_UP, Y_DOWN = (3, 7, 10, 15, 17), (4, 8, 9, 16, 18)
 Y_ALL = Y_UP + Y_DOWN
 REST = tuple(k for k in range(19) if k not in Y_ALL)
+RUNS = ((0, 3), (5, 2), (11, 4))
+PARTS = 4
 FLAG_ROW = (5, 6, 7, 5, 5)
 
 
@@ -95,20 +97,24 @@
     return live
 
 
-def live_lanes(live, t):
-    low_half = t < TILES // 2
-    left = jnp.where(low_half, live[0], live[2])
-    right = jnp.where(low_half, live[1], live[3])
-    return jnp.where(iota(1) < SIDE // 2, left, right) != 0
-
-
-def collide_block(count_ref, list_ref, f_v, mask_v, r_v, solid_v, active_v, y_pre, columns):
-    live = live_blocks(count_ref, list_ref)
+def collide_block(
+    f_hbm, m_hbm, live_v, f_v, r_v, solid_v, active_v, y_pre, mask_v, columns, sems
+):
     lane, row = iota(1), iota(0)
+    rows = SIDE // CHUNKS
+    copies = [pltpu.make_async_copy(m_hbm, mask_v, sems.at[CHUNKS])]
+    for c in range(CHUNKS):
+        part = pl.ds(c * rows, rows)
+        copies.append(
+            pltpu.make_async_copy(f_hbm.at[:, part, :], f_v.at[:, part, :], sems.at[c])
+        )
+    for copy in copies:
+        copy.start()
+    copies[0].wait()
 
     def tile(t, carry):
         at = pl.ds(pl.multiple_of(t * 8, 8), 8)
-        is_live = live_lanes(live, t)
+        is_live = live_v[t // (TILES // 2)] != 0.0
         f = [f_v[k, at, :] for k in range(19)]
         out = relax(f)
         out = [jnp.where(is_live, out[k], f[k]) for k in range(19)]
@@ -126,7 +132,9 @@
         columns[at, :] = packed
         return carry
 
-    lax.fori_loop(0, TILES, tile, 0)
+    for c in range(CHUNKS):
+        copies[1 + c].wait()
+        lax.fori_loop(c * (rows // 8), (c + 1) * (rows // 8), tile, 0, unroll=rows // 8)
 
     turned = jnp.transpose(columns[...])
     high, low = turned[0:8, :], turned[8:16, :]
@@ -138,37 +146,34 @@
     y_pre[1] = jnp.where(
         fore, pltpu.roll(low, SIDE - 1, 1), jnp.where(back, pltpu.roll(low, 1, 1), low)
     )
-    for slab, flags, first, second in ((2, low, 0, 2), (3, high, 1, 3)):
-        is_live = jnp.where(lane < SIDE // 2, live[first], live[second]) != 0
+    for slab, flags in ((2, low), (3, high)):
         free = jnp.broadcast_to(flags[5:6, :], (8, SIDE)) == 0.0
-        y_pre[slab] = jnp.where(jnp.logical_and(is_live, free), 1.0, 0.0)
+        y_pre[slab] = jnp.where(free, live_v[slab], 0.0)
 
 
 def rim_kernel(
     count_hbm, list_hbm, f_hbm, m_hbm,
-    chip_msg, off_msg, f_v, mask_v, r_v, solid_v, active_v, y_pre,
-    edge_f, edge_m, count_ref, list_ref, columns, sems,
+    chip_msg, off_msg, live_v, f_v, r_v, solid_v, active_v, y_pre,
+    edge_f, edge_m, count_ref, list_ref, mask_v, columns, sems, edge_sems,
 ):
     ends = (pl.ds(SIDE - 8, 8), pl.ds(0, 8))
     pairs = [(count_hbm, count_ref), (list_hbm, list_ref)]
     for n, end in enumerate(ends):
         pairs += [(m_hbm.at[end, :], edge_m.at[n]), (f_hbm.at[:, end, :], edge_f.at[n])]
-    first = len(pairs)
-    pairs += [(m_hbm, mask_v)]
-    for c in range(CHUNKS):
-        part = pl.ds(c * (SIDE // CHUNKS), SIDE // CHUNKS)
-        pairs.append((f_hbm.at[:, part, :], f_v.at[:, part, :]))
-    copies = [pltpu.make_async_copy(s, t, sems.at[n]) for n, (s, t) in enumerate(pairs)]
+    copies = [pltpu.make_async_copy(s, t, edge_sems.at[n]) for n, (s, t) in enumerate(pairs)]
     for copy in copies:
         copy.start()
-    for copy in copies[:first]:
+    for copy in copies:
         copy.wait()
     live = live_blocks(count_ref, list_ref)
+    lane = iota(1)
+    for n, (left, right) in enumerate(((0, 1), (2, 3), (0, 2), (1, 3))):
+        live_v[n] = jnp.where(lane < SIDE // 2, live[left], live[right]).astype(F32)
     messages = []
     for n, (pops, inner) in enumerate(((X_UP, 7), (X_DOWN, 0))):
         f = [edge_f[n, k] for k in range(19)]
         out = relax(f)
-        is_live = live_lanes(live, TILES - 1 if n == 0 else 0)
+        is_live = live_v[1 - n] != 0.0
         solid = edge_m[n].astype(F32)
         rows = [jnp.where(is_live, out[k], f[k])[inner : inner + 1, :] for k in pops]
         rows += [solid[inner : inner + 1, :]] * 3
@@ -177,26 +182,24 @@
     even = lax.rem(lax.axis_index("bx"), 2) == 0
     chip_msg[...] = jnp.where(even, up, down)
     off_msg[...] = jnp.where(even, down, up)
-    for copy in copies[first:]:
-        copy.wait()
 
     @pl.when(is_early())
     def _():
         collide_block(
-            count_ref, list_ref, f_v, mask_v, r_v, solid_v, active_v, y_pre, columns
+            f_hbm, m_hbm, live_v, f_v, r_v, solid_v, active_v, y_pre, mask_v, columns, sems
         )
 
 
 def collide_kernel(
-    count_ref, list_ref, f_v, mask_v, r_in, solid_in, active_in, y_in,
-    r_v, solid_v, active_v, y_pre, columns,
+    f_hbm, m_hbm, live_v, f_in, r_in, solid_in, active_in, y_in,
+    f_v, r_v, solid_v, active_v, y_pre, mask_v, columns, sems,
 ):
-    del r_in, solid_in, active_in, y_in
+    del f_in, r_in, solid_in, active_in, y_in
 
     @pl.when(jnp.logical_not(is_early()))
     def _():
         collide_block(
-            count_ref, list_ref, f_v, mask_v, r_v, solid_v, active_v, y_pre, columns
+            f_hbm, m_hbm, live_v, f_v, r_v, solid_v, active_v, y_pre, mask_v, columns, sems
         )
 
 
@@ -282,12 +285,20 @@
                 stage[REST.index(k), at, :] = result
         return carry
 
-    lax.fori_loop(0, TILES, tile, 0)
-    copies = [
-        pltpu.make_async_copy(stage.at[n], out_hbm.at[k], sems.at[n]) for n, k in enumerate(REST)
-    ]
-    for copy in copies:
-        copy.start()
+    copies = []
+    for part in range(PARTS):
+        tiles = TILES // PARTS
+        lax.fori_loop(part * tiles, (part + 1) * tiles, tile, 0, unroll=tiles)
+        rows = pl.ds(part * tiles * 8, tiles * 8)
+        for n, (start, count) in enumerate(RUNS):
+            first = REST.index(start)
+            copy = pltpu.make_async_copy(
+                stage.at[first : first + count, rows, :],
+                out_hbm.at[start : start + count, rows, :],
+                sems.at[part * len(RUNS) + n],
+            )
+            copy.start()
+            copies.append(copy)
     for copy in copies:
         copy.wait()
 
@@ -365,45 +376,50 @@
 
 def local(n_bx, n_by, populations, solid_mask, pore_list, pore_count):
     vmem = pl.BlockSpec(memory_space=pltpu.VMEM)
-    smem = pl.BlockSpec(memory_space=pltpu.SMEM)
     hbm = pl.BlockSpec(memory_space=pltpu.HBM)
     anywhere = pl.BlockSpec(memory_space=pl.ANY)
     params = pltpu.CompilerParams(vmem_limit_bytes=24 * 2**20)
     plane = (SIDE, SIDE)
-    f = populations.reshape(19, *plane)
-    count, listed = pore_count.T, pore_list
+    f, mask = stay(populations.reshape(19, *plane)), stay(solid_mask.reshape(plane))
     message = in_vmem(8, SIDE)
-    collided = (in_vmem(19, *plane), in_vmem(*plane), in_vmem(*plane), in_vmem(4, 8, SIDE))
-    chip_msg, off_msg, f_v, mask_v, *begun = pl.pallas_call(
+    collided = (
+        in_vmem(19, *plane), in_vmem(19, *plane), in_vmem(*plane), in_vmem(*plane),
+        in_vmem(4, 8, SIDE),
+    )
+    work = [
+        pltpu.VMEM(plane, jnp.int32), pltpu.VMEM(plane, F32),
+        pltpu.SemaphoreType.DMA((CHUNKS + 1,)),
+    ]
+    chip_msg, off_msg, live_v, *begun = pl.pallas_call(
         rim_kernel,
-        out_shape=(message, message, in_vmem(19, *plane), pltpu.VMEM(plane, jnp.int32)) + collided,
+        out_shape=(message, message, in_vmem(4, 8, SIDE)) + collided,
         in_specs=[hbm] * 4,
         out_specs=[vmem] * 8,
         scratch_shapes=[
             pltpu.VMEM((2, 19, 8, SIDE), F32), pltpu.VMEM((2, 8, SIDE), jnp.int32),
             pltpu.SMEM((1, n_bx), jnp.int32), pltpu.SMEM((1, 1, 4), jnp.int32),
-            pltpu.VMEM(plane, F32), pltpu.SemaphoreType.DMA((7 + CHUNKS,)),
+            *work, pltpu.SemaphoreType.DMA((6,)),
         ],
         compiler_params=params,
         name="rim",
-    )(stay(count), stay(listed), stay(f), stay(solid_mask.reshape(plane)))
+    )(stay(pore_count.T), stay(pore_list), f, mask)
 
     chip = lax.ppermute(chip_msg, "bx", pairs_of(0, n_bx))
     off = lax.ppermute(off_msg, "bx", pairs_of(1, n_bx - 1) + wrap_pairs(n_bx))
 
-    r_v, solid_v, active_v, y_pre = pl.pallas_call(
+    f_v, r_v, solid_v, active_v, y_pre = pl.pallas_call(
         collide_kernel,
         out_shape=collided,
-        in_specs=[smem] * 2 + [vmem] * 6,
-        out_specs=[vmem] * 4,
-        scratch_shapes=[pltpu.VMEM(plane, F32)],
-        input_output_aliases={4: 0, 5: 1, 6: 2, 7: 3},
+        in_specs=[hbm] * 2 + [vmem] * 6,
+        out_specs=[vmem] * 5,
+        scratch_shapes=work,
+        input_output_aliases={3: 0, 4: 1, 5: 2, 6: 3, 7: 4},
         compiler_params=params,
         cost_estimate=pl.CostEstimate(
             flops=8_000_000, bytes_accessed=4_000_000, transcendentals=0
         ),
         name="collide",
-    )(count, listed, keep(f_v), keep(mask_v), *(keep(x) for x in begun))
+    )(f, mask, keep(live_v), *(keep(x) for x in begun))
 
     first_msg, far_msg, second_msg = pl.pallas_call(
         corner_kernel,
@@ -426,7 +442,7 @@
         out_specs=[anywhere, vmem],
         scratch_shapes=[
             pltpu.VMEM((9, *plane), F32), pltpu.VMEM((2, 8, SIDE), F32),
-            pltpu.SemaphoreType.DMA((9,)),
+            pltpu.SemaphoreType.DMA((PARTS * len(RUNS),)),
         ],
         compiler_params=params,
         cost_estimate=pl.CostEstimate(

time: 36.5 us -> 36.1 us (0.989)
  waiting for transfers between devices: 0.83 us -> 3.32 us
  Pallas kernels: 7.91 us -> 5.55 us
  starting transfers between devices: 27.4 us -> 26.9 us
    ppermute x1, waiting for transfers between devices: 0.12 us -> 2.07 us  [local(): far = lax.ppermute(far_msg, 'by', pairs_of(1, n_by - 1) + wrap_pairs(n_by))]
    pallas_call x1, Pallas kernels: 2.37 us -> 1.1 us  [local(): pl.pallas_call(stream_kernel, out_shape=(shape(19, *plane), in_vmem(10, *...]
    pallas_call x2, Pallas kernels: 4.26 us -> 3.16 us  [the longest x1 3.11 us: local(): pl.pallas_call(rim_kernel, out_shape=(message, message, in_vmem(4, 8, SID...]
    ppermute x1, starting transfers between devices: 10.1 us -> 9.42 us  [local(): far = lax.ppermute(far_msg, 'by', pairs_of(1, n_by - 1) + wrap_pairs(n_by))]
    ppermute x1, waiting for transfers between devices: 0.7 us -> 1.24 us  [local(): off = lax.ppermute(off_msg, 'bx', pairs_of(1, n_bx - 1) + wrap_pairs(n_bx))]
  transfers between devices with their start and end apart: 5 -> 5, of which waited for: 2 -> 2; matrix products, arithmetic and copies ran while one was open for 0% -> 0% of each run, Pallas kernels for 8% -> 3%
where the time goes in v4:
time: 36.1 us; the launch traced here: 35.9 us
  starting transfers between devices  26.9 us (75%)
  Pallas kernels  5.55 us (15%)
  waiting for transfers between devices  3.32 us (9%)
    ppermute x1, starting transfers between devices, local(): off = lax.ppermute(off_msg, 'bx', pairs_of(1, n_bx - 1) + wrap_pairs(n_bx))  13 us
    ppermute x1, starting transfers between devices, local(): far = lax.ppermute(far_msg, 'by', pairs_of(1, n_by - 1) + wrap_pairs(n_by))  9.42 us
    pallas_call x1, Pallas kernels, local(): pl.pallas_call(rim_kernel, out_shape=(message, message, in_vmem(4, 8, SID...  3.11 us
    ppermute x1, waiting for transfers between devices, local(): far = lax.ppermute(far_msg, 'by', pairs_of(1, n_by - 1) + wrap_pairs(n_by))  2.07 us
    ppermute x1, starting transfers between devices, local(): chip = lax.ppermute(chip_msg, 'bx', pairs_of(0, n_bx))  1.92 us
    ppermute x1, starting transfers between devices, local(): second = lax.ppermute(second_msg, ('bx', 'by'), rest)  1.29 us
    ppermute x1, starting transfers between devices, local(): first = lax.ppermute(first_msg, ('bx', 'by'), ahead)  1.28 us
    ppermute x1, waiting for transfers between devices, local(): off = lax.ppermute(off_msg, 'bx', pairs_of(1, n_bx - 1) + wrap_pairs(n_bx))  1.24 us
  transfers between devices with their start and end apart: 5, of which 2 were waited for; matrix products, arithmetic and copies ran while one was open for 0% of the time, Pallas kernels for 3%

profile of v4, /device:TPU:56, one launch (start us, length us, event | category | flops | bytes accessed | tf_op | source)
XLA Modules:
  0.0 35.9 jit_solution(2859388446746388430)
XLA Ops:
  0.0 3.1 %rim.1 = (f32[8,128]{1,0:T(8,128)S(1)}, f32[8,128]{1,0:T(8,128)S(1)}, f32[4,8,128]{2,1,0:T(8,128)S(1)}, f32[19,128,128]{2,1,0:T(8,128)S(1)}, f32[19,128,128]{2,1...) custom-call(s32[1,48]{1,0:T(1,128)} %bitcast.10, s32[1,1,4]{2,1,0:T(1,128)} %list_hbm.1, ...), custom_call_target="tpu_custom_call" | custom-call | tf_op jit(solution)/shard_map/rim/pallas_call | solution.py:393
  3.1 1.9 %collective-permute-start = (f32[8,128]{1,0:T(8,128)S(1)}, f32[8,128]{1,0:T(8,128)S(1)}, u32[]{:S(2)}, u32[]{:S(2)}) collective-permute-start(f32[8,128]{1,0:T(8,128)S(1)} %get-tuple-element.30), channel_id=1, source_target_pairs={{0,16},{16,0},{32,48},{48,32},{64,80},{80,64},{96,112},{112,96},{1... | collective-permute-start | bytes 12296 | tf_op jit(solution)/shard_map/ppermute | solution.py:407
  5.0 13.0 %collective-permute-start.1 = (f32[8,128]{1,0:T(8,128)S(1)}, f32[8,128]{1,0:T(8,128)S(1)}, u32[]{:S(2)}, u32[]{:S(2)}) collective-permute-start(f32[8,128]{1,0:T(8,128)S(1)} %get-tuple-element.31), channel_id=1, source_target_pairs={{16,32},{32,16},{48,64},{64,48},{80,96},{96,80},{112,128},{128,112... | collective-permute-start | bytes 12296 | tf_op jit(solution)/shard_map/ppermute | solution.py:408
  18.1 0.1 collide.1
  18.1 0.0 collective-permute-done.chip_ref
  18.1 1.2 %collective-permute-done.1.off_ref = f32[8,128]{1,0:T(8,128)S(1)} collective-permute-done((f32[8,128]{1,0:T(8,128)S(1)}, f32[8,128]{1,0:T(8,128)S(1)}, u32[]{:S(2)}, u32[]{:S(2)}) %collective-permute-start.1) | collective-permute-done | bytes 4128 | tf_op jit(solution)/shard_map/ppermute | solution.py:408
  19.4 0.1 corner.1
  19.4 1.3 %collective-permute-start.2 = (f32[8,128]{1,0:T(8,128)S(1)}, f32[8,128]{1,0:T(8,128)S(1)}, u32[]{:S(2)}, u32[]{:S(2)}) collective-permute-start(f32[8,128]{1,0:T(8,128)S(1)} %get-tuple-element.32), channel_id=1, source_target_pairs={{0,1},{1,0},{6,7},{17,16},{22,23},{33,32},{38,39},{49,48},{54,55},... | collective-permute-start | bytes 12296 | tf_op jit(solution)/shard_map/ppermute | solution.py:434
  20.7 9.4 %collective-permute-start.3 = (f32[8,128]{1,0:T(8,128)S(1)}, f32[8,128]{1,0:T(8,128)S(1)}, u32[]{:S(2)}, u32[]{:S(2)}) collective-permute-start(f32[8,128]{1,0:T(8,128)S(1)} %get-tuple-element.33), channel_id=1, source_target_pairs={{1,2},{2,1},{3,4},{4,3},{5,6},{6,5},{7,8},{8,7},{9,10},{10,9},{11,... | collective-permute-start | bytes 12296 | tf_op jit(solution)/shard_map/ppermute | solution.py:435
  30.2 1.3 %collective-permute-start.4 = (f32[8,128]{1,0:T(8,128)S(1)}, f32[8,128]{1,0:T(8,128)S(1)}, u32[]{:S(2)}, u32[]{:S(2)}) collective-permute-start(f32[8,128]{1,0:T(8,128)S(1)} %get-tuple-element.34), channel_id=1, source_target_pairs={{2,3},{3,2},{4,5},{5,4},{7,6},{8,9},{9,8},{10,11},{11,10},{12,13},... | collective-permute-start | bytes 12296 | tf_op jit(solution)/shard_map/ppermute | solution.py:436
  31.5 1.1 %stream.1 = (f32[19,128,128]{2,1,0:T(8,128)}, f32[10,128,128]{2,1,0:T(8,128)S(1)}) custom-call(f32[19,128,128]{2,1,0:T(8,128)S(1)} %get-tuple-element.35.f_v, f32[19,128,128]{2,1,0:T(8,128)S(1)} %get-tuple-element.36.r_v, f32[128,128]{1,0:T(8,128)S(1)} %get-tuple-element.37.solid_v, f32[128,128]{1,0:T(8,128)S(1)} %get-tuple-element.38.active_v, ...), custom_call_target="tpu_custom_call" | custom-call | flops 8000000 | bytes 4000000 | tf_op jit(solution)/shard_map/stream/pallas_call | solution.py:438
  32.6 0.0 collective-permute-done.2.first_ref
  32.6 2.1 %collective-permute-done.3.far_ref = f32[8,128]{1,0:T(8,128)S(1)} collective-permute-done((f32[8,128]{1,0:T(8,128)S(1)}, f32[8,128]{1,0:T(8,128)S(1)}, u32[]{:S(2)}, u32[]{:S(2)}) %collective-permute-start.3) | collective-permute-done | bytes 4128 | tf_op jit(solution)/shard_map/ppermute | solution.py:435
  34.6 0.0 collective-permute-done.4.second_ref
  34.7 1.2 %patch.1 = f32[19,128,128]{2,1,0:T(8,128)} custom-call(f32[8,128]{1,0:T(8,128)S(1)} %collective-permute-done.2.first_ref, f32[8,128]{1,0:T(8,128)S(1)} %collective-permute-done.3.far_ref, f32[8,128]{1,0:T(8,128)S(1)} %collective-permute-done.4.second_ref, f32[4,8,128]{2,1,0:T(8,128)S(1)} %get-tuple-element.29.y_pre, ...), custom_call_target="tpu_custom_call", output_to_operand_aliasing={{}: (5, {})} | custom-call | tf_op jit(solution)/shard_map/patch/pallas_call | solution.py:454
Async XLA Ops:
  3.1 15.0 %collective-permute-start = (f32[8,128]{1,0:T(8,128)S(1)}, f32[8,128]{1,0:T(8,128)S(1)}, u32[]{:S(2)}, u32[]{:S(2)}) collective-permute-start(f32[8,128]{1,0:T(8,128)S(1)} %get-tuple-element.30), channel_id=1, source_target_pairs={{0,16},{16,0},{32,48},{48,32},{64,80},{80,64},{96,112},{112,96},{1... | collective-permute-start | bytes 12296 | tf_op jit(solution)/shard_map/ppermute | solution.py:407
  5.0 14.3 %collective-permute-start.1 = (f32[8,128]{1,0:T(8,128)S(1)}, f32[8,128]{1,0:T(8,128)S(1)}, u32[]{:S(2)}, u32[]{:S(2)}) collective-permute-start(f32[8,128]{1,0:T(8,128)S(1)} %get-tuple-element.31), channel_id=1, source_target_pairs={{16,32},{32,16},{48,64},{64,48},{80,96},{96,80},{112,128},{128,112... | collective-permute-start | bytes 12296 | tf_op jit(solution)/shard_map/ppermute | solution.py:408
  19.4 13.1 %collective-permute-start.2 = (f32[8,128]{1,0:T(8,128)S(1)}, f32[8,128]{1,0:T(8,128)S(1)}, u32[]{:S(2)}, u32[]{:S(2)}) collective-permute-start(f32[8,128]{1,0:T(8,128)S(1)} %get-tuple-element.32), channel_id=1, source_target_pairs={{0,1},{1,0},{6,7},{17,16},{22,23},{33,32},{38,39},{49,48},{54,55},... | collective-permute-start | bytes 12296 | tf_op jit(solution)/shard_map/ppermute | solution.py:434
  20.7 13.9 %collective-permute-start.3 = (f32[8,128]{1,0:T(8,128)S(1)}, f32[8,128]{1,0:T(8,128)S(1)}, u32[]{:S(2)}, u32[]{:S(2)}) collective-permute-start(f32[8,128]{1,0:T(8,128)S(1)} %get-tuple-element.33), channel_id=1, source_target_pairs={{1,2},{2,1},{3,4},{4,3},{5,6},{6,5},{7,8},{8,7},{9,10},{10,9},{11,... | collective-permute-start | bytes 12296 | tf_op jit(solution)/shard_map/ppermute | solution.py:435
  30.2 4.5 %collective-permute-start.4 = (f32[8,128]{1,0:T(8,128)S(1)}, f32[8,128]{1,0:T(8,128)S(1)}, u32[]{:S(2)}, u32[]{:S(2)}) collective-permute-start(f32[8,128]{1,0:T(8,128)S(1)} %get-tuple-element.34), channel_id=1, source_target_pairs={{2,3},{3,2},{4,5},{5,4},{7,6},{8,9},{9,8},{10,11},{11,10},{12,13},... | collective-permute-start | bytes 12296 | tf_op jit(solution)/shard_map/ppermute | solution.py:436

commit v5 on v4

--- a/solution.py
+++ b/solution.py
@@ -2,6 +2,7 @@
 
 import jax
 import jax.numpy as jnp
+import numpy as np
 from jax import lax
 from jax.experimental import pallas as pl
 from jax.experimental.pallas import tpu as pltpu
@@ -11,6 +12,7 @@
 SIDE = 128
 TILES = SIDE // 8
 CHUNKS = 2
+X_SLOTS, Y_SLOTS = 3, 3
 
 PAIRS = (
     (1, 2, (1, 0, 0)),
@@ -152,12 +154,15 @@
 
 
 def rim_kernel(
-    count_hbm, list_hbm, f_hbm, m_hbm,
-    chip_msg, off_msg, live_v, f_v, r_v, solid_v, active_v, y_pre,
-    edge_f, edge_m, count_ref, list_ref, mask_v, columns, sems, edge_sems,
+    count_hbm, list_hbm, plan_hbm, f_hbm, m_hbm, *refs,
 ):
+    x_msgs, refs = refs[:X_SLOTS], refs[X_SLOTS:]
+    (
+        picks, live_v, f_v, r_v, solid_v, active_v, y_pre,
+        edge_f, edge_m, count_ref, list_ref, plan_ref, mask_v, columns, sems, edge_sems,
+    ) = refs
     ends = (pl.ds(SIDE - 8, 8), pl.ds(0, 8))
-    pairs = [(count_hbm, count_ref), (list_hbm, list_ref)]
+    pairs = [(count_hbm, count_ref), (list_hbm, list_ref), (plan_hbm, plan_ref)]
     for n, end in enumerate(ends):
         pairs += [(m_hbm.at[end, :], edge_m.at[n]), (f_hbm.at[:, end, :], edge_f.at[n])]
     copies = [pltpu.make_async_copy(s, t, edge_sems.at[n]) for n, (s, t) in enumerate(pairs)]
@@ -179,9 +184,14 @@
         rows += [solid[inner : inner + 1, :]] * 3
         messages.append(jnp.concatenate(rows, axis=0))
     up, down = messages
-    even = lax.rem(lax.axis_index("bx"), 2) == 0
-    chip_msg[...] = jnp.where(even, up, down)
-    off_msg[...] = jnp.where(even, down, up)
+    code = plan_ref[0, lax.axis_index("bx") * lax.axis_size("by") + lax.axis_index("by")]
+    for n in range(4):
+        picks[n] = jnp.broadcast_to(lax.rem(code >> (2 * n), 4), (8, SIDE)).astype(F32)
+    for n in range(X_SLOTS):
+        x_msgs[n][...] = jnp.where(lax.rem(code >> (8 + n), 2) == 1, up, down)
+    for n in range(Y_SLOTS):
+        bit = lax.rem(code >> (8 + X_SLOTS + n), 2)
+        picks[4 + n] = jnp.broadcast_to(bit, (8, SIDE)).astype(F32)
 
     @pl.when(is_early())
     def _():
@@ -203,14 +213,16 @@
         )
 
 
-def halos(chip_ref, off_ref):
-    parity = lax.rem(lax.axis_index("bx"), 2)
-    chip, off = chip_ref[...], off_ref[...]
-    return jnp.where(parity == 0, off, chip), jnp.where(parity == 0, chip, off)
-
-
-def corner_kernel(y_pre, chip_ref, off_ref, first_msg, far_msg, second_msg):
-    low, high = halos(chip_ref, off_ref)
+def chosen(pick, refs):
+    taken = refs[0][...]
+    for n, ref in enumerate(refs[1:], 1):
+        taken = jnp.where(pick == float(n), ref[...], taken)
+    return taken
+
+
+def corner_kernel(y_pre, picks, *refs):
+    halos, y_msgs = refs[:X_SLOTS], refs[X_SLOTS:]
+    low, high = chosen(picks[0], halos), chosen(picks[1], halos)
     lane, row = iota(1), iota(0)
     fore = jnp.logical_or(row == 1, row == 6)
     back = jnp.logical_or(row == 2, row == 7)
@@ -219,17 +231,15 @@
     up = jnp.where(jnp.logical_and(back, last), high, up)
     down = jnp.where(jnp.logical_and(fore, last), pltpu.roll(high, SIDE - 1, 1), y_pre[1])
     down = jnp.where(jnp.logical_and(back, first), low, down)
-    even = lax.rem(lax.axis_index("by"), 2) == 0
-    first_msg[...] = jnp.where(even, up, down)
-    far_msg[...] = jnp.where(even, down, up)
-    second_msg[...] = jnp.where(even, up, down)
+    for n, message in enumerate(y_msgs):
+        message[...] = jnp.where(picks[4 + n] == 1.0, up, down)
 
 
 def stream_kernel(
-    f_v, r_v, solid_v, active_v, chip_ref, off_ref, out_hbm, partial, stage, edges, sems
+    f_v, r_v, solid_v, active_v, picks, *refs,
 ):
-    low, high = halos(chip_ref, off_ref)
-    edges[0], edges[1] = low, high
+    halos, (out_hbm, partial, stage, edges, sems) = refs[:X_SLOTS], refs[X_SLOTS:]
+    edges[0], edges[1] = chosen(picks[0], halos), chosen(picks[1], halos)
     lane, row = iota(1), iota(0)
     top, bottom = row == 0, row == 7
     first, last = lane == 0, lane == SIDE - 1
@@ -303,16 +313,10 @@
         copy.wait()
 
 
-def patch_kernel(first_ref, far_ref, second_ref, y_pre, partial, started, out_hbm, stage, sems):
+def patch_kernel(y_pre, picks, partial, started, *refs):
     del started
-    x, y, n_by = lax.axis_index("bx"), lax.axis_index("by"), lax.axis_size("by")
-    even = lax.rem(y, 2) == 0
-    seam = jnp.logical_or(y == 0, y == n_by // 2 - 1)
-    ahead = jnp.logical_or(
-        jnp.logical_and(x < lax.axis_size("bx") // 2, seam), jnp.logical_and(x == 0, y == 1)
-    )
-    near, far = jnp.where(ahead, first_ref[...], second_ref[...]), far_ref[...]
-    below, above = jnp.where(even, far, near), jnp.where(even, near, far)
+    halos, (out_hbm, stage, sems) = refs[:Y_SLOTS], refs[Y_SLOTS:]
+    below, above = chosen(picks[2], halos), chosen(picks[3], halos)
     flags = iota(0) >= 5
     free = [
         jnp.where(flags, jnp.where(message == 0.0, y_pre[slab], 0.0), message)
@@ -353,25 +357,40 @@
     return pltpu.with_memory_space_constraint(x, pltpu.HBM)
 
 
-def pairs_of(first, last):
-    pairs = []
-    for low in range(first, last, 2):
-        pairs += [(low, low + 1), (low + 1, low)]
-    return pairs
-
-
-def wrap_pairs(count):
-    return [(count - 1, 0), (0, count - 1)]
-
-
-def near_pairs(n_bx, n_by):
-    ahead, rest = [], []
+def slots(n_bx, n_by):
+    chosen_slots = {}
     for x in range(n_bx):
-        for source, target in pairs_of(0, n_by):
-            early = x < n_bx // 2 and target in (0, n_by // 2 - 1)
-            pair = (x * n_by + source, x * n_by + target)
-            (ahead if early or (x == 0 and target == 1) else rest).append(pair)
-    return ahead, rest
+        for y in range(n_by):
+            if x % 2 == 0:
+                slot = 1 if y == 0 else 2 if x == n_bx - 2 else 0
+            else:
+                slot = 1 if y else 2 if x == n_bx - 1 else 0
+            chosen_slots["x", x, y, 1] = chosen_slots["x", (x + 1) % n_bx, y, -1] = slot
+            up, down = (x, y, 1), (x, (y + 1) % n_by, -1)
+            for source, target in ((up, y + 1), (down, y)):
+                ahead = x < n_bx // 2 and target in (0, n_by // 2 - 1)
+                chosen_slots["y", *source] = 1 if y % 2 else 0 if ahead else 2
+            if x == 0 and (y < 4 or y >= n_by - 3):
+                special = {0: 1, 1: 0, 2: 2, 3: 0, n_by - 3: 1, n_by - 2: 0, n_by - 1: 2}
+                chosen_slots["y", *up] = chosen_slots["y", *down] = special[y]
+    return chosen_slots
+
+
+def plan(n_bx, n_by):
+    chosen_slots = slots(n_bx, n_by)
+    pairs = {"x": [[] for _ in range(X_SLOTS)], "y": [[] for _ in range(Y_SLOTS)]}
+    codes = np.zeros((n_bx, n_by), np.int32)
+    for (axis, x, y, step), slot in chosen_slots.items():
+        to = ((x + step) % n_bx, y) if axis == "x" else (x, (y + step) % n_by)
+        pairs[axis][slot].append((x * n_by + y, to[0] * n_by + to[1]))
+        side = (0 if axis == "x" else 2) + (0 if step > 0 else 1)
+        codes[to] += slot << (2 * side)
+        if step > 0:
+            codes[x, y] += 1 << (8 + slot + (0 if axis == "x" else X_SLOTS))
+    for group in pairs["x"] + pairs["y"]:
+        for end in zip(*group):
+            assert len(set(end)) == len(end)
+    return pairs, codes.reshape(1, -1)
 
 
 def local(n_bx, n_by, populations, solid_mask, pore_list, pore_count):
@@ -390,22 +409,24 @@
         pltpu.VMEM(plane, jnp.int32), pltpu.VMEM(plane, F32),
         pltpu.SemaphoreType.DMA((CHUNKS + 1,)),
     ]
-    chip_msg, off_msg, live_v, *begun = pl.pallas_call(
+    pairs, codes = plan(n_bx, n_by)
+    *x_msgs, picks, live_v, f_v, r_v, solid_v, active_v, y_pre = pl.pallas_call(
         rim_kernel,
-        out_shape=(message, message, in_vmem(4, 8, SIDE)) + collided,
-        in_specs=[hbm] * 4,
-        out_specs=[vmem] * 8,
+        out_shape=(message,) * X_SLOTS + (in_vmem(4 + Y_SLOTS, 8, SIDE), in_vmem(4, 8, SIDE)) + collided,
+        in_specs=[hbm] * 5,
+        out_specs=[vmem] * (X_SLOTS + 7),
         scratch_shapes=[
             pltpu.VMEM((2, 19, 8, SIDE), F32), pltpu.VMEM((2, 8, SIDE), jnp.int32),
             pltpu.SMEM((1, n_bx), jnp.int32), pltpu.SMEM((1, 1, 4), jnp.int32),
-            *work, pltpu.SemaphoreType.DMA((6,)),
+            pltpu.SMEM(codes.shape, jnp.int32), *work, pltpu.SemaphoreType.DMA((7,)),
         ],
         compiler_params=params,
         name="rim",
-    )(stay(pore_count.T), stay(pore_list), f, mask)
-
-    chip = lax.ppermute(chip_msg, "bx", pairs_of(0, n_bx))
-    off = lax.ppermute(off_msg, "bx", pairs_of(1, n_bx - 1) + wrap_pairs(n_bx))
+    )(stay(pore_count.T), stay(pore_list), stay(jnp.asarray(codes)), f, mask)
+
+    x_halos = [
+        keep(lax.ppermute(message, ("bx", "by"), group)) for message, group in zip(x_msgs, pairs["x"])
+    ]
 
     f_v, r_v, solid_v, active_v, y_pre = pl.pallas_call(
         collide_kernel,
@@ -419,26 +440,25 @@
             flops=8_000_000, bytes_accessed=4_000_000, transcendentals=0
         ),
         name="collide",
-    )(f, mask, keep(live_v), *(keep(x) for x in begun))
-
-    first_msg, far_msg, second_msg = pl.pallas_call(
+    )(f, mask, keep(live_v), *(keep(x) for x in (f_v, r_v, solid_v, active_v, y_pre)))
+
+    y_msgs = pl.pallas_call(
         corner_kernel,
-        out_shape=(message,) * 3,
-        in_specs=[vmem] * 3,
-        out_specs=[vmem] * 3,
+        out_shape=(message,) * Y_SLOTS,
+        in_specs=[vmem] * (2 + X_SLOTS),
+        out_specs=[vmem] * Y_SLOTS,
         compiler_params=params,
         name="corner",
-    )(keep(y_pre), keep(chip), keep(off))
-
-    ahead, rest = near_pairs(n_bx, n_by)
-    first = lax.ppermute(first_msg, ("bx", "by"), ahead)
-    far = lax.ppermute(far_msg, "by", pairs_of(1, n_by - 1) + wrap_pairs(n_by))
-    second = lax.ppermute(second_msg, ("bx", "by"), rest)
+    )(keep(y_pre), keep(picks), *x_halos)
+
+    y_halos = [
+        keep(lax.ppermute(message, ("bx", "by"), group)) for message, group in zip(y_msgs, pairs["y"])
+    ]
 
     out, partial = pl.pallas_call(
         stream_kernel,
         out_shape=(shape(19, *plane), in_vmem(10, *plane)),
-        in_specs=[vmem] * 6,
+        in_specs=[vmem] * (5 + X_SLOTS),
         out_specs=[anywhere, vmem],
         scratch_shapes=[
             pltpu.VMEM((9, *plane), F32), pltpu.VMEM((2, 8, SIDE), F32),
@@ -449,18 +469,18 @@
             flops=8_000_000, bytes_accessed=4_000_000, transcendentals=0
         ),
         name="stream",
-    )(keep(f_v), keep(r_v), keep(solid_v), keep(active_v), keep(chip), keep(off))
+    )(keep(f_v), keep(r_v), keep(solid_v), keep(active_v), keep(picks), *x_halos)
 
     out = pl.pallas_call(
         patch_kernel,
         out_shape=shape(19, *plane),
-        in_specs=[vmem] * 5 + [anywhere],
+        in_specs=[vmem] * 3 + [anywhere] + [vmem] * Y_SLOTS,
         out_specs=anywhere,
         scratch_shapes=[pltpu.VMEM((10, *plane), F32), pltpu.SemaphoreType.DMA((10,))],
-        input_output_aliases={5: 0},
+        input_output_aliases={3: 0},
         compiler_params=params,
         name="patch",
-    )(keep(first), keep(far), keep(second), keep(y_pre), keep(partial), out)
+    )(keep(y_pre), keep(picks), keep(partial), out, *y_halos)
     return out.reshape(19, 1, *plane)
 
 

time: 36.1 us -> 35 us (0.970)
  the two profiles are of different devices: /device:TPU:56 before, /device:TPU:48 now
where the time goes in v5:
time: 35 us; the launch traced here: 34.7 us
  starting transfers between devices  19.4 us (55%)
  waiting for transfers between devices  9.53 us (27%)
  Pallas kernels  5.65 us (16%)
    ppermute x6, starting transfers between devices, local(): lax.ppermute(message, ('bx', 'by'), group)  19.4 us
    ppermute x6, waiting for transfers between devices, local(): lax.ppermute(message, ('bx', 'by'), group)  9.53 us
    pallas_call x1, Pallas kernels, local(): pl.pallas_call(rim_kernel, out_shape=(message,) * X_SLOTS + (in_vmem(4 +...  3.13 us
    pallas_call x1, Pallas kernels, local(): pl.pallas_call(patch_kernel, out_shape=shape(19, *plane), in_specs=[vmem]...  1.2 us
    pallas_call x1, Pallas kernels, local(): pl.pallas_call(stream_kernel, out_shape=(shape(19, *plane), in_vmem(10, *...  1.19 us
  transfers between devices with their start and end apart: 6, of which 3 were waited for; matrix products, arithmetic and copies ran while one was open for 0% of the time, Pallas kernels for 4%

profile of v5, /device:TPU:48, one launch (start us, length us, event | category | flops | bytes accessed | tf_op | source)
XLA Modules:
  0.0 34.7 jit_solution(8825561114738222835)
XLA Ops:
  0.0 3.1 %rim.1 = (f32[8,128]{1,0:T(8,128)S(1)}, f32[8,128]{1,0:T(8,128)S(1)}, f32[8,128]{1,0:T(8,128)S(1)}, f32[7,8,128]{2,1,0:T(8,128)S(1)}, f32[4,8,128]{2,1,0:T(8,128...) custom-call(s32[1,48]{1,0:T(1,128)} %bitcast.10, ...), custom_call_target="tpu_custom_call" | custom-call | tf_op jit(solution)/shard_map/rim/pallas_call | solution.py:413
  3.1 1.9 %collective-permute-start = (f32[8,128]{1,0:T(8,128)S(1)}, f32[8,128]{1,0:T(8,128)S(1)}, u32[]{:S(2)}, u32[]{:S(2)}) collective-permute-start(f32[8,128]{1,0:T(8,128)S(1)} %get-tuple-element.37), channel_id=1, source_target_pairs={{1,17},{17,1},{2,18},{18,2},{3,19},{19,3},{4,20},{20,4},{5,21},{21... | collective-permute-start | bytes 12296 | tf_op jit(solution)/shard_map/ppermute | solution.py:428
  5.1 11.1 %collective-permute-start.1 = (f32[8,128]{1,0:T(8,128)S(1)}, f32[8,128]{1,0:T(8,128)S(1)}, u32[]{:S(2)}, u32[]{:S(2)}) collective-permute-start(f32[8,128]{1,0:T(8,128)S(1)} %get-tuple-element.38), channel_id=1, source_target_pairs={{0,16},{16,0},{17,33},{33,17},{18,34},{34,18},{19,35},{35,19},{20,... | collective-permute-start | bytes 12296 | tf_op jit(solution)/shard_map/ppermute | solution.py:428
  16.1 0.7 %collective-permute-start.2 = (f32[8,128]{1,0:T(8,128)S(1)}, f32[8,128]{1,0:T(8,128)S(1)}, u32[]{:S(2)}, u32[]{:S(2)}) collective-permute-start(f32[8,128]{1,0:T(8,128)S(1)} %get-tuple-element.39), channel_id=1, source_target_pairs={{737,753},{753,737},{738,754},{754,738},{739,755},{755,739},{740,7... | collective-permute-start | bytes 12296 | tf_op jit(solution)/shard_map/ppermute | solution.py:428
  16.8 0.1 collide.1
  16.9 0.0 collective-permute-done.refs_0_
  16.9 0.6 %collective-permute-done.1.refs_1_ = f32[8,128]{1,0:T(8,128)S(1)} collective-permute-done((f32[8,128]{1,0:T(8,128)S(1)}, f32[8,128]{1,0:T(8,128)S(1)}, u32[]{:S(2)}, u32[]{:S(2)}) %collective-permute-start.1) | collective-permute-done | bytes 4128 | tf_op jit(solution)/shard_map/ppermute | solution.py:428
  17.5 0.0 collective-permute-done.2.refs_2_
  17.5 0.1 corner.1
  17.5 2.6 %collective-permute-start.3 = (f32[8,128]{1,0:T(8,128)S(1)}, f32[8,128]{1,0:T(8,128)S(1)}, u32[]{:S(2)}, u32[]{:S(2)}) collective-permute-start(f32[8,128]{1,0:T(8,128)S(1)} %get-tuple-element.42), channel_id=1, source_target_pairs={{1,2},{2,1},{3,4},{4,3},{6,7},{14,15},{15,14},{17,16},{22,23},{33,... | collective-permute-start | bytes 12296 | tf_op jit(solution)/shard_map/ppermute | solution.py:455
  20.1 1.9 %collective-permute-start.4 = (f32[8,128]{1,0:T(8,128)S(1)}, f32[8,128]{1,0:T(8,128)S(1)}, u32[]{:S(2)}, u32[]{:S(2)}) collective-permute-start(f32[8,128]{1,0:T(8,128)S(1)} %get-tuple-element.43), channel_id=1, source_target_pairs={{0,1},{1,0},{5,6},{6,5},{7,8},{8,7},{9,10},{10,9},{11,12},{12,11},... | collective-permute-start | bytes 12296 | tf_op jit(solution)/shard_map/ppermute | solution.py:455
  22.0 1.3 %collective-permute-start.5 = (f32[8,128]{1,0:T(8,128)S(1)}, f32[8,128]{1,0:T(8,128)S(1)}, u32[]{:S(2)}, u32[]{:S(2)}) collective-permute-start(f32[8,128]{1,0:T(8,128)S(1)} %get-tuple-element.44), channel_id=1, source_target_pairs={{2,3},{3,2},{4,5},{5,4},{7,6},{8,9},{9,8},{10,11},{11,10},{12,13},... | collective-permute-start | bytes 12296 | tf_op jit(solution)/shard_map/ppermute | solution.py:455
  23.3 1.2 %stream.1 = (f32[19,128,128]{2,1,0:T(8,128)}, f32[10,128,128]{2,1,0:T(8,128)S(1)}) custom-call(f32[19,128,128]{2,1,0:T(8,128)S(1)} %get-tuple-element.33.f_v, f32[19,128,128]{2,1,0:T(8,128)S(1)} %get-tuple-element.34.r_v, f32[128,128]{1,0:T(8,128)S(1)} %get-tuple-element.35.solid_v, f32[128,128]{1,0:T(8,128)S(1)} %get-tuple-element.36.active_v, ...), custom_call_target="tpu_custom_call" | custom-call | flops 8000000 | bytes 4000000 | tf_op jit(solution)/shard_map/stream/pallas_call | solution.py:458
  24.5 0.0 collective-permute-done.3.refs_0_
  24.6 1.1 %collective-permute-done.4.refs_1_ = f32[8,128]{1,0:T(8,128)S(1)} collective-permute-done((f32[8,128]{1,0:T(8,128)S(1)}, f32[8,128]{1,0:T(8,128)S(1)}, u32[]{:S(2)}, u32[]{:S(2)}) %collective-permute-start.4) | collective-permute-done | bytes 4128 | tf_op jit(solution)/shard_map/ppermute | solution.py:455
  25.6 7.9 %collective-permute-done.5.refs_2_ = f32[8,128]{1,0:T(8,128)S(1)} collective-permute-done((f32[8,128]{1,0:T(8,128)S(1)}, f32[8,128]{1,0:T(8,128)S(1)}, u32[]{:S(2)}, u32[]{:S(2)}) %collective-permute-start.5) | collective-permute-done | bytes 4128 | tf_op jit(solution)/shard_map/ppermute | solution.py:455
  33.5 1.2 %patch.1 = f32[19,128,128]{2,1,0:T(8,128)} custom-call(f32[4,8,128]{2,1,0:T(8,128)S(1)} %get-tuple-element.31.y_pre, f32[7,8,128]{2,1,0:T(8,128)S(1)} %get-tuple-element.32.picks, f32[10,128,128]{2,1,0:T(8,128)S(1)} %get-tuple-element.40.partial, f32[19,128,128]{2,1,0:T(8,128)} %get-tuple-element.41.started, ...), custom_call_target="tpu_custom_call", output_to_operand_aliasing={{}: (3, {})} | custom-call | tf_op jit(solution)/shard_map/patch/pallas_call | solution.py:474
Async XLA Ops:
  3.1 13.7 %collective-permute-start = (f32[8,128]{1,0:T(8,128)S(1)}, f32[8,128]{1,0:T(8,128)S(1)}, u32[]{:S(2)}, u32[]{:S(2)}) collective-permute-start(f32[8,128]{1,0:T(8,128)S(1)} %get-tuple-element.37), channel_id=1, source_target_pairs={{1,17},{17,1},{2,18},{18,2},{3,19},{19,3},{4,20},{20,4},{5,21},{21... | collective-permute-start | bytes 12296 | tf_op jit(solution)/shard_map/ppermute | solution.py:428
  5.1 12.4 %collective-permute-start.1 = (f32[8,128]{1,0:T(8,128)S(1)}, f32[8,128]{1,0:T(8,128)S(1)}, u32[]{:S(2)}, u32[]{:S(2)}) collective-permute-start(f32[8,128]{1,0:T(8,128)S(1)} %get-tuple-element.38), channel_id=1, source_target_pairs={{0,16},{16,0},{17,33},{33,17},{18,34},{34,18},{19,35},{35,19},{20,... | collective-permute-start | bytes 12296 | tf_op jit(solution)/shard_map/ppermute | solution.py:428
  16.1 1.3 %collective-permute-start.2 = (f32[8,128]{1,0:T(8,128)S(1)}, f32[8,128]{1,0:T(8,128)S(1)}, u32[]{:S(2)}, u32[]{:S(2)}) collective-permute-start(f32[8,128]{1,0:T(8,128)S(1)} %get-tuple-element.39), channel_id=1, source_target_pairs={{737,753},{753,737},{738,754},{754,738},{739,755},{755,739},{740,7... | collective-permute-start | bytes 12296 | tf_op jit(solution)/shard_map/ppermute | solution.py:428
  17.5 7.0 %collective-permute-start.3 = (f32[8,128]{1,0:T(8,128)S(1)}, f32[8,128]{1,0:T(8,128)S(1)}, u32[]{:S(2)}, u32[]{:S(2)}) collective-permute-start(f32[8,128]{1,0:T(8,128)S(1)} %get-tuple-element.42), channel_id=1, source_target_pairs={{1,2},{2,1},{3,4},{4,3},{6,7},{14,15},{15,14},{17,16},{22,23},{33,... | collective-permute-start | bytes 12296 | tf_op jit(solution)/shard_map/ppermute | solution.py:455
  20.1 5.5 %collective-permute-start.4 = (f32[8,128]{1,0:T(8,128)S(1)}, f32[8,128]{1,0:T(8,128)S(1)}, u32[]{:S(2)}, u32[]{:S(2)}) collective-permute-start(f32[8,128]{1,0:T(8,128)S(1)} %get-tuple-element.43), channel_id=1, source_target_pairs={{0,1},{1,0},{5,6},{6,5},{7,8},{8,7},{9,10},{10,9},{11,12},{12,11},... | collective-permute-start | bytes 12296 | tf_op jit(solution)/shard_map/ppermute | solution.py:455
  22.0 11.5 %collective-permute-start.5 = (f32[8,128]{1,0:T(8,128)S(1)}, f32[8,128]{1,0:T(8,128)S(1)}, u32[]{:S(2)}, u32[]{:S(2)}) collective-permute-start(f32[8,128]{1,0:T(8,128)S(1)} %get-tuple-element.44), channel_id=1, source_target_pairs={{2,3},{3,2},{4,5},{5,4},{7,6},{8,9},{9,8},{10,11},{11,10},{12,13},... | collective-permute-start | bytes 12296 | tf_op jit(solution)/shard_map/ppermute | solution.py:455

commit v6 on v5

--- a/solution.py
+++ b/solution.py
@@ -99,20 +99,9 @@
     return live
 
 
-def collide_block(
-    f_hbm, m_hbm, live_v, f_v, r_v, solid_v, active_v, y_pre, mask_v, columns, sems
-):
+def collide_block(live_v, f_v, mask_v, r_v, solid_v, active_v, y_pre, columns):
     lane, row = iota(1), iota(0)
     rows = SIDE // CHUNKS
-    copies = [pltpu.make_async_copy(m_hbm, mask_v, sems.at[CHUNKS])]
-    for c in range(CHUNKS):
-        part = pl.ds(c * rows, rows)
-        copies.append(
-            pltpu.make_async_copy(f_hbm.at[:, part, :], f_v.at[:, part, :], sems.at[c])
-        )
-    for copy in copies:
-        copy.start()
-    copies[0].wait()
 
     def tile(t, carry):
         at = pl.ds(pl.multiple_of(t * 8, 8), 8)
@@ -135,7 +124,6 @@
         return carry
 
     for c in range(CHUNKS):
-        copies[1 + c].wait()
         lax.fori_loop(c * (rows // 8), (c + 1) * (rows // 8), tile, 0, unroll=rows // 8)
 
     turned = jnp.transpose(columns[...])
@@ -158,14 +146,14 @@
 ):
     x_msgs, refs = refs[:X_SLOTS], refs[X_SLOTS:]
     (
-        picks, live_v, f_v, r_v, solid_v, active_v, y_pre,
-        edge_f, edge_m, count_ref, list_ref, plan_ref, mask_v, columns, sems, edge_sems,
+        picks, live_v, r_v, solid_v, active_v, y_pre,
+        edge_f, edge_m, count_ref, list_ref, plan_ref, f_v, mask_v, columns, sems,
     ) = refs
     ends = (pl.ds(SIDE - 8, 8), pl.ds(0, 8))
     pairs = [(count_hbm, count_ref), (list_hbm, list_ref), (plan_hbm, plan_ref)]
     for n, end in enumerate(ends):
         pairs += [(m_hbm.at[end, :], edge_m.at[n]), (f_hbm.at[:, end, :], edge_f.at[n])]
-    copies = [pltpu.make_async_copy(s, t, edge_sems.at[n]) for n, (s, t) in enumerate(pairs)]
+    copies = [pltpu.make_async_copy(s, t, sems.at[n]) for n, (s, t) in enumerate(pairs)]
     for copy in copies:
         copy.start()
     for copy in copies:
@@ -195,22 +183,26 @@
 
     @pl.when(is_early())
     def _():
-        collide_block(
-            f_hbm, m_hbm, live_v, f_v, r_v, solid_v, active_v, y_pre, mask_v, columns, sems
-        )
+        whole = [
+            pltpu.make_async_copy(m_hbm, mask_v, sems.at[0]),
+            pltpu.make_async_copy(f_hbm, f_v, sems.at[1]),
+        ]
+        for copy in whole:
+            copy.start()
+        for copy in whole:
+            copy.wait()
+        collide_block(live_v, f_v, mask_v, r_v, solid_v, active_v, y_pre, columns)
 
 
 def collide_kernel(
-    f_hbm, m_hbm, live_v, f_in, r_in, solid_in, active_in, y_in,
-    f_v, r_v, solid_v, active_v, y_pre, mask_v, columns, sems,
+    f_v, mask_v, live_v, r_in, solid_in, active_in, y_in,
+    r_v, solid_v, active_v, y_pre, columns,
 ):
-    del f_in, r_in, solid_in, active_in, y_in
+    del r_in, solid_in, active_in, y_in
 
     @pl.when(jnp.logical_not(is_early()))
     def _():
-        collide_block(
-            f_hbm, m_hbm, live_v, f_v, r_v, solid_v, active_v, y_pre, mask_v, columns, sems
-        )
+        collide_block(live_v, f_v, mask_v, r_v, solid_v, active_v, y_pre, columns)
 
 
 def chosen(pick, refs):
@@ -317,24 +309,22 @@
     del started
     halos, (out_hbm, stage, sems) = refs[:Y_SLOTS], refs[Y_SLOTS:]
     below, above = chosen(picks[2], halos), chosen(picks[3], halos)
-    flags = iota(0) >= 5
-    free = [
-        jnp.where(flags, jnp.where(message == 0.0, y_pre[slab], 0.0), message)
-        for message, slab in ((below, 2), (above, 3))
-    ]
-    turned = jnp.transpose(
-        jnp.concatenate(free + [jnp.zeros((SIDE - 16, SIDE), F32)], axis=0)
-    )
-    lane = lax.broadcasted_iota(jnp.int32, (SIDE, SIDE), 1)
+    rows = []
+    for message, slab in ((below, 2), (above, 3)):
+        for n, flag in enumerate(FLAG_ROW):
+            free = jnp.logical_and(message[flag : flag + 1, :] == 0.0, y_pre[slab, 0:1, :] != 0.0)
+            rows.append(jnp.where(free, message[n : n + 1, :], jnp.nan))
+    rows.append(jnp.zeros((6, SIDE), F32))
+    turned = jnp.transpose(jnp.concatenate(rows, axis=0))
+    lane = iota(1)
     copies = []
     for n, k in enumerate(Y_ALL):
-        side, which = n // 5, n % 5
-        value = turned[:, side * 8 + which : side * 8 + which + 1]
-        flag = side * 8 + FLAG_ROW[which]
-        take = jnp.logical_and(
-            lane == (0 if side == 0 else SIDE - 1), turned[:, flag : flag + 1] != 0.0
-        )
-        stage[n] = jnp.where(take, value, partial[n])
+        edge = lane == (0 if n < 5 else SIDE - 1)
+        for t in range(TILES):
+            at = pl.ds(8 * t, 8)
+            value = jnp.broadcast_to(turned[8 * t : 8 * t + 8, n : n + 1], (8, SIDE))
+            value = jnp.where(edge, value, jnp.nan)
+            stage[n, at, :] = jnp.where(value == value, value, partial[n, at, :])
         copies.append(pltpu.make_async_copy(stage.at[n], out_hbm.at[k], sems.at[n]))
         copies[-1].start()
     for copy in copies:
@@ -362,13 +352,14 @@
     for x in range(n_bx):
         for y in range(n_by):
             if x % 2 == 0:
-                slot = 1 if y == 0 else 2 if x == n_bx - 2 else 0
+                slot = 1 if y == 0 else 2 if x == n_bx - 2 or (x == 0 and y == n_by // 2) else 0
             else:
                 slot = 1 if y else 2 if x == n_bx - 1 else 0
             chosen_slots["x", x, y, 1] = chosen_slots["x", (x + 1) % n_bx, y, -1] = slot
             up, down = (x, y, 1), (x, (y + 1) % n_by, -1)
             for source, target in ((up, y + 1), (down, y)):
                 ahead = x < n_bx // 2 and target in (0, n_by // 2 - 1)
+                ahead = ahead or (1 < x < 2 * n_bx // 3 and y in (0, n_by // 2 - 2))
                 chosen_slots["y", *source] = 1 if y % 2 else 0 if ahead else 2
             if x == 0 and (y < 4 or y >= n_by - 3):
                 special = {0: 1, 1: 0, 2: 2, 3: 0, n_by - 3: 1, n_by - 2: 0, n_by - 1: 2}
@@ -399,48 +390,46 @@
     anywhere = pl.BlockSpec(memory_space=pl.ANY)
     params = pltpu.CompilerParams(vmem_limit_bytes=24 * 2**20)
     plane = (SIDE, SIDE)
-    f, mask = stay(populations.reshape(19, *plane)), stay(solid_mask.reshape(plane))
+    f, mask = populations.reshape(19, *plane), solid_mask.reshape(plane)
     message = in_vmem(8, SIDE)
     collided = (
-        in_vmem(19, *plane), in_vmem(19, *plane), in_vmem(*plane), in_vmem(*plane),
-        in_vmem(4, 8, SIDE),
-    )
-    work = [
-        pltpu.VMEM(plane, jnp.int32), pltpu.VMEM(plane, F32),
-        pltpu.SemaphoreType.DMA((CHUNKS + 1,)),
-    ]
+        in_vmem(19, *plane), in_vmem(*plane), in_vmem(*plane), in_vmem(4, 8, SIDE),
+    )
     pairs, codes = plan(n_bx, n_by)
-    *x_msgs, picks, live_v, f_v, r_v, solid_v, active_v, y_pre = pl.pallas_call(
+    *x_msgs, picks, live_v, r_v, solid_v, active_v, y_pre = pl.pallas_call(
         rim_kernel,
         out_shape=(message,) * X_SLOTS + (in_vmem(4 + Y_SLOTS, 8, SIDE), in_vmem(4, 8, SIDE)) + collided,
         in_specs=[hbm] * 5,
-        out_specs=[vmem] * (X_SLOTS + 7),
+        out_specs=[vmem] * (X_SLOTS + 6),
         scratch_shapes=[
             pltpu.VMEM((2, 19, 8, SIDE), F32), pltpu.VMEM((2, 8, SIDE), jnp.int32),
             pltpu.SMEM((1, n_bx), jnp.int32), pltpu.SMEM((1, 1, 4), jnp.int32),
-            pltpu.SMEM(codes.shape, jnp.int32), *work, pltpu.SemaphoreType.DMA((7,)),
+            pltpu.SMEM(codes.shape, jnp.int32), pltpu.VMEM((19, *plane), F32),
+            pltpu.VMEM(plane, jnp.int32), pltpu.VMEM(plane, F32), pltpu.SemaphoreType.DMA((7,)),
         ],
         compiler_params=params,
         name="rim",
-    )(stay(pore_count.T), stay(pore_list), stay(jnp.asarray(codes)), f, mask)
+    )(stay(pore_count.T), stay(pore_list), stay(jnp.asarray(codes)), stay(f), stay(mask))
 
     x_halos = [
         keep(lax.ppermute(message, ("bx", "by"), group)) for message, group in zip(x_msgs, pairs["x"])
     ]
 
-    f_v, r_v, solid_v, active_v, y_pre = pl.pallas_call(
+    f_v, mask_v, _ = lax.optimization_barrier((f, mask, live_v))
+
+    r_v, solid_v, active_v, y_pre = pl.pallas_call(
         collide_kernel,
         out_shape=collided,
-        in_specs=[hbm] * 2 + [vmem] * 6,
-        out_specs=[vmem] * 5,
-        scratch_shapes=work,
-        input_output_aliases={3: 0, 4: 1, 5: 2, 6: 3, 7: 4},
+        in_specs=[vmem] * 7,
+        out_specs=[vmem] * 4,
+        scratch_shapes=[pltpu.VMEM(plane, F32)],
+        input_output_aliases={3: 0, 4: 1, 5: 2, 6: 3},
         compiler_params=params,
         cost_estimate=pl.CostEstimate(
             flops=8_000_000, bytes_accessed=4_000_000, transcendentals=0
         ),
         name="collide",
-    )(f, mask, keep(live_v), *(keep(x) for x in (f_v, r_v, solid_v, active_v, y_pre)))
+    )(keep(f_v), keep(mask_v), keep(live_v), *(keep(x) for x in (r_v, solid_v, active_v, y_pre)))
 
     y_msgs = pl.pallas_call(
         corner_kernel,

time: 35 us -> 34.3 us (0.980)
  the two profiles are of different devices: /device:TPU:48 before, /device:TPU:56 now
where the time goes in v6:
time: 34.3 us; the launch traced here: 34 us
  starting transfers between devices  26.4 us (77%)
  Pallas kernels  5.84 us (17%)
  waiting for transfers between devices  1.61 us (5%)
    ppermute x6, starting transfers between devices, local(): lax.ppermute(message, ('bx', 'by'), group)  26.4 us
    pallas_call x1, Pallas kernels, local(): pl.pallas_call(rim_kernel, out_shape=(message,) * X_SLOTS + (in_vmem(4 +...  3.38 us
    ppermute x6, waiting for transfers between devices, local(): lax.ppermute(message, ('bx', 'by'), group)  1.61 us
    pallas_call x1, Pallas kernels, local(): pl.pallas_call(stream_kernel, out_shape=(shape(19, *plane), in_vmem(10, *...  1.21 us
    pallas_call x1, Pallas kernels, local(): pl.pallas_call(patch_kernel, out_shape=shape(19, *plane), in_specs=[vmem]...  1.15 us
  transfers between devices with their start and end apart: 6, of which 2 were waited for; matrix products, arithmetic and copies ran while one was open for 0% of the time, Pallas kernels for 4%

profile of v6, /device:TPU:56, one launch (start us, length us, event | category | flops | bytes accessed | tf_op | source)
XLA Modules:
  0.0 34.0 jit_solution(13024303905387070433)
XLA Ops:
  0.0 0.0 copy-start
  0.0 0.0 copy-start.1
  0.0 3.4 %rim.1 = (f32[8,128]{1,0:T(8,128)S(1)}, f32[8,128]{1,0:T(8,128)S(1)}, f32[8,128]{1,0:T(8,128)S(1)}, f32[7,8,128]{2,1,0:T(8,128)S(1)}, f32[4,8,128]{2,1,0:T(8,128...) custom-call(s32[1,48]{1,0:T(1,128)} %bitcast.11, ...), custom_call_target="tpu_custom_call" | custom-call | tf_op jit(solution)/shard_map/rim/pallas_call | solution.py:399
  3.4 1.9 %collective-permute-start = (f32[8,128]{1,0:T(8,128)S(1)}, f32[8,128]{1,0:T(8,128)S(1)}, u32[]{:S(2)}, u32[]{:S(2)}) collective-permute-start(f32[8,128]{1,0:T(8,128)S(1)} %get-tuple-element.37), channel_id=1, source_target_pairs={{1,17},{17,1},{2,18},{18,2},{3,19},{19,3},{4,20},{20,4},{5,21},{21... | collective-permute-start | bytes 12296 | tf_op jit(solution)/shard_map/ppermute | solution.py:415
  5.3 10.9 %collective-permute-start.1 = (f32[8,128]{1,0:T(8,128)S(1)}, f32[8,128]{1,0:T(8,128)S(1)}, u32[]{:S(2)}, u32[]{:S(2)}) collective-permute-start(f32[8,128]{1,0:T(8,128)S(1)} %get-tuple-element.38), channel_id=1, source_target_pairs={{0,16},{16,0},{17,33},{33,17},{18,34},{34,18},{19,35},{35,19},{20,... | collective-permute-start | bytes 12296 | tf_op jit(solution)/shard_map/ppermute | solution.py:415
  16.2 0.7 %collective-permute-start.2 = (f32[8,128]{1,0:T(8,128)S(1)}, f32[8,128]{1,0:T(8,128)S(1)}, u32[]{:S(2)}, u32[]{:S(2)}) collective-permute-start(f32[8,128]{1,0:T(8,128)S(1)} %get-tuple-element.39), channel_id=1, source_target_pairs={{8,24},{24,8},{737,753},{753,737},{738,754},{754,738},{739,755},{7... | collective-permute-start | bytes 12296 | tf_op jit(solution)/shard_map/ppermute | solution.py:415
  16.9 0.0 copy-done
  16.9 0.0 copy-done.1
  17.0 0.0 collective-permute-done.refs_0_
  17.0 0.6 %collective-permute-done.1.refs_1_ = f32[8,128]{1,0:T(8,128)S(1)} collective-permute-done((f32[8,128]{1,0:T(8,128)S(1)}, f32[8,128]{1,0:T(8,128)S(1)}, u32[]{:S(2)}, u32[]{:S(2)}) %collective-permute-start.1) | collective-permute-done | bytes 4128 | tf_op jit(solution)/shard_map/ppermute | solution.py:415
  17.5 0.0 collective-permute-done.2.refs_2_
  17.5 0.1 corner.1
  17.6 1.3 %collective-permute-start.3 = (f32[8,128]{1,0:T(8,128)S(1)}, f32[8,128]{1,0:T(8,128)S(1)}, u32[]{:S(2)}, u32[]{:S(2)}) collective-permute-start(f32[8,128]{1,0:T(8,128)S(1)} %get-tuple-element.42), channel_id=1, source_target_pairs={{1,2},{2,1},{3,4},{4,3},{6,7},{14,15},{15,14},{17,16},{22,23},{32,... | collective-permute-start | bytes 12296 | tf_op jit(solution)/shard_map/ppermute | solution.py:444
  18.9 10.4 %collective-permute-start.4 = (f32[8,128]{1,0:T(8,128)S(1)}, f32[8,128]{1,0:T(8,128)S(1)}, u32[]{:S(2)}, u32[]{:S(2)}) collective-permute-start(f32[8,128]{1,0:T(8,128)S(1)} %get-tuple-element.43), channel_id=1, source_target_pairs={{0,1},{1,0},{5,6},{6,5},{7,8},{8,7},{9,10},{10,9},{11,12},{12,11},... | collective-permute-start | bytes 12296 | tf_op jit(solution)/shard_map/ppermute | solution.py:444
  29.3 1.3 %collective-permute-start.5 = (f32[8,128]{1,0:T(8,128)S(1)}, f32[8,128]{1,0:T(8,128)S(1)}, u32[]{:S(2)}, u32[]{:S(2)}) collective-permute-start(f32[8,128]{1,0:T(8,128)S(1)} %get-tuple-element.44), channel_id=1, source_target_pairs={{2,3},{3,2},{4,5},{5,4},{7,6},{8,9},{9,8},{10,11},{11,10},{12,13},... | collective-permute-start | bytes 12296 | tf_op jit(solution)/shard_map/ppermute | solution.py:444
  30.6 1.2 %stream.1 = (f32[19,128,128]{2,1,0:T(8,128)}, f32[10,128,128]{2,1,0:T(8,128)S(1)}) custom-call(f32[19,128,128]{2,1,0:T(8,128)S(1)} %bitcast.8, f32[19,128,128]{2,1,0:T(8,128)S(1)} %get-tuple-element.34.r_v, f32[128,128]{1,0:T(8,128)S(1)} %get-tuple-element.35.solid_v, f32[128,128]{1,0:T(8,128)S(1)} %get-tuple-element.36.active_v, ...), custom_call_target="tpu_custom_call" | custom-call | flops 8000000 | bytes 4000000 | tf_op jit(solution)/shard_map/stream/pallas_call | solution.py:447
  31.8 0.0 collective-permute-done.3.refs_0_
  31.8 1.0 %collective-permute-done.4.refs_1_ = f32[8,128]{1,0:T(8,128)S(1)} collective-permute-done((f32[8,128]{1,0:T(8,128)S(1)}, f32[8,128]{1,0:T(8,128)S(1)}, u32[]{:S(2)}, u32[]{:S(2)}) %collective-permute-start.4) | collective-permute-done | bytes 4128 | tf_op jit(solution)/shard_map/ppermute | solution.py:444
  32.8 0.0 collective-permute-done.5.refs_2_
  32.8 1.1 %patch.1 = f32[19,128,128]{2,1,0:T(8,128)} custom-call(f32[4,8,128]{2,1,0:T(8,128)S(1)} %get-tuple-element.32.y_pre, f32[7,8,128]{2,1,0:T(8,128)S(1)} %get-tuple-element.33.picks, f32[10,128,128]{2,1,0:T(8,128)S(1)} %get-tuple-element.40.partial, f32[19,128,128]{2,1,0:T(8,128)} %get-tuple-element.41.started, ...), custom_call_target="tpu_custom_call", output_to_operand_aliasing={{}: (3, {})} | custom-call | tf_op jit(solution)/shard_map/patch/pallas_call | solution.py:463
  (1 shorter events, 0.0 us)
Async XLA Ops:
  0.0 16.9 %copy-start = (f32[19,1,128,128]{3,2,1,0:T(8,128)S(1)}, f32[19,1,128,128]{3,2,1,0:T(8,128)}, u32[]{:S(2)}) copy-start(f32[19,1,128,128]{3,2,1,0:T(8,128)} %param.5) | copy-start | bytes 3735556
  0.0 16.9 %copy-start.1 = (s32[1,128,128]{2,1,0:T(8,128)S(1)}, s32[1,128,128]{2,1,0:T(8,128)}, u32[]{:S(2)}) copy-start(s32[1,128,128]{2,1,0:T(8,128)} %param.6) | copy-start | bytes 196612
  3.4 13.6 %collective-permute-start = (f32[8,128]{1,0:T(8,128)S(1)}, f32[8,128]{1,0:T(8,128)S(1)}, u32[]{:S(2)}, u32[]{:S(2)}) collective-permute-start(f32[8,128]{1,0:T(8,128)S(1)} %get-tuple-element.37), channel_id=1, source_target_pairs={{1,17},{17,1},{2,18},{18,2},{3,19},{19,3},{4,20},{20,4},{5,21},{21... | collective-permute-start | bytes 12296 | tf_op jit(solution)/shard_map/ppermute | solution.py:415
  5.3 12.2 %collective-permute-start.1 = (f32[8,128]{1,0:T(8,128)S(1)}, f32[8,128]{1,0:T(8,128)S(1)}, u32[]{:S(2)}, u32[]{:S(2)}) collective-permute-start(f32[8,128]{1,0:T(8,128)S(1)} %get-tuple-element.38), channel_id=1, source_target_pairs={{0,16},{16,0},{17,33},{33,17},{18,34},{34,18},{19,35},{35,19},{20,... | collective-permute-start | bytes 12296 | tf_op jit(solution)/shard_map/ppermute | solution.py:415
  16.2 1.3 %collective-permute-start.2 = (f32[8,128]{1,0:T(8,128)S(1)}, f32[8,128]{1,0:T(8,128)S(1)}, u32[]{:S(2)}, u32[]{:S(2)}) collective-permute-start(f32[8,128]{1,0:T(8,128)S(1)} %get-tuple-element.39), channel_id=1, source_target_pairs={{8,24},{24,8},{737,753},{753,737},{738,754},{754,738},{739,755},{7... | collective-permute-start | bytes 12296 | tf_op jit(solution)/shard_map/ppermute | solution.py:415
  17.6 14.2 %collective-permute-start.3 = (f32[8,128]{1,0:T(8,128)S(1)}, f32[8,128]{1,0:T(8,128)S(1)}, u32[]{:S(2)}, u32[]{:S(2)}) collective-permute-start(f32[8,128]{1,0:T(8,128)S(1)} %get-tuple-element.42), channel_id=1, source_target_pairs={{1,2},{2,1},{3,4},{4,3},{6,7},{14,15},{15,14},{17,16},{22,23},{32,... | collective-permute-start | bytes 12296 | tf_op jit(solution)/shard_map/ppermute | solution.py:444
  18.9 13.9 %collective-permute-start.4 = (f32[8,128]{1,0:T(8,128)S(1)}, f32[8,128]{1,0:T(8,128)S(1)}, u32[]{:S(2)}, u32[]{:S(2)}) collective-permute-start(f32[8,128]{1,0:T(8,128)S(1)} %get-tuple-element.43), channel_id=1, source_target_pairs={{0,1},{1,0},{5,6},{6,5},{7,8},{8,7},{9,10},{10,9},{11,12},{12,11},... | collective-permute-start | bytes 12296 | tf_op jit(solution)/shard_map/ppermute | solution.py:444
  29.3 3.6 %collective-permute-start.5 = (f32[8,128]{1,0:T(8,128)S(1)}, f32[8,128]{1,0:T(8,128)S(1)}, u32[]{:S(2)}, u32[]{:S(2)}) collective-permute-start(f32[8,128]{1,0:T(8,128)S(1)} %get-tuple-element.44), channel_id=1, source_target_pairs={{2,3},{3,2},{4,5},{5,4},{7,6},{8,9},{9,8},{10,11},{11,10},{12,13},... | collective-permute-start | bytes 12296 | tf_op jit(solution)/shard_map/ppermute | solution.py:444

commit v7 on v6

--- a/solution.py
+++ b/solution.py
@@ -349,21 +349,24 @@
 
 def slots(n_bx, n_by):
     chosen_slots = {}
+    half = n_by // 2
     for x in range(n_bx):
         for y in range(n_by):
+            middle = 1 < y < half - 2
             if x % 2 == 0:
-                slot = 1 if y == 0 else 2 if x == n_bx - 2 or (x == 0 and y == n_by // 2) else 0
+                slot = 1 if y == 0 or (x == n_bx - 2 and middle) else 2 if x == n_bx - 2 else 0
+                slot = 2 if x == 0 and y == half else slot
             else:
                 slot = 1 if y else 2 if x == n_bx - 1 else 0
+                slot = 2 if x in (n_bx - 3, n_bx - 1) and middle else slot
             chosen_slots["x", x, y, 1] = chosen_slots["x", (x + 1) % n_bx, y, -1] = slot
             up, down = (x, y, 1), (x, (y + 1) % n_by, -1)
             for source, target in ((up, y + 1), (down, y)):
-                ahead = x < n_bx // 2 and target in (0, n_by // 2 - 1)
-                ahead = ahead or (1 < x < 2 * n_bx // 3 and y in (0, n_by // 2 - 2))
+                ahead = x < n_bx // 2 and target in (0, half - 1)
+                ahead = ahead or (1 < x < 2 * n_bx // 3 and y in (0, half - 2))
+                ahead = ahead or (x == 1 and y == half - 2)
+                ahead = ahead or (x == 0 and y in (0, 2, n_by - 2))
                 chosen_slots["y", *source] = 1 if y % 2 else 0 if ahead else 2
-            if x == 0 and (y < 4 or y >= n_by - 3):
-                special = {0: 1, 1: 0, 2: 2, 3: 0, n_by - 3: 1, n_by - 2: 0, n_by - 1: 2}
-                chosen_slots["y", *up] = chosen_slots["y", *down] = special[y]
     return chosen_slots
 
 

time: 34.3 us -> 34.2 us (level)
  no operation moved by 1% of the time
where the time goes in v7:
time: 34.2 us; the launch traced here: 34 us
  starting transfers between devices  26.4 us (77%)
  Pallas kernels  5.84 us (17%)
  waiting for transfers between devices  1.61 us (5%)
    ppermute x6, starting transfers between devices, local(): lax.ppermute(message, ('bx', 'by'), group)  26.4 us
    pallas_call x1, Pallas kernels, local(): pl.pallas_call(rim_kernel, out_shape=(message,) * X_SLOTS + (in_vmem(4 +...  3.38 us
    ppermute x6, waiting for transfers between devices, local(): lax.ppermute(message, ('bx', 'by'), group)  1.61 us
    pallas_call x1, Pallas kernels, local(): pl.pallas_call(stream_kernel, out_shape=(shape(19, *plane), in_vmem(10, *...  1.21 us
    pallas_call x1, Pallas kernels, local(): pl.pallas_call(patch_kernel, out_shape=shape(19, *plane), in_specs=[vmem]...  1.15 us
  transfers between devices with their start and end apart: 6, of which 2 were waited for; matrix products, arithmetic and copies ran while one was open for 0% of the time, Pallas kernels for 4%

profile of v7, /device:TPU:56, one launch (start us, length us, event | category | flops | bytes accessed | tf_op | source)
XLA Modules:
  0.0 34.0 jit_solution(4573298863823414029)
XLA Ops:
  0.0 0.0 copy-start
  0.0 0.0 copy-start.1
  0.0 3.4 %rim.1 = (f32[8,128]{1,0:T(8,128)S(1)}, f32[8,128]{1,0:T(8,128)S(1)}, f32[8,128]{1,0:T(8,128)S(1)}, f32[7,8,128]{2,1,0:T(8,128)S(1)}, f32[4,8,128]{2,1,0:T(8,128...) custom-call(s32[1,48]{1,0:T(1,128)} %bitcast.11, ...), custom_call_target="tpu_custom_call" | custom-call | tf_op jit(solution)/shard_map/rim/pallas_call | solution.py:402
  3.4 1.9 %collective-permute-start = (f32[8,128]{1,0:T(8,128)S(1)}, f32[8,128]{1,0:T(8,128)S(1)}, u32[]{:S(2)}, u32[]{:S(2)}) collective-permute-start(f32[8,128]{1,0:T(8,128)S(1)} %get-tuple-element.37), channel_id=1, source_target_pairs={{1,17},{17,1},{2,18},{18,2},{3,19},{19,3},{4,20},{20,4},{5,21},{21... | collective-permute-start | bytes 12296 | tf_op jit(solution)/shard_map/ppermute | solution.py:418
  5.3 10.9 %collective-permute-start.1 = (f32[8,128]{1,0:T(8,128)S(1)}, f32[8,128]{1,0:T(8,128)S(1)}, u32[]{:S(2)}, u32[]{:S(2)}) collective-permute-start(f32[8,128]{1,0:T(8,128)S(1)} %get-tuple-element.38), channel_id=1, source_target_pairs={{0,16},{16,0},{17,33},{33,17},{18,34},{34,18},{19,35},{35,19},{20,... | collective-permute-start | bytes 12296 | tf_op jit(solution)/shard_map/ppermute | solution.py:418
  16.2 0.7 %collective-permute-start.2 = (f32[8,128]{1,0:T(8,128)S(1)}, f32[8,128]{1,0:T(8,128)S(1)}, u32[]{:S(2)}, u32[]{:S(2)}) collective-permute-start(f32[8,128]{1,0:T(8,128)S(1)} %get-tuple-element.39), channel_id=1, source_target_pairs={{8,24},{24,8},{722,738},{738,722},{723,739},{739,723},{724,740},{7... | collective-permute-start | bytes 12296 | tf_op jit(solution)/shard_map/ppermute | solution.py:418
  16.9 0.0 copy-done
  16.9 0.0 copy-done.1
  17.0 0.0 collective-permute-done.refs_0_
  17.0 0.6 %collective-permute-done.1.refs_1_ = f32[8,128]{1,0:T(8,128)S(1)} collective-permute-done((f32[8,128]{1,0:T(8,128)S(1)}, f32[8,128]{1,0:T(8,128)S(1)}, u32[]{:S(2)}, u32[]{:S(2)}) %collective-permute-start.1) | collective-permute-done | bytes 4128 | tf_op jit(solution)/shard_map/ppermute | solution.py:418
  17.5 0.0 collective-permute-done.2.refs_2_
  17.5 0.1 corner.1
  17.6 1.3 %collective-permute-start.3 = (f32[8,128]{1,0:T(8,128)S(1)}, f32[8,128]{1,0:T(8,128)S(1)}, u32[]{:S(2)}, u32[]{:S(2)}) collective-permute-start(f32[8,128]{1,0:T(8,128)S(1)} %get-tuple-element.42), channel_id=1, source_target_pairs={{0,1},{1,0},{2,3},{3,2},{6,7},{14,15},{15,14},{17,16},{22,23},{23,... | collective-permute-start | bytes 12296 | tf_op jit(solution)/shard_map/ppermute | solution.py:447
  18.9 10.4 %collective-permute-start.4 = (f32[8,128]{1,0:T(8,128)S(1)}, f32[8,128]{1,0:T(8,128)S(1)}, u32[]{:S(2)}, u32[]{:S(2)}) collective-permute-start(f32[8,128]{1,0:T(8,128)S(1)} %get-tuple-element.43), channel_id=1, source_target_pairs={{1,2},{2,1},{3,4},{4,3},{5,6},{6,5},{7,8},{8,7},{9,10},{10,9},{11,... | collective-permute-start | bytes 12296 | tf_op jit(solution)/shard_map/ppermute | solution.py:447
  29.3 1.3 %collective-permute-start.5 = (f32[8,128]{1,0:T(8,128)S(1)}, f32[8,128]{1,0:T(8,128)S(1)}, u32[]{:S(2)}, u32[]{:S(2)}) collective-permute-start(f32[8,128]{1,0:T(8,128)S(1)} %get-tuple-element.44), channel_id=1, source_target_pairs={{4,5},{5,4},{7,6},{8,9},{9,8},{10,11},{11,10},{12,13},{13,12},{16,... | collective-permute-start | bytes 12296 | tf_op jit(solution)/shard_map/ppermute | solution.py:447
  30.6 1.2 %stream.1 = (f32[19,128,128]{2,1,0:T(8,128)}, f32[10,128,128]{2,1,0:T(8,128)S(1)}) custom-call(f32[19,128,128]{2,1,0:T(8,128)S(1)} %bitcast.8, f32[19,128,128]{2,1,0:T(8,128)S(1)} %get-tuple-element.34.r_v, f32[128,128]{1,0:T(8,128)S(1)} %get-tuple-element.35.solid_v, f32[128,128]{1,0:T(8,128)S(1)} %get-tuple-element.36.active_v, ...), custom_call_target="tpu_custom_call" | custom-call | flops 8000000 | bytes 4000000 | tf_op jit(solution)/shard_map/stream/pallas_call | solution.py:450
  31.8 0.0 collective-permute-done.3.refs_0_
  31.8 1.0 %collective-permute-done.4.refs_1_ = f32[8,128]{1,0:T(8,128)S(1)} collective-permute-done((f32[8,128]{1,0:T(8,128)S(1)}, f32[8,128]{1,0:T(8,128)S(1)}, u32[]{:S(2)}, u32[]{:S(2)}) %collective-permute-start.4) | collective-permute-done | bytes 4128 | tf_op jit(solution)/shard_map/ppermute | solution.py:447
  32.8 0.0 collective-permute-done.5.refs_2_
  32.8 1.1 %patch.1 = f32[19,128,128]{2,1,0:T(8,128)} custom-call(f32[4,8,128]{2,1,0:T(8,128)S(1)} %get-tuple-element.32.y_pre, f32[7,8,128]{2,1,0:T(8,128)S(1)} %get-tuple-element.33.picks, f32[10,128,128]{2,1,0:T(8,128)S(1)} %get-tuple-element.40.partial, f32[19,128,128]{2,1,0:T(8,128)} %get-tuple-element.41.started, ...), custom_call_target="tpu_custom_call", output_to_operand_aliasing={{}: (3, {})} | custom-call | tf_op jit(solution)/shard_map/patch/pallas_call | solution.py:466
  (1 shorter events, 0.0 us)
Async XLA Ops:
  0.0 16.9 %copy-start = (f32[19,1,128,128]{3,2,1,0:T(8,128)S(1)}, f32[19,1,128,128]{3,2,1,0:T(8,128)}, u32[]{:S(2)}) copy-start(f32[19,1,128,128]{3,2,1,0:T(8,128)} %param.5) | copy-start | bytes 3735556
  0.0 16.9 %copy-start.1 = (s32[1,128,128]{2,1,0:T(8,128)S(1)}, s32[1,128,128]{2,1,0:T(8,128)}, u32[]{:S(2)}) copy-start(s32[1,128,128]{2,1,0:T(8,128)} %param.6) | copy-start | bytes 196612
  3.4 13.6 %collective-permute-start = (f32[8,128]{1,0:T(8,128)S(1)}, f32[8,128]{1,0:T(8,128)S(1)}, u32[]{:S(2)}, u32[]{:S(2)}) collective-permute-start(f32[8,128]{1,0:T(8,128)S(1)} %get-tuple-element.37), channel_id=1, source_target_pairs={{1,17},{17,1},{2,18},{18,2},{3,19},{19,3},{4,20},{20,4},{5,21},{21... | collective-permute-start | bytes 12296 | tf_op jit(solution)/shard_map/ppermute | solution.py:418
  5.3 12.2 %collective-permute-start.1 = (f32[8,128]{1,0:T(8,128)S(1)}, f32[8,128]{1,0:T(8,128)S(1)}, u32[]{:S(2)}, u32[]{:S(2)}) collective-permute-start(f32[8,128]{1,0:T(8,128)S(1)} %get-tuple-element.38), channel_id=1, source_target_pairs={{0,16},{16,0},{17,33},{33,17},{18,34},{34,18},{19,35},{35,19},{20,... | collective-permute-start | bytes 12296 | tf_op jit(solution)/shard_map/ppermute | solution.py:418
  16.2 1.3 %collective-permute-start.2 = (f32[8,128]{1,0:T(8,128)S(1)}, f32[8,128]{1,0:T(8,128)S(1)}, u32[]{:S(2)}, u32[]{:S(2)}) collective-permute-start(f32[8,128]{1,0:T(8,128)S(1)} %get-tuple-element.39), channel_id=1, source_target_pairs={{8,24},{24,8},{722,738},{738,722},{723,739},{739,723},{724,740},{7... | collective-permute-start | bytes 12296 | tf_op jit(solution)/shard_map/ppermute | solution.py:418
  17.6 14.2 %collective-permute-start.3 = (f32[8,128]{1,0:T(8,128)S(1)}, f32[8,128]{1,0:T(8,128)S(1)}, u32[]{:S(2)}, u32[]{:S(2)}) collective-permute-start(f32[8,128]{1,0:T(8,128)S(1)} %get-tuple-element.42), channel_id=1, source_target_pairs={{0,1},{1,0},{2,3},{3,2},{6,7},{14,15},{15,14},{17,16},{22,23},{23,... | collective-permute-start | bytes 12296 | tf_op jit(solution)/shard_map/ppermute | solution.py:447
  18.9 13.9 %collective-permute-start.4 = (f32[8,128]{1,0:T(8,128)S(1)}, f32[8,128]{1,0:T(8,128)S(1)}, u32[]{:S(2)}, u32[]{:S(2)}) collective-permute-start(f32[8,128]{1,0:T(8,128)S(1)} %get-tuple-element.43), channel_id=1, source_target_pairs={{1,2},{2,1},{3,4},{4,3},{5,6},{6,5},{7,8},{8,7},{9,10},{10,9},{11,... | collective-permute-start | bytes 12296 | tf_op jit(solution)/shard_map/ppermute | solution.py:447
  29.3 3.6 %collective-permute-start.5 = (f32[8,128]{1,0:T(8,128)S(1)}, f32[8,128]{1,0:T(8,128)S(1)}, u32[]{:S(2)}, u32[]{:S(2)}) collective-permute-start(f32[8,128]{1,0:T(8,128)S(1)} %get-tuple-element.44), channel_id=1, source_target_pairs={{4,5},{5,4},{7,6},{8,9},{9,8},{10,11},{11,10},{12,13},{13,12},{16,... | collective-permute-start | bytes 12296 | tf_op jit(solution)/shard_map/ppermute | solution.py:447

commit v8 on v7

--- a/solution.py
+++ b/solution.py
@@ -150,9 +150,10 @@
         edge_f, edge_m, count_ref, list_ref, plan_ref, f_v, mask_v, columns, sems,
     ) = refs
     ends = (pl.ds(SIDE - 8, 8), pl.ds(0, 8))
-    pairs = [(count_hbm, count_ref), (list_hbm, list_ref), (plan_hbm, plan_ref)]
+    pairs = []
     for n, end in enumerate(ends):
         pairs += [(m_hbm.at[end, :], edge_m.at[n]), (f_hbm.at[:, end, :], edge_f.at[n])]
+    pairs += [(count_hbm, count_ref), (list_hbm, list_ref), (plan_hbm, plan_ref)]
     copies = [pltpu.make_async_copy(s, t, sems.at[n]) for n, (s, t) in enumerate(pairs)]
     for copy in copies:
         copy.start()

time: 34.2 us -> 34.3 us (level)
  no operation moved by 1% of the time
where the time goes in v8:
time: 34.3 us; the launch traced here: 34 us
  starting transfers between devices  26.4 us (77%)
  Pallas kernels  5.86 us (17%)
  waiting for transfers between devices  1.61 us (5%)
    ppermute x6, starting transfers between devices, local(): lax.ppermute(message, ('bx', 'by'), group)  26.4 us
    pallas_call x1, Pallas kernels, local(): pl.pallas_call(rim_kernel, out_shape=(message,) * X_SLOTS + (in_vmem(4 +...  3.4 us
    ppermute x6, waiting for transfers between devices, local(): lax.ppermute(message, ('bx', 'by'), group)  1.61 us
    pallas_call x1, Pallas kernels, local(): pl.pallas_call(stream_kernel, out_shape=(shape(19, *plane), in_vmem(10, *...  1.21 us
    pallas_call x1, Pallas kernels, local(): pl.pallas_call(patch_kernel, out_shape=shape(19, *plane), in_specs=[vmem]...  1.15 us
  transfers between devices with their start and end apart: 6, of which 2 were waited for; matrix products, arithmetic and copies ran while one was open for 0% of the time, Pallas kernels for 4%

profile of v8, /device:TPU:56, one launch (start us, length us, event | category | flops | bytes accessed | tf_op | source)
XLA Modules:
  0.0 34.0 jit_solution(13962511338282089456)
XLA Ops:
  0.0 0.0 copy-start
  0.0 0.0 copy-start.1
  0.0 3.4 %rim.1 = (f32[8,128]{1,0:T(8,128)S(1)}, f32[8,128]{1,0:T(8,128)S(1)}, f32[8,128]{1,0:T(8,128)S(1)}, f32[7,8,128]{2,1,0:T(8,128)S(1)}, f32[4,8,128]{2,1,0:T(8,128...) custom-call(s32[1,48]{1,0:T(1,128)} %bitcast.11, ...), custom_call_target="tpu_custom_call" | custom-call | tf_op jit(solution)/shard_map/rim/pallas_call | solution.py:403
  3.4 1.9 %collective-permute-start = (f32[8,128]{1,0:T(8,128)S(1)}, f32[8,128]{1,0:T(8,128)S(1)}, u32[]{:S(2)}, u32[]{:S(2)}) collective-permute-start(f32[8,128]{1,0:T(8,128)S(1)} %get-tuple-element.37), channel_id=1, source_target_pairs={{1,17},{17,1},{2,18},{18,2},{3,19},{19,3},{4,20},{20,4},{5,21},{21... | collective-permute-start | bytes 12296 | tf_op jit(solution)/shard_map/ppermute | solution.py:419
  5.3 10.9 %collective-permute-start.1 = (f32[8,128]{1,0:T(8,128)S(1)}, f32[8,128]{1,0:T(8,128)S(1)}, u32[]{:S(2)}, u32[]{:S(2)}) collective-permute-start(f32[8,128]{1,0:T(8,128)S(1)} %get-tuple-element.38), channel_id=1, source_target_pairs={{0,16},{16,0},{17,33},{33,17},{18,34},{34,18},{19,35},{35,19},{20,... | collective-permute-start | bytes 12296 | tf_op jit(solution)/shard_map/ppermute | solution.py:419
  16.3 0.7 %collective-permute-start.2 = (f32[8,128]{1,0:T(8,128)S(1)}, f32[8,128]{1,0:T(8,128)S(1)}, u32[]{:S(2)}, u32[]{:S(2)}) collective-permute-start(f32[8,128]{1,0:T(8,128)S(1)} %get-tuple-element.39), channel_id=1, source_target_pairs={{8,24},{24,8},{722,738},{738,722},{723,739},{739,723},{724,740},{7... | collective-permute-start | bytes 12296 | tf_op jit(solution)/shard_map/ppermute | solution.py:419
  16.9 0.0 copy-done
  16.9 0.0 copy-done.1
  17.0 0.0 collective-permute-done.refs_0_
  17.0 0.6 %collective-permute-done.1.refs_1_ = f32[8,128]{1,0:T(8,128)S(1)} collective-permute-done((f32[8,128]{1,0:T(8,128)S(1)}, f32[8,128]{1,0:T(8,128)S(1)}, u32[]{:S(2)}, u32[]{:S(2)}) %collective-permute-start.1) | collective-permute-done | bytes 4128 | tf_op jit(solution)/shard_map/ppermute | solution.py:419
  17.6 0.0 collective-permute-done.2.refs_2_
  17.6 0.1 corner.1
  17.6 1.3 %collective-permute-start.3 = (f32[8,128]{1,0:T(8,128)S(1)}, f32[8,128]{1,0:T(8,128)S(1)}, u32[]{:S(2)}, u32[]{:S(2)}) collective-permute-start(f32[8,128]{1,0:T(8,128)S(1)} %get-tuple-element.42), channel_id=1, source_target_pairs={{0,1},{1,0},{2,3},{3,2},{6,7},{14,15},{15,14},{17,16},{22,23},{23,... | collective-permute-start | bytes 12296 | tf_op jit(solution)/shard_map/ppermute | solution.py:448
  18.9 10.4 %collective-permute-start.4 = (f32[8,128]{1,0:T(8,128)S(1)}, f32[8,128]{1,0:T(8,128)S(1)}, u32[]{:S(2)}, u32[]{:S(2)}) collective-permute-start(f32[8,128]{1,0:T(8,128)S(1)} %get-tuple-element.43), channel_id=1, source_target_pairs={{1,2},{2,1},{3,4},{4,3},{5,6},{6,5},{7,8},{8,7},{9,10},{10,9},{11,... | collective-permute-start | bytes 12296 | tf_op jit(solution)/shard_map/ppermute | solution.py:448
  29.3 1.3 %collective-permute-start.5 = (f32[8,128]{1,0:T(8,128)S(1)}, f32[8,128]{1,0:T(8,128)S(1)}, u32[]{:S(2)}, u32[]{:S(2)}) collective-permute-start(f32[8,128]{1,0:T(8,128)S(1)} %get-tuple-element.44), channel_id=1, source_target_pairs={{4,5},{5,4},{7,6},{8,9},{9,8},{10,11},{11,10},{12,13},{13,12},{16,... | collective-permute-start | bytes 12296 | tf_op jit(solution)/shard_map/ppermute | solution.py:448
  30.6 1.2 %stream.1 = (f32[19,128,128]{2,1,0:T(8,128)}, f32[10,128,128]{2,1,0:T(8,128)S(1)}) custom-call(f32[19,128,128]{2,1,0:T(8,128)S(1)} %bitcast.8, f32[19,128,128]{2,1,0:T(8,128)S(1)} %get-tuple-element.34.r_v, f32[128,128]{1,0:T(8,128)S(1)} %get-tuple-element.35.solid_v, f32[128,128]{1,0:T(8,128)S(1)} %get-tuple-element.36.active_v, ...), custom_call_target="tpu_custom_call" | custom-call | flops 8000000 | bytes 4000000 | tf_op jit(solution)/shard_map/stream/pallas_call | solution.py:451
  31.8 0.0 collective-permute-done.3.refs_0_
  31.8 1.0 %collective-permute-done.4.refs_1_ = f32[8,128]{1,0:T(8,128)S(1)} collective-permute-done((f32[8,128]{1,0:T(8,128)S(1)}, f32[8,128]{1,0:T(8,128)S(1)}, u32[]{:S(2)}, u32[]{:S(2)}) %collective-permute-start.4) | collective-permute-done | bytes 4128 | tf_op jit(solution)/shard_map/ppermute | solution.py:448
  32.9 0.0 collective-permute-done.5.refs_2_
  32.9 1.1 %patch.1 = f32[19,128,128]{2,1,0:T(8,128)} custom-call(f32[4,8,128]{2,1,0:T(8,128)S(1)} %get-tuple-element.32.y_pre, f32[7,8,128]{2,1,0:T(8,128)S(1)} %get-tuple-element.33.picks, f32[10,128,128]{2,1,0:T(8,128)S(1)} %get-tuple-element.40.partial, f32[19,128,128]{2,1,0:T(8,128)} %get-tuple-element.41.started, ...), custom_call_target="tpu_custom_call", output_to_operand_aliasing={{}: (3, {})} | custom-call | tf_op jit(solution)/shard_map/patch/pallas_call | solution.py:467
  (1 shorter events, 0.0 us)
Async XLA Ops:
  0.0 16.9 %copy-start = (f32[19,1,128,128]{3,2,1,0:T(8,128)S(1)}, f32[19,1,128,128]{3,2,1,0:T(8,128)}, u32[]{:S(2)}) copy-start(f32[19,1,128,128]{3,2,1,0:T(8,128)} %param.5) | copy-start | bytes 3735556
  0.0 16.9 %copy-start.1 = (s32[1,128,128]{2,1,0:T(8,128)S(1)}, s32[1,128,128]{2,1,0:T(8,128)}, u32[]{:S(2)}) copy-start(s32[1,128,128]{2,1,0:T(8,128)} %param.6) | copy-start | bytes 196612
  3.4 13.6 %collective-permute-start = (f32[8,128]{1,0:T(8,128)S(1)}, f32[8,128]{1,0:T(8,128)S(1)}, u32[]{:S(2)}, u32[]{:S(2)}) collective-permute-start(f32[8,128]{1,0:T(8,128)S(1)} %get-tuple-element.37), channel_id=1, source_target_pairs={{1,17},{17,1},{2,18},{18,2},{3,19},{19,3},{4,20},{20,4},{5,21},{21... | collective-permute-start | bytes 12296 | tf_op jit(solution)/shard_map/ppermute | solution.py:419
  5.3 12.2 %collective-permute-start.1 = (f32[8,128]{1,0:T(8,128)S(1)}, f32[8,128]{1,0:T(8,128)S(1)}, u32[]{:S(2)}, u32[]{:S(2)}) collective-permute-start(f32[8,128]{1,0:T(8,128)S(1)} %get-tuple-element.38), channel_id=1, source_target_pairs={{0,16},{16,0},{17,33},{33,17},{18,34},{34,18},{19,35},{35,19},{20,... | collective-permute-start | bytes 12296 | tf_op jit(solution)/shard_map/ppermute | solution.py:419
  16.3 1.3 %collective-permute-start.2 = (f32[8,128]{1,0:T(8,128)S(1)}, f32[8,128]{1,0:T(8,128)S(1)}, u32[]{:S(2)}, u32[]{:S(2)}) collective-permute-start(f32[8,128]{1,0:T(8,128)S(1)} %get-tuple-element.39), channel_id=1, source_target_pairs={{8,24},{24,8},{722,738},{738,722},{723,739},{739,723},{724,740},{7... | collective-permute-start | bytes 12296 | tf_op jit(solution)/shard_map/ppermute | solution.py:419
  17.6 14.2 %collective-permute-start.3 = (f32[8,128]{1,0:T(8,128)S(1)}, f32[8,128]{1,0:T(8,128)S(1)}, u32[]{:S(2)}, u32[]{:S(2)}) collective-permute-start(f32[8,128]{1,0:T(8,128)S(1)} %get-tuple-element.42), channel_id=1, source_target_pairs={{0,1},{1,0},{2,3},{3,2},{6,7},{14,15},{15,14},{17,16},{22,23},{23,... | collective-permute-start | bytes 12296 | tf_op jit(solution)/shard_map/ppermute | solution.py:448
  18.9 13.9 %collective-permute-start.4 = (f32[8,128]{1,0:T(8,128)S(1)}, f32[8,128]{1,0:T(8,128)S(1)}, u32[]{:S(2)}, u32[]{:S(2)}) collective-permute-start(f32[8,128]{1,0:T(8,128)S(1)} %get-tuple-element.43), channel_id=1, source_target_pairs={{1,2},{2,1},{3,4},{4,3},{5,6},{6,5},{7,8},{8,7},{9,10},{10,9},{11,... | collective-permute-start | bytes 12296 | tf_op jit(solution)/shard_map/ppermute | solution.py:448
  29.3 3.6 %collective-permute-start.5 = (f32[8,128]{1,0:T(8,128)S(1)}, f32[8,128]{1,0:T(8,128)S(1)}, u32[]{:S(2)}, u32[]{:S(2)}) collective-permute-start(f32[8,128]{1,0:T(8,128)S(1)} %get-tuple-element.44), channel_id=1, source_target_pairs={{4,5},{5,4},{7,6},{8,9},{9,8},{10,11},{11,10},{12,13},{13,12},{16,... | collective-permute-start | bytes 12296 | tf_op jit(solution)/shard_map/ppermute | solution.py:448
